TPU v7x, 128 devices: a whole 4x4x4 slice. The times are simulated.
128 devices in a mesh: section: 8 (over x, core), dp: 16 (over z, y).
Axes of the slice: x: 4, y: 4, z: 4, core: 2. Of those that a mesh axis runs over, the one named last changes fastest.
Arguments:
- text: bfloat16 [16, 128, 8192], P('dp'), may hold values from -6 to 6
- cotangent: bfloat16 [16, 128, 8192], P('dp'), may hold values from -6 to 6
- dec_down: bfloat16 [8, 8192, 128], P('section'), may hold values from -0.0625 to 0.0625
- dec_up: bfloat16 [8, 128, 8192], P('section'), may hold values from -0.5 to 0.5
- images: bfloat16 [16, 8, 2, 32, 3200], P('dp', 'section'), may hold values from -6 to 6
- enc_down: bfloat16 [3200, 128], replicated, may hold values from -0.109375 to 0.109375
- enc_up: bfloat16 [128, 3200], replicated, may hold values from -0.5 to 0.5
- proj_in: bfloat16 [12800, 128], replicated, may hold values from -0.0546875 to 0.0546875
- proj_out: bfloat16 [128, 8192], replicated, may hold values from -0.5 to 0.5
- frame: int32 [16, 16], P('dp'), may hold values from -1 to 15, as said below
Outputs:
- grad_dec_down: float32 [8, 8192, 128], P('section', 'dp')
- grad_dec_up: float32 [8, 128, 8192], P('section', None, 'dp')
- grad_enc_down: float32 [3200, 128], P(('section', 'dp'))
- grad_enc_up: float32 [128, 3200], P(None, ('section', 'dp'))
- grad_proj_in: float32 [12800, 128], P(('section', 'dp'))
- grad_proj_out: float32 [128, 8192], P(None, ('section', 'dp'))
Inputs may be any that keep to these rules, and one draw needn't show every extreme that they name: In each row the entries that are not -1 are distinct; the largest frame and -1 occur in every draw.
All inputs are finite; a program needn't handle non-finite values.
Results may differ from a plain program's by a relative error of at most 0.035.
Values may be sent and summed in bfloat16 or wider, within the bound.
No kernel may reach another device: no remote copies, remote signals or barrier semaphores. Data moves between devices by JAX's collectives and lax.ppermute only.
A program may use at most 128 MiB of HBM per device.

v0:
```python
import jax
import jax.numpy as jnp
from jax import lax
from jax.sharding import PartitionSpec as P

SEQ = 32


EPS = 1e-06
GELU_C = 0.7978845608028654


def passed_along(value, axis, steps):
    count = lax.axis_size(axis)
    first, last = (max(0, -steps), min(count, count - steps))
    return lax.ppermute(value, axis, [(source, source + steps) for source in range(first, last)])


def from_root(block, axis, owner):
    block = jnp.where(lax.axis_index(axis) == owner, block, jnp.zeros_like(block))
    return lax.psum(block, axis)


def gelu_tanh(value):
    return 0.5 * value * (1.0 + jnp.tanh(GELU_C * (value + 0.044715 * value * value * value)))


def gelu_slope(value):
    inner = jnp.tanh(GELU_C * (value + 0.044715 * value * value * value))
    return 0.5 * (1.0 + inner) + 0.5 * value * (1.0 - inner * inner) * GELU_C * (
        1.0 + 3.0 * 0.044715 * value * value
    )


def silu_slope(value):
    sig = jax.nn.sigmoid(value)
    return sig * (1.0 + value * (1.0 - sig))


def norm_scale(rows32):
    return lax.rsqrt(jnp.mean(rows32 * rows32, axis=-1, keepdims=True) + EPS)


def norm_back(rows32, scale, grad):
    normed = rows32 * scale
    return scale * (grad - normed * jnp.mean(grad * normed, axis=-1, keepdims=True))


def inner_dot(left, right):
    return lax.dot_general(
        left, right, (((0,), (0,)), ((), ())), preferred_element_type=jnp.float32
    )


def outer_dot(left, right):
    return lax.dot_general(
        left, right, (((1,), (1,)), ((), ())), preferred_element_type=jnp.float32
    )


def encoder_front(patches, enc_down, enc_up, proj_in):
    patch32 = patches.astype(jnp.float32)
    enc_normed = (patch32 * norm_scale(patch32)).astype(jnp.bfloat16)
    enc_pre = jnp.dot(enc_normed, enc_down, preferred_element_type=jnp.float32)
    enc_act = gelu_tanh(enc_pre).astype(jnp.bfloat16)
    enc_out = (patch32 + jnp.dot(enc_act, enc_up, preferred_element_type=jnp.float32)).astype(
        jnp.bfloat16
    )
    merged = enc_out.reshape(patches.shape[0] // 4, 4 * patches.shape[1]).astype(jnp.float32)
    proj_scale = norm_scale(merged)
    proj_normed = (merged * proj_scale).astype(jnp.bfloat16)
    proj_pre = jnp.dot(proj_normed, proj_in, preferred_element_type=jnp.float32)
    proj_act = gelu_tanh(proj_pre).astype(jnp.bfloat16)
    return (enc_normed, enc_pre, enc_act, merged, proj_scale, proj_normed, proj_pre, proj_act)


def encoder_factors(patches, d_feature, enc_down, enc_up, proj_in):
    enc_normed, enc_pre, enc_act, merged, proj_scale, proj_normed, proj_pre, proj_act = (
        encoder_front(patches, enc_down, enc_up, proj_in)
    )
    d_proj = (d_feature * gelu_slope(proj_pre)).astype(jnp.bfloat16)
    d_pn = outer_dot(d_proj, proj_in)
    d_merged = norm_back(merged, proj_scale, d_pn).reshape(patches.shape).astype(jnp.bfloat16)
    d_enc = (outer_dot(d_merged, enc_up) * gelu_slope(enc_pre)).astype(jnp.bfloat16)
    return (enc_normed, d_enc, enc_act, d_merged, proj_normed, d_proj)


def layer_forward(hidden, weight_down, weight_up):
    h32 = hidden.astype(jnp.float32)
    normed = (h32 * norm_scale(h32)).astype(jnp.bfloat16)
    pre = jnp.dot(normed, weight_down, preferred_element_type=jnp.float32)
    act = jax.nn.silu(pre).astype(jnp.bfloat16)
    return (h32 + jnp.dot(act, weight_up, preferred_element_type=jnp.float32)).astype(jnp.bfloat16)


def layer_backward(hidden, grad, weight_down, weight_up):
    h32 = hidden.astype(jnp.float32)
    scale = norm_scale(h32)
    normed = (h32 * scale).astype(jnp.bfloat16)
    pre = jnp.dot(normed, weight_down, preferred_element_type=jnp.float32)
    act = jax.nn.silu(pre).astype(jnp.bfloat16)
    d_act = outer_dot(grad, weight_up)
    d_pre = (d_act * silu_slope(pre)).astype(jnp.bfloat16)
    d_normed = outer_dot(d_pre, weight_down)
    grad_in = (grad.astype(jnp.float32) + norm_back(h32, scale, d_normed)).astype(jnp.bfloat16)
    return (grad_in, normed, act, d_pre)


def shards(text, cotangent, dec_down, dec_up, images, enc_down, enc_up, proj_in, proj_out, frame):
    sections = lax.axis_size("section")
    position = lax.axis_index("section")
    slot_count = images.shape[2]
    patch_count = images.shape[3]
    enc_width = images.shape[4]
    image_tokens = patch_count // 4
    rows_total = text.shape[1]
    width = text.shape[2]
    rank_dec = dec_down.shape[2]
    rank_enc = enc_down.shape[1]
    rank_proj = proj_out.shape[0]
    frame_total = rows_total // image_tokens
    micro = rows_total // SEQ
    weight_down = dec_down[0]
    weight_up = dec_up[0]
    frames = frame[0]
    match = frames[None, :] == jnp.arange(frame_total, dtype=jnp.int32)[:, None]
    match_half = match.astype(jnp.bfloat16)
    frame_live = jnp.any(match, axis=1)
    own_frames = lax.dynamic_slice_in_dim(frames, position * slot_count, slot_count)

    def front_only(patches):
        return encoder_front(patches, enc_down, enc_up, proj_in)[-1]

    def front_empty(patches):
        return jnp.zeros((image_tokens, rank_proj), jnp.bfloat16)

    features = []
    for slot in range(slot_count):
        features.append(
            lax.cond(own_frames[slot] >= 0, front_only, front_empty, images[0, 0, slot])
        )
    local_act = jnp.stack(features)
    local_rows = jnp.dot(
        local_act.reshape(-1, rank_proj), proj_out, preferred_element_type=jnp.float32
    )
    local_rows = local_rows.astype(jnp.bfloat16).reshape(slot_count, image_tokens, width)
    every_rows = lax.all_gather(local_rows, "section", axis=0, tiled=True)
    placed = jnp.einsum(
        "fk,kid->fid", match_half, every_rows, preferred_element_type=jnp.float32
    ).astype(jnp.bfloat16)
    base = text[0].reshape(frame_total, image_tokens, width)
    first_input = jnp.where(frame_live[:, None, None], placed, base).reshape(micro, SEQ, width)
    ticks = micro + sections - 1

    def forward_tick(tick, carry):
        received, saved = carry
        index = tick - position
        valid = (index >= 0) & (index < micro)
        clipped = jnp.clip(index, 0, micro - 1)
        start_rows = lax.dynamic_index_in_dim(first_input, clipped, 0, keepdims=False)
        layer_in = jnp.where(position == 0, start_rows, received)
        layer_out = layer_forward(layer_in, weight_down, weight_up)
        previous = lax.dynamic_index_in_dim(saved, clipped, 0, keepdims=False)
        saved = lax.dynamic_update_index_in_dim(
            saved, jnp.where(valid, layer_in, previous), clipped, 0
        )
        received = passed_along(layer_out, "section", 1)
        return (received, saved)

    empty_rows = jnp.zeros((SEQ, width), jnp.bfloat16)
    empty_block = jnp.zeros((micro, SEQ, width), jnp.bfloat16)
    empty_rank = jnp.zeros((micro, SEQ, rank_dec), jnp.bfloat16)
    received, saved = lax.fori_loop(0, ticks, forward_tick, (empty_rows, empty_block))
    cot_blocks = cotangent[0].reshape(micro, SEQ, width)

    def backward_tick(tick, carry):
        received, normed_buf, grad_buf, act_buf, pre_buf, first_buf = carry
        index = tick - (sections - 1 - position)
        valid = (index >= 0) & (index < micro)
        clipped = jnp.clip(index, 0, micro - 1)
        last_rows = lax.dynamic_index_in_dim(cot_blocks, clipped, 0, keepdims=False)
        grad = jnp.where(position == sections - 1, last_rows, received)
        layer_in = lax.dynamic_index_in_dim(saved, clipped, 0, keepdims=False)
        grad_in, normed, act, d_pre = layer_backward(layer_in, grad, weight_down, weight_up)

        def keep(buffer, value):
            previous = lax.dynamic_index_in_dim(buffer, clipped, 0, keepdims=False)
            return lax.dynamic_update_index_in_dim(
                buffer, jnp.where(valid, value, previous), clipped, 0
            )

        normed_buf = keep(normed_buf, normed)
        grad_buf = keep(grad_buf, grad)
        act_buf = keep(act_buf, act)
        pre_buf = keep(pre_buf, d_pre)
        first_buf = keep(first_buf, grad_in)
        received = passed_along(grad_in, "section", -1)
        return (received, normed_buf, grad_buf, act_buf, pre_buf, first_buf)

    start = (empty_rows, empty_block, empty_block, empty_rank, empty_rank, empty_block)
    received, normed_buf, grad_buf, act_buf, pre_buf, first_buf = lax.fori_loop(
        0, ticks, backward_tick, start
    )
    part_down = inner_dot(normed_buf.reshape(-1, width), pre_buf.reshape(-1, rank_dec))
    part_up = inner_dot(act_buf.reshape(-1, rank_dec), grad_buf.reshape(-1, width))
    grad_dec_down, grad_dec_up = (
        lax.psum_scatter(
            part_down.astype(jnp.bfloat16), "dp", scatter_dimension=0, tiled=True
        ).astype(jnp.float32),
        lax.psum_scatter(
            part_up.astype(jnp.bfloat16), "dp", scatter_dimension=1, tiled=True
        ).astype(jnp.float32),
    )
    first_view = first_buf.reshape(frame_total, image_tokens, width)
    every_grad = jnp.einsum(
        "fk,fid->kid", match_half, first_view, preferred_element_type=jnp.float32
    ).astype(jnp.bfloat16)
    root_grad = from_root(every_grad, "section", 0)
    own_grad = lax.dynamic_slice_in_dim(root_grad, position * slot_count, slot_count, 0).reshape(
        -1, width
    )
    part_proj_out = inner_dot(local_act.reshape(-1, rank_proj), own_grad)
    own_feature = outer_dot(own_grad, proj_out).reshape(slot_count, image_tokens, rank_proj)

    def back_live(operands):
        return encoder_factors(operands[0], operands[1], enc_down, enc_up, proj_in)

    def back_empty(operands):
        return (
            jnp.zeros((patch_count, enc_width), jnp.bfloat16),
            jnp.zeros((patch_count, rank_enc), jnp.bfloat16),
            jnp.zeros((patch_count, rank_enc), jnp.bfloat16),
            jnp.zeros((patch_count, enc_width), jnp.bfloat16),
            jnp.zeros((image_tokens, 4 * enc_width), jnp.bfloat16),
            jnp.zeros((image_tokens, rank_proj), jnp.bfloat16),
        )

    factor_list = []
    for slot in range(slot_count):
        factor_list.append(
            lax.cond(
                own_frames[slot] >= 0,
                back_live,
                back_empty,
                (images[0, 0, slot], own_feature[slot]),
            )
        )
    part_enc_down = jnp.zeros(enc_down.shape, jnp.float32)
    part_enc_up = jnp.zeros(enc_up.shape, jnp.float32)
    part_proj_in = jnp.zeros(proj_in.shape, jnp.float32)
    for factors in factor_list:
        part_enc_down = part_enc_down + inner_dot(factors[0], factors[1])
        part_enc_up = part_enc_up + inner_dot(factors[2], factors[3])
        part_proj_in = part_proj_in + inner_dot(factors[4], factors[5])
    grad_enc_down, grad_enc_up, grad_proj_in, grad_proj_out = (
        lax.psum_scatter(part_enc_down, ("section", "dp"), scatter_dimension=0, tiled=True),
        lax.psum_scatter(part_enc_up, ("section", "dp"), scatter_dimension=1, tiled=True),
        lax.psum_scatter(part_proj_in, ("section", "dp"), scatter_dimension=0, tiled=True),
        lax.psum_scatter(part_proj_out, ("section", "dp"), scatter_dimension=1, tiled=True),
    )
    return (
        grad_dec_down[None],
        grad_dec_up[None],
        grad_enc_down,
        grad_enc_up,
        grad_proj_in,
        grad_proj_out,
    )


def solution(mesh):
    placed = (
        P("dp", None, None),
        P("dp", None, None),
        P("section", None, None),
        P("section", None, None),
        P("dp", "section", None, None, None),
        P(),
        P(),
        P(),
        P(),
        P("dp", None),
    )
    return jax.shard_map(
        shards,
        mesh=mesh,
        in_specs=placed,
        out_specs=(
            P("section", "dp", None),
            P("section", None, "dp"),
            P(("section", "dp"), None),
            P(None, ("section", "dp")),
            P(("section", "dp"), None),
            P(None, ("section", "dp")),
        ),
        check_vma=False,
    )
```

profile of v0, /device:TPU:0, one launch (start us, length us, event | category | flops | bytes accessed | tf_op | source)
XLA Modules:
  0.0 1426.9 jit_solution(7918069795427136393)
XLA Ops:
  22.5 27.3 %all-gather.2.cloned.1.call-done = bf16[16,8,8192]{2,1,0:T(8,128)(2,1)} async-done(((bf16[2,8,8192]{2,1,0:T(8,128)(2,1)}), bf16[16,8,8192]{2,1,0:T(8,128)(2,1)}) %all-gather.2.cloned.1.call-update) | async-done | bytes 2097168 | tf_op jit(solution)/shard_map/all_gather | solution.py:147
  60.7 189.4 %while.41 = (s32[]{:T(128)}, bf16[32,8192]{1,0:T(8,128)(2,1)S(1)}, bf16[4,32,8192]{2,1,0:T(8,128)(2,1)}, pred[]{:T(512)}, s32[]{:T(128)}, /*index=5*/bf16[4,32,8...) while((s32[]{:T(128)}, bf16[32,8192]{1,0:T(8,128)(2,1)S(1)}, ...), condition=%wide.region_13.14_spmd, body=%wide.region_11.13_spmd.sunk | while | flops 137121824 | bytes 11535583 | solution.py:173
  95.4 9.0 collective-permute-start
  131.4 9.0 collective-permute-start
  149.4 9.0 collective-permute-start
  256.0 276.4 %while.42 = (s32[]{:T(128)}, bf16[32,8192]{1,0:T(8,128)(2,1)S(1)}, bf16[4,32,8192]{2,1,0:T(8,128)(2,1)}, bf16[4,32,8192]{2,1,0:T(8,128)(2,1)}, bf16[4,32,128]{2,...) while((s32[]{:T(128)}, bf16[32,8192]{1,0:T(8,128)(2,1)S(1)}, ...), condition=%wide.region_17.18_spmd, body=%wide.region_14.17_spmd.sunk | while | flops 207683616 | bytes 46292260 | solution.py:201
  271.9 9.1 collective-permute-done.1
  296.9 9.8 collective-permute-done.1
  322.6 9.2 collective-permute-done.1
  347.7 9.2 collective-permute-done.1
  372.8 9.2 collective-permute-done.1
  397.9 9.2 collective-permute-done.1
  422.9 9.2 collective-permute-done.1
  448.0 9.2 collective-permute-done.1
  473.2 9.2 collective-permute-done.1
  498.3 9.1 collective-permute-done.1
  523.3 9.2 collective-permute-done.1
  546.8 64.5 %all-reduce.9.cloned.1.call-done = bf16[16,8,8192]{2,0,1:T(8,128)(2,1)} async-done(((bf16[16,8,8192]{2,0,1:T(8,128)(2,1)}), bf16[16,8,8192]{2,0,1:T(8,128)(2,1)}) %all-reduce.9.cloned.1.call-update) | async-done | bytes 2097168 | tf_op jit(solution)/shard_map/psum | solution.py:21
  618.8 13.6 conditional.6
  633.1 15.2 %conditional.7 = (bf16[32,3200]{1,0:T(8,128)(2,1)}, bf16[32,128]{1,0:T(8,128)(2,1)S(1)}, bf16[32,128]{1,0:T(8,128)(2,1)}, bf16[32,3200]{1,0:T(8,128)(2,1)}, bf16...) conditional(s32[]{:T(128)} %bitcast.20, () %tuple.87, (bf16[32,3200]{1,0:T(8,128)(2,1)S(1)}, ...), branch_computations={%region_27.28_spmd, %region_28.33_spmd} | conditional | flops 133458984 | bytes 29386212 | solution.py:241
  663.0 363.0 %fusion.154 = (f32[32,128]{1,0:T(8,128)S(1)}, f32[128,32]{0,1:T(8,128)S(1)}, f32[112,128]{1,0:T(8,128)S(1)}) fusion(f32[3200,128]{1,0:T(8,128)} %convolution_add_fusion.7, f32[128,3200]{0,1:T(8,128)} %convolution_add_fusion.6, f32[12800,128]{1,0:T(8,128)} %convolution_add_fusion.5), kind=kCustom, calls=%all-reduce-scatter.3 | all-reduce-scatter fusion | flops 2883586 | bytes 9920512
  1061.7 13.3 collective-permute-start.41
  1198.9 15.4 %concatenate = f32[921,128]{1,0:T(8,128)S(1)} concatenate(f32[25,128]{1,0:T(8,128)S(1)} %collective-permute-done.29, f32[32,128]{1,0:T(8,128)} %copy-done.40, f32[32,128]{1,0:T(8,128)} %copy-done.39, f32[32,128]{1,0:T(8,128)} %copy-done.38, f32[32,128]{1,0:T(8,128)} %copy-done.37, f32[32,128]{1,0:T(8,128)} %copy-done.36, f32[32,128]{1,0:T(8,128)} %copy-done.35, ...), dimensions={0} | concatenate | bytes 943104
  1255.1 165.3 %reduce-scatter.14.cloned.1.call-done = f32[128,64]{0,1:T(8,128)} async-done(((f32[128,8192]{0,1:T(8,128)}), f32[128,64]{0,1:T(8,128)}) %reduce-scatter.14.cloned.1.call-update) | async-done | bytes 32784 | tf_op jit(solution)/shard_map/reduce_scatter | solution.py:259
  (627 shorter events, 641.7 us)
Async XLA Ops:
  7.2 42.7 %all-gather.2.cloned.1.call-start = ((), (), s32[]{:S(2)}) async-start(), calls=%async_computation.3 | async-start | bytes 2359296 | tf_op jit(solution)/shard_map/all_gather | solution.py:147
  22.4 588.9 %all-reduce.9.cloned.1.call-start = ((), (), s32[]{:S(2)}) async-start(), calls=%async_computation.6 | async-start | bytes 4194304 | tf_op jit(solution)/shard_map/psum | solution.py:21
  537.9 713.9 %reduce-scatter.12.cloned.1.call-start = ((), (), s32[]{:S(2)}) async-start(), calls=%async_computation.5 | async-start | bytes 2228224 | tf_op jit(solution)/shard_map/reduce_scatter | solution.py:210
  542.3 711.1 %reduce-scatter.10.cloned.1.call-start = ((), (), s32[]{:S(2)}) async-start(), calls=%async_computation.4 | async-start | bytes 2228224 | tf_op jit(solution)/shard_map/reduce_scatter | solution.py:207
  546.7 873.6 %reduce-scatter.14.cloned.1.call-start = ((), (), s32[]{:S(2)}) async-start(), calls=%async_computation.7 | async-start | bytes 4227072 | tf_op jit(solution)/shard_map/reduce_scatter | solution.py:259
  1037.8 16.3 %collective-permute-start.35 = (f32[128,32]{0,1:T(8,128)S(1)}, f32[128,32]{0,1:T(8,128)S(1)}, u32[]{:S(2)}, u32[]{:S(2)}) collective-permute-start(f32[128,32]{0,1:T(8,128)S(1)} %get-tuple-element.587), channel_id=1, source_target_pairs={{0,6},{1,7},{2,8},{3,9},{4,10},{5,11},{6,12},{7,13},{8,14},{9,15},... | collective-permute-start | bytes 49160
  1039.1 22.6 %collective-permute-start.36 = (f32[128,32]{0,1:T(8,128)S(1)}, f32[128,32]{0,1:T(8,128)S(1)}, u32[]{:S(2)}, u32[]{:S(2)}) collective-permute-start(f32[128,32]{0,1:T(8,128)S(1)} %get-tuple-element.587), channel_id=1, source_target_pairs={{0,7},{1,8},{2,9},{3,10},{4,11},{5,12},{6,13},{7,14},{8,15},{9,16}... | collective-permute-start | bytes 49160
  1040.4 34.6 %collective-permute-start.37 = (f32[128,32]{0,1:T(8,128)S(1)}, f32[128,32]{0,1:T(8,128)S(1)}, u32[]{:S(2)}, u32[]{:S(2)}) collective-permute-start(f32[128,32]{0,1:T(8,128)S(1)} %get-tuple-element.587), channel_id=1, source_target_pairs={{0,8},{1,9},{2,10},{3,11},{4,12},{5,13},{6,14},{7,15},{8,16},{9,17... | collective-permute-start | bytes 49160
  1044.9 31.7 %collective-permute-start.38 = (f32[128,32]{0,1:T(8,128)S(1)}, f32[128,32]{0,1:T(8,128)S(1)}, u32[]{:S(2)}, u32[]{:S(2)}) collective-permute-start(f32[128,32]{0,1:T(8,128)S(1)} %get-tuple-element.587), channel_id=1, source_target_pairs={{0,9},{1,10},{2,11},{3,12},{4,13},{5,14},{6,15},{7,16},{8,17},{9,1... | collective-permute-start | bytes 49160
  1050.0 29.5 %collective-permute-start.39 = (f32[128,32]{0,1:T(8,128)S(1)}, f32[128,32]{0,1:T(8,128)S(1)}, u32[]{:S(2)}, u32[]{:S(2)}) collective-permute-start(f32[128,32]{0,1:T(8,128)S(1)} %get-tuple-element.587), channel_id=1, source_target_pairs={{0,10},{1,11},{2,12},{3,13},{4,14},{5,15},{6,16},{7,17},{8,18},{9,... | collective-permute-start | bytes 49160
  1054.1 29.2 %collective-permute-start.40 = (f32[128,32]{0,1:T(8,128)S(1)}, f32[128,32]{0,1:T(8,128)S(1)}, u32[]{:S(2)}, u32[]{:S(2)}) collective-permute-start(f32[128,32]{0,1:T(8,128)S(1)} %get-tuple-element.587), channel_id=1, source_target_pairs={{0,11},{1,12},{2,13},{3,14},{4,15},{5,16},{6,17},{7,18},{8,19},{9,... | collective-permute-start | bytes 49160
  1061.7 22.9 %collective-permute-start.41 = (f32[128,32]{0,1:T(8,128)S(1)}, f32[128,32]{0,1:T(8,128)S(1)}, u32[]{:S(2)}, u32[]{:S(2)}) collective-permute-start(f32[128,32]{0,1:T(8,128)S(1)} %get-tuple-element.587), channel_id=1, source_target_pairs={{0,12},{1,13},{2,14},{3,15},{4,16},{5,17},{6,18},{7,19},{8,20},{9,... | collective-permute-start | bytes 49160
  1106.1 14.8 %collective-permute-start.10 = (f32[32,128]{1,0:T(8,128)S(1)}, f32[32,128]{1,0:T(8,128)S(1)}, u32[]{:S(2)}, u32[]{:S(2)}) collective-permute-start(f32[32,128]{1,0:T(8,128)S(1)} %get-tuple-element.586), channel_id=1, source_target_pairs={{0,9},{1,10},{2,11},{3,12},{4,13},{5,14},{6,15},{7,16},{8,17},{9,1... | collective-permute-start | bytes 49160
  1150.6 16.8 %collective-permute-start.3 = (f32[32,128]{1,0:T(8,128)S(1)}, f32[32,128]{1,0:T(8,128)}, u32[]{:S(2)}, u32[]{:S(2)}) collective-permute-start(f32[32,128]{1,0:T(8,128)S(1)} %get-tuple-element.586), channel_id=1, source_target_pairs={{0,2},{1,3},{2,4},{3,5},{4,6},{5,7},{6,8},{7,9},{8,10},{9,11},{10,... | collective-permute-start | bytes 49160
  1153.4 16.6 %collective-permute-start.4 = (f32[32,128]{1,0:T(8,128)S(1)}, f32[32,128]{1,0:T(8,128)S(1)}, u32[]{:S(2)}, u32[]{:S(2)}) collective-permute-start(f32[32,128]{1,0:T(8,128)S(1)} %get-tuple-element.586), channel_id=1, source_target_pairs={{0,3},{1,4},{2,5},{3,6},{4,7},{5,8},{6,9},{7,10},{8,11},{9,12},{10... | collective-permute-start | bytes 49160
  1159.6 58.5 %collective-permute-start.58 = (f32[112,128]{1,0:T(8,128)S(1)}, f32[112,128]{1,0:T(8,128)S(1)}, u32[]{:S(2)}, u32[]{:S(2)}) collective-permute-start(f32[112,128]{1,0:T(8,128)S(1)} %get-tuple-element.588), channel_id=1, source_target_pairs={{0,1},{1,2},{2,3},{3,4},{4,5},{5,6},{6,7},{7,8},{8,9},{9,10},{10,1... | collective-permute-start | bytes 172040
  1161.1 60.5 %collective-permute-start.59 = (f32[112,128]{1,0:T(8,128)S(1)}, f32[112,128]{1,0:T(8,128)S(1)}, u32[]{:S(2)}, u32[]{:S(2)}) collective-permute-start(f32[112,128]{1,0:T(8,128)S(1)} %get-tuple-element.588), channel_id=1, source_target_pairs={{0,2},{1,3},{2,4},{3,5},{4,6},{5,7},{6,8},{7,9},{8,10},{9,11},{10,... | collective-permute-start | bytes 172040
  1167.4 57.8 %collective-permute-start.60 = (f32[112,128]{1,0:T(8,128)S(1)}, f32[112,128]{1,0:T(8,128)S(1)}, u32[]{:S(2)}, u32[]{:S(2)}) collective-permute-start(f32[112,128]{1,0:T(8,128)S(1)} %get-tuple-element.588), channel_id=1, source_target_pairs={{0,3},{1,4},{2,5},{3,6},{4,7},{5,8},{6,9},{7,10},{8,11},{9,12},{10... | collective-permute-start | bytes 172040
  1175.8 38.6 %collective-permute-start.71 = (f32[68,128]{1,0:T(8,128)S(1)}, f32[68,128]{1,0:T(8,128)}, u32[]{:S(2)}, u32[]{:S(2)}) collective-permute-start(f32[68,128]{1,0:T(8,128)S(1)} %slice.34), channel_id=1, source_target_pairs={{0,14},{1,15},{2,16},{3,17},{4,18},{5,19},{6,20},{7,21},{8,22},{9,... | collective-permute-start | bytes 104456
  1195.9 32.8 %collective-permute-start.61 = (f32[112,128]{1,0:T(8,128)S(1)}, f32[112,128]{1,0:T(8,128)S(1)}, u32[]{:S(2)}, u32[]{:S(2)}) collective-permute-start(f32[112,128]{1,0:T(8,128)S(1)} %get-tuple-element.588), channel_id=1, source_target_pairs={{0,4},{1,5},{2,6},{3,7},{4,8},{5,9},{6,10},{7,11},{8,12},{9,13},{1... | collective-permute-start | bytes 172040
  1214.4 19.9 %collective-permute-start.62 = (f32[112,128]{1,0:T(8,128)S(1)}, f32[112,128]{1,0:T(8,128)S(1)}, u32[]{:S(2)}, u32[]{:S(2)}) collective-permute-start(f32[112,128]{1,0:T(8,128)S(1)} %get-tuple-element.588), channel_id=1, source_target_pairs={{0,5},{1,6},{2,7},{3,8},{4,9},{5,10},{6,11},{7,12},{8,13},{9,14},{... | collective-permute-start | bytes 172040
  1218.1 18.1 %collective-permute-start.63 = (f32[112,128]{1,0:T(8,128)S(1)}, f32[112,128]{1,0:T(8,128)S(1)}, u32[]{:S(2)}, u32[]{:S(2)}) collective-permute-start(f32[112,128]{1,0:T(8,128)S(1)} %get-tuple-element.588), channel_id=1, source_target_pairs={{0,6},{1,7},{2,8},{3,9},{4,10},{5,11},{6,12},{7,13},{8,14},{9,15},... | collective-permute-start | bytes 172040
  1221.6 16.4 %collective-permute-start.64 = (f32[112,128]{1,0:T(8,128)S(1)}, f32[112,128]{1,0:T(8,128)S(1)}, u32[]{:S(2)}, u32[]{:S(2)}) collective-permute-start(f32[112,128]{1,0:T(8,128)S(1)} %get-tuple-element.588), channel_id=1, source_target_pairs={{0,7},{1,8},{2,9},{3,10},{4,11},{5,12},{6,13},{7,14},{8,15},{9,16}... | collective-permute-start | bytes 172040
  1225.2 15.4 %collective-permute-start.65 = (f32[112,128]{1,0:T(8,128)S(1)}, f32[112,128]{1,0:T(8,128)S(1)}, u32[]{:S(2)}, u32[]{:S(2)}) collective-permute-start(f32[112,128]{1,0:T(8,128)S(1)} %get-tuple-element.588), channel_id=1, source_target_pairs={{0,8},{1,9},{2,10},{3,11},{4,12},{5,13},{6,14},{7,15},{8,16},{9,17... | collective-permute-start | bytes 172040
  (170 other events, 1372.6 us)
Sparse Core Ops, SparseCore 0:
  22.5 27.3 all-gather.1
  538.0 73.2 all-reduce.8
  614.6 75.7 reduce-scatter.11
  693.8 79.5 reduce-scatter.9
  776.1 644.2 reduce-scatter.13
where the time goes:
time: 1440 us; the launch traced here: 1430 us
  waiting for transfers between devices  379 us (26%)
  blocking collectives  363 us (25%)
  starting transfers between devices  298 us (21%)
  matrix products  169 us (12%)
  other arithmetic  107 us (7%)
  local copies, waits for them, and re-layouts  92.8 us (6%)
  between operations  16.6 us (1%)
    unnamed x1, blocking collectives  363 us
    unnamed x70, starting transfers between devices  194 us
    reduce_scatter x1, waiting for transfers between devices, shards(): lax.psum_scatter(part_proj_out, ('section', 'dp'), scatter_dimension=1, t...  165 us
    ppermute x22, waiting for transfers between devices, passed_along(): lax.ppermute(value, axis, [(source, source + steps) for source in range(f...  120 us
    ppermute x22, starting transfers between devices, passed_along(): lax.ppermute(value, axis, [(source, source + steps) for source in range(f...  104 us
    psum x1, waiting for transfers between devices, from_root(): return lax.psum(block, axis)  64.5 us
    dynamic_update_slice x22, other arithmetic, keep(): lax.dynamic_update_index_in_dim(buffer, jnp.where(valid, value, previous)...  54.4 us
    dot_general x11, matrix products, layer_forward(): jnp.dot(act, weight_up, preferred_element_type=jnp.float32)  43.1 us
  transfers between devices with their start and end apart: 97, of which 26 were waited for; matrix products, arithmetic and copies ran while one was open for 32% of the time, Pallas kernels for 0%

commit v1 on v0

v1 whole, which is shorter than its diff:
```python
import functools

import jax
import jax.numpy as jnp
from jax import lax
from jax.experimental import pallas as pl
from jax.experimental.pallas import tpu as pltpu
from jax.sharding import PartitionSpec as P

EPS = 1e-06
GELU_C = 0.7978845608028654
BF = jnp.bfloat16
F32 = jnp.float32


def gelu_tanh(value):
    return 0.5 * value * (1.0 + jnp.tanh(GELU_C * (value + 0.044715 * value * value * value)))


def gelu_slope(value):
    inner = jnp.tanh(GELU_C * (value + 0.044715 * value * value * value))
    return 0.5 * (1.0 + inner) + 0.5 * value * (1.0 - inner * inner) * GELU_C * (
        1.0 + 3.0 * 0.044715 * value * value
    )


def norm_scale(rows32):
    return lax.rsqrt(jnp.mean(rows32 * rows32, axis=-1, keepdims=True) + EPS)


def dot(left, right, dims):
    return lax.dot_general(left, right, ((dims[:1], dims[1:]), ((), ())), preferred_element_type=F32)


def dot_nn(left, right):
    return dot(left, right, (1, 0))


def dot_tn(left, right):
    return dot(left, right, (0, 0))


def dot_nt(left, right):
    return dot(left, right, (1, 1))


def rank_kernel(
    layers, groups, width,
    place_ref, gram_ref, gath_ref, cot_ref, norm_ref, image_gram_ref, sel_ref,
    coef_ref, factor_ref, image_ref,
    weight, acts, act_cat, grads, scaled, back, pre_ref, slope_ref, inner_ref, scale_ref,
):
    rank = 128
    own = place_ref[0]

    def lay(layer, carry):
        for j in range(layers + 1):
            tile = gram_ref[pl.ds(layer * groups, groups), j * 16:(j + 1) * 16, :].astype(F32)
            rows = slice(j * rank, (j + 1) * rank)
            weight[layer, rows, :rank] = tile[:, :8, :].reshape(rank, rank).astype(BF)
            weight[layer, rows, rank:] = tile[:, 8:, :].reshape(rank, rank).astype(BF)
        return carry

    lax.fori_loop(0, layers, lay, 0)

    proj_pre = jnp.concatenate(
        [gath_ref[l, 4 * rank:4 * rank + 16, :] for l in range(layers)], axis=0
    ).astype(F32)
    sel = sel_ref[...]
    placed = dot_nn(sel, gelu_tanh(proj_pre).astype(BF))
    placed_half = placed.astype(BF)
    acts[0] = placed_half
    act_cat[:, :rank] = placed_half
    image_inner = dot_nn(placed_half, image_gram_ref[...])
    total = norm_ref[...] + jnp.sum(placed * image_inner, axis=1, keepdims=True)
    for l in range(layers):
        here = (l + 1) * rank
        scale = lax.rsqrt(jnp.maximum(total, 0.0) * (1.0 / width) + EPS)
        both = dot_nn(act_cat[:, :here], weight[l, :here, :])
        pre = scale * (gath_ref[l, :rank, :].astype(F32) + both[:, :rank])
        inner = gath_ref[l, rank:2 * rank, :].astype(F32) + both[:, rank:]
        sig = jax.nn.sigmoid(pre)
        act = (pre * sig).astype(BF)
        acts[l + 1] = act
        act_cat[:, here:here + rank] = act
        after = inner + dot_nn(act, weight[l, here:here + rank, rank:])
        total = total + jnp.sum(act.astype(F32) * (inner + after), axis=1, keepdims=True)
        pre_ref[l] = pre
        slope_ref[l] = sig * (1.0 + pre * (1.0 - sig))
        inner_ref[l] = after
        scale_ref[l] = scale
    back[...] = jnp.zeros_like(back)
    sums = jnp.zeros_like(total)
    for l in reversed(range(layers)):
        here = (l + 1) * rank
        cot = gath_ref[l, 2 * rank:3 * rank, :].astype(F32)
        d_act = cot - sums * inner_ref[l] + back[:, here:here + rank]
        d_pre = (d_act * slope_ref[l]).astype(BF).astype(F32)
        scale = scale_ref[l]
        mean = jnp.sum(d_pre * pre_ref[l], axis=1, keepdims=True) * (1.0 / width)
        grad = (scale * d_pre).astype(BF)
        part = (sums * acts[l + 1].astype(F32)).astype(BF)
        grads[l] = grad
        scaled[l + 1] = part
        pair = jnp.concatenate([grad, -part], axis=1)
        back[:, :here] += dot_nt(pair, weight[l, :here, :])
        sums = sums + scale * scale * mean
    d_image = cot_ref[...] - sums * image_inner + back[:, :rank]
    scaled[0] = (sums * placed).astype(BF)
    d_slot = dot_tn(sel, d_image.astype(BF))
    image_ref[0] = (d_slot * gelu_slope(proj_pre)).astype(BF)
    image_ref[1] = placed_half
    image_ref[2] = scaled[0]

    own_act = acts[own + 1]
    own_grad = grads[own]
    own_scaled = scaled[own + 1]
    factor_ref[0] = own_grad
    factor_ref[1] = own_act
    factor_ref[2] = own_scaled
    coef_ref[0] = dot_tn(acts[0], own_grad).astype(BF)
    for l in range(layers):
        low = l < own
        left = jnp.where(low, acts[l + 1], grads[l])
        right = jnp.where(low, own_grad, own_act)
        coef_ref[l + 1] = dot_tn(left, right).astype(BF)
    for l in range(layers + 1):
        low = l <= own + 1
        left = jnp.where(low, acts[l], scaled[l])
        right = jnp.where(low, own_scaled, own_act)
        coef_ref[layers + 1 + l] = dot_tn(left, right).astype(BF)


def rank_space(position, gram, gath, cot, norms, image_gram, sel, width):
    layers = gath.shape[0]
    groups = gram.shape[0] // layers
    rank = 128
    vmem = pl.BlockSpec(memory_space=pltpu.VMEM)
    tall = (layers + 1) * rank
    return pl.pallas_call(
        functools.partial(rank_kernel, layers, groups, width),
        in_specs=[pl.BlockSpec(memory_space=pltpu.SMEM)] + [vmem] * 6,
        out_specs=[vmem] * 3,
        out_shape=[
            jax.ShapeDtypeStruct((2 * layers + 2, rank, rank), BF),
            jax.ShapeDtypeStruct((3, rank, rank), BF),
            jax.ShapeDtypeStruct((3, rank, rank), BF),
        ],
        scratch_shapes=[
            pltpu.VMEM((layers, tall, 2 * rank), BF),
            pltpu.VMEM((layers + 1, rank, rank), BF),
            pltpu.VMEM((rank, tall), BF),
            pltpu.VMEM((layers, rank, rank), BF),
            pltpu.VMEM((layers + 1, rank, rank), BF),
            pltpu.VMEM((rank, tall), F32),
            pltpu.VMEM((layers, rank, rank), F32),
            pltpu.VMEM((layers, rank, rank), F32),
            pltpu.VMEM((layers, rank, rank), F32),
            pltpu.VMEM((layers, rank, 1), F32),
        ],
        compiler_params=pltpu.CompilerParams(vmem_limit_bytes=40 * 1024 * 1024),
    )(position.reshape(1).astype(jnp.int32), gram, gath, cot, norms, image_gram, sel)


def section_gather(value):
    count = lax.axis_size("section")
    parts = [value]
    for step in range(1, count):
        pairs = [((at + step) % count, at) for at in range(count)]
        parts.append(lax.ppermute(value, "section", pairs))
    return jnp.roll(jnp.stack(parts), lax.axis_index("section"), axis=0)


def split_pair(value):
    high = value.astype(BF)
    return high, (value - high.astype(F32)).astype(BF)


def shards(text, cotangent, dec_down, dec_up, images, enc_down, enc_up, proj_in, proj_out, frame):
    sections = lax.axis_size("section")
    groups = lax.axis_size("dp")
    sec = lax.axis_index("section")
    grp = lax.axis_index("dp")
    slot_count, patch_count, enc_width = images.shape[2:]
    tokens = patch_count // 4
    rows_total, width = text.shape[1:]
    rank = dec_down.shape[2]
    frame_total = rows_total // tokens
    weight_down = dec_down[0]
    weight_up = dec_up[0]
    frames = frame[0]
    text = text[0]
    cot = cotangent[0]
    piece = rank // groups

    own_rows = lax.dynamic_slice_in_dim(weight_up, grp * piece, piece, 0)
    up_rows = lax.all_gather(own_rows, "section", axis=0)

    slot_row = jnp.repeat(frames, tokens)[None, :]
    row = jnp.arange(rows_total, dtype=jnp.int32)[:, None]
    column = jnp.arange(rows_total, dtype=jnp.int32)[None, :]
    sel = (slot_row == row // tokens) & (row % tokens == column % tokens)
    live = jnp.any(sel, axis=1, keepdims=True)
    sel = sel.astype(BF)
    text = jnp.where(live, jnp.zeros_like(text), text)
    text_down = dot_nn(text, weight_down).astype(BF)
    text_up = dot_nt(text, weight_up).astype(BF)
    cot_up = dot_nt(cot, weight_up).astype(BF)
    cot_image = dot_nt(cot, proj_out)
    text32 = text.astype(F32)
    text_norm = jnp.sum(text32 * text32, axis=1, keepdims=True)
    image_gram = dot_nt(proj_out, proj_out).astype(BF)

    patches = images[0, 0].reshape(slot_count * patch_count, enc_width)
    patch32 = patches.astype(F32)
    enc_scale = norm_scale(patch32)
    enc_pre = dot_nn((patch32 * enc_scale).astype(BF), enc_down)
    enc_act = gelu_tanh(enc_pre).astype(BF)
    enc_out = (patch32 + dot_nn(enc_act, enc_up)).astype(BF)
    enc_inner = dot_nt(enc_out, enc_up)
    merged = enc_out.reshape(slot_count * tokens, 4 * enc_width).astype(F32)
    proj_scale = norm_scale(merged)
    proj_normed = (merged * proj_scale).astype(BF)
    proj_pre = dot_nn(proj_normed, proj_in)
    scale_row = jnp.concatenate(
        [part[:, 0] for part in split_pair(enc_scale) + split_pair(proj_scale)]
    )
    scale_row = jnp.pad(scale_row, (0, 16 * rank - scale_row.shape[0])).reshape(16, rank)
    payload = jnp.concatenate(
        [
            text_down, text_up, cot_up, enc_pre.astype(BF), enc_inner.astype(BF),
            proj_pre.astype(BF), scale_row,
        ],
        axis=0,
    )
    gath = section_gather(payload)

    image_rows = lax.dynamic_slice_in_dim(proj_out, grp * piece, piece, 0)
    rows = jnp.concatenate([image_rows[None], up_rows], axis=0).reshape(-1, width)
    gram = jnp.stack(
        [
            dot_nn(rows, weight_down).reshape(sections + 1, piece, rank),
            dot_nt(rows, weight_up).reshape(sections + 1, piece, rank),
        ],
        axis=1,
    ).astype(BF).reshape(-1, rank)
    every_gram = lax.all_gather(gram, ("section", "dp"), axis=0)

    patch_cols = lax.all_to_all(patches, "section", 1, 0, tiled=True)
    normed_cols = lax.all_to_all(proj_normed, "section", 1, 0, tiled=True)
    text_late, cot_late, _ = lax.optimization_barrier((text, cot, gram))
    text_cols = lax.all_to_all(text_late, "dp", 1, 0, tiled=True)
    cot_cols = lax.all_to_all(cot_late, "dp", 1, 0, tiled=True)
    share = width // groups
    own_slices = jnp.concatenate(
        [
            lax.dynamic_slice_in_dim(weight_down, grp * share, share, 0).T,
            lax.dynamic_slice_in_dim(weight_up, grp * share, share, 1),
        ],
        axis=0,
    )
    own_slices, every_gram = lax.optimization_barrier((own_slices, every_gram))
    slices = lax.all_gather(own_slices, "section", axis=0)
    down_slices = slices[:, :rank].reshape(-1, share)
    up_slices = jnp.concatenate(
        [
            lax.dynamic_slice_in_dim(proj_out, grp * share, share, 1),
            slices[:, rank:].reshape(-1, share),
        ],
        axis=0,
    )

    coef, factor, image = rank_space(
        sec, every_gram, gath, cot_image, text_norm, image_gram, sel, width
    )
    d_proj, placed, placed_scaled = image[0], image[1], image[2]
    factors = lax.all_gather(factor, "dp", axis=0)
    coef = lax.all_to_all(coef.reshape(groups, -1, rank), "dp", 0, 0)
    coef = jnp.sum(coef.astype(F32), axis=0).astype(BF)
    coef = lax.all_gather(coef, "dp", axis=0, tiled=True)

    at = 3 * rank
    many = slot_count * patch_count
    group_enc_pre = gath[:, at:at + many].reshape(-1, rank).astype(F32)
    group_inner = gath[:, at + many:at + 2 * many].reshape(-1, rank).astype(F32)
    at += 2 * many
    few = slot_count * tokens
    group_proj_pre = gath[:, at:at + few].reshape(-1, rank).astype(F32)
    scales = gath[:, at + few:].reshape(sections, -1).astype(F32)
    group_enc_scale = (scales[:, :many] + scales[:, many:2 * many]).reshape(-1, 1)
    group_proj_scale = (
        scales[:, 2 * many:2 * many + few] + scales[:, 2 * many + few:2 * many + 2 * few]
    ).reshape(-1, 1)
    group_act = gelu_tanh(group_enc_pre).astype(BF)
    block = enc_width // sections
    own_up = lax.dynamic_slice_in_dim(enc_up, sec * block, block, 1)
    out_cols = (patch_cols.astype(F32) + dot_nn(group_act, own_up)).astype(BF)
    enc_cols = (patch_cols.astype(F32) * group_enc_scale).astype(BF)
    quarters = proj_in.reshape(4, enc_width, rank)
    cross = jnp.einsum("ker,qe->rkq", quarters, enc_up, preferred_element_type=F32).astype(BF)
    own_in = lax.dynamic_slice_in_dim(quarters, sec * block, block, 1)
    cot_block = lax.dynamic_slice_in_dim(cot, sec * (width // sections), width // sections, 1)
    out_block = lax.dynamic_slice_in_dim(proj_out, sec * (width // sections), width // sections, 1)

    d_proj32 = d_proj.astype(F32)
    mean = jnp.sum(d_proj32 * group_proj_pre, axis=1, keepdims=True) / (4 * enc_width)
    d_scaled = (d_proj32 * group_proj_scale).astype(BF)
    pull = jnp.repeat(mean * group_proj_scale * group_proj_scale, 4, axis=0)
    d_enc = dot_nn(d_scaled, cross.reshape(rank, -1)).reshape(-1, rank)
    d_enc = ((d_enc - pull * group_inner) * gelu_slope(group_enc_pre)).astype(BF)
    part_enc_down = dot_tn(enc_cols, d_enc)
    inner = jnp.einsum(
        "ir,ika->kra", d_scaled, group_act.reshape(-1, 4, rank), preferred_element_type=F32
    ).astype(BF)
    part_enc_up = jnp.einsum("ker,kra->ea", own_in, inner, preferred_element_type=F32)
    part_enc_up = part_enc_up - dot_tn(out_cols, (pull * group_act.astype(F32)).astype(BF))
    part_proj_in = dot_tn(normed_cols, d_proj)
    part_out = dot_tn(cot_block, placed) - dot_tn(
        out_block, dot_tn(placed, placed_scaled).astype(BF)
    )
    parts = jnp.concatenate(
        [
            part.astype(BF).reshape(groups, -1, rank)
            for part in (part_enc_down, part_enc_up, part_proj_in, part_out)
        ],
        axis=1,
    )
    parts = jnp.sum(lax.all_to_all(parts, "dp", 0, 0).astype(F32), axis=0)
    n_enc = block // groups
    n_in = 4 * n_enc
    grad_enc_down = parts[:n_enc]
    grad_enc_up = parts[n_enc:2 * n_enc].T
    grad_proj_in = parts[2 * n_enc:2 * n_enc + n_in]
    own_out = parts[2 * n_enc + n_in:]

    tall = (sections + 1) * rank
    layer_of = jnp.arange(tall, dtype=jnp.int32)[:, None] // rank - 1
    pair_coef = coef[:tall]
    self_coef = coef[tall:]
    zero = jnp.zeros_like(pair_coef)
    low_coef = jnp.where(layer_of < sec, pair_coef, zero)
    high_coef = jnp.where(layer_of > sec, pair_coef, zero)[rank:]
    all_grad = factors[:, 0].reshape(-1, rank)
    all_act = factors[:, 1].reshape(-1, rank)
    all_scaled = factors[:, 2].reshape(-1, rank)
    grad_dec_down = dot_tn(text_cols, all_grad) + dot_tn(up_slices, low_coef)
    grad_dec_up = (
        dot_tn(all_act, cot_cols)
        - dot_tn(all_scaled, text_cols)
        + dot_tn(high_coef, down_slices)
        - dot_tn(self_coef, up_slices)
    )

    few_cols = width // (sections * groups)
    down_pick = lax.dynamic_slice_in_dim(
        weight_down.reshape(sections, -1, rank), grp * few_cols, few_cols, 1
    ).reshape(-1, rank)
    up_pick = lax.dynamic_slice_in_dim(
        weight_up.reshape(rank, sections, -1), grp * few_cols, few_cols, 2
    ).reshape(rank, -1)
    term = dot_nt(down_pick, pair_coef[:rank]) - dot(up_pick, self_coef[:rank], (0, 1))
    term = lax.all_to_all(term.astype(BF).reshape(sections, few_cols, rank), "section", 0, 0)
    grad_proj_out = (own_out + jnp.sum(term.astype(F32), axis=0)).T
    return (
        grad_dec_down[None],
        grad_dec_up[None],
        grad_enc_down,
        grad_enc_up,
        grad_proj_in,
        grad_proj_out,
    )


def solution(mesh):
    placed = (
        P("dp", None, None),
        P("dp", None, None),
        P("section", None, None),
        P("section", None, None),
        P("dp", "section", None, None, None),
        P(),
        P(),
        P(),
        P(),
        P("dp", None),
    )
    return jax.shard_map(
        shards,
        mesh=mesh,
        in_specs=placed,
        out_specs=(
            P("section", "dp", None),
            P("section", None, "dp"),
            P(("section", "dp"), None),
            P(None, ("section", "dp")),
            P(("section", "dp"), None),
            P(None, ("section", "dp")),
        ),
        check_vma=False,
    )
```

time: 1440 us -> 307 us (0.21)
  blocking collectives: 363 us -> 24.5 us
  waiting for transfers between devices: 379 us -> 46 us
  starting transfers between devices: 298 us -> 43 us
  matrix products: 169 us -> 46.7 us
  other arithmetic: 107 us -> 27.1 us
    unnamed x1 -> x0, blocking collectives: 363 us -> none
    unnamed x70 -> x0, starting transfers between devices: 194 us -> none
    reduce_scatter x3 -> x0, waiting for transfers between devices: 165 us -> none  [the longest x1 165 us: shards(): lax.psum_scatter(part_proj_out, ('section', 'dp'), scatter_dimension=1, t...]
    dot_general x71 -> x27, matrix products: 169 us -> 46.7 us  [the longest x25 42.1 us: dot(): lax.dot_general(left, right, ((dims[:1], dims[1:]), ((), ())), preferred_...]
    ppermute x22 -> x7, waiting for transfers between devices: 120 us -> 0.02 us  [section_gather(): parts.append(lax.ppermute(value, 'section', pairs))]
    ppermute x22 -> x7, starting transfers between devices: 104 us -> 6.79 us  [section_gather(): parts.append(lax.ppermute(value, 'section', pairs))]
    dynamic_update_slice x33 -> x0, other arithmetic: 77 us -> none  [the longest x22 54.4 us: keep(): lax.dynamic_update_index_in_dim(buffer, jnp.where(valid, value, previous)...]
    psum x1 -> x0, waiting for transfers between devices: 64.5 us -> none  [from_root(): return lax.psum(block, axis)]
  transfers between devices with their start and end apart: 97 -> 18, of which waited for: 26 -> 5; matrix products, arithmetic and copies ran while one was open for 32% -> 48% of each run, Pallas kernels for 0% -> 2%
where the time goes in v1:
time: 307 us; the launch traced here: 304 us
  local copies, waits for them, and re-layouts  96.9 us (32%)
  matrix products  46.7 us (15%)
  waiting for transfers between devices  46 us (15%)
  starting transfers between devices  43 us (14%)
  other arithmetic  27.1 us (9%)
  blocking collectives  24.5 us (8%)
  between operations  14.1 us (5%)
  Pallas kernels  5.29 us (2%)
    unnamed x75, local copies, waits for them, and re-layouts  46.1 us
    dot_general x25, matrix products, dot(): lax.dot_general(left, right, ((dims[:1], dims[1:]), ((), ())), preferred_...  42.1 us
    all_gather x1, blocking collectives, shards(): coef = lax.all_gather(coef, 'dp', axis=0, tiled=True)  24.5 us
    all_gather x1, waiting for transfers between devices, shards(): up_rows = lax.all_gather(own_rows, 'section', axis=0)  19.9 us
    all_to_all x1, waiting for transfers between devices, shards(): coef = lax.all_to_all(coef.reshape(groups, -1, rank), 'dp', 0, 0)  10.9 us
    all_to_all x1, starting transfers between devices, shards(): coef = lax.all_to_all(coef.reshape(groups, -1, rank), 'dp', 0, 0)  7.21 us
    all_to_all x1, starting transfers between devices, shards(): cot_cols = lax.all_to_all(cot_late, 'dp', 1, 0, tiled=True)  7.07 us
    ppermute x7, starting transfers between devices, section_gather(): parts.append(lax.ppermute(value, 'section', pairs))  6.79 us
  transfers between devices with their start and end apart: 18, of which 5 were waited for; matrix products, arithmetic and copies ran while one was open for 48% of the time, Pallas kernels for 2%

profile of v1, /device:TPU:0, one launch (start us, length us, event | category | flops | bytes accessed | tf_op | source)
XLA Modules:
  0.0 303.6 jit_solution(4560417641349951730)
XLA Ops:
  11.8 3.6 %fusion.33 = bf16[544,128]{1,0:T(8,128)(2,1)} fusion(bf16[1,8192,128]{2,1,0:T(8,128)(2,1)} %param.12, bf16[1,128,8192]{2,1,0:T(8,128)(2,1)} %param.10, pred[128]{0:T(512)(128)(4,1)S(1)} %get-tuple-element.36), kind=kOutput, calls=%fused_computation.48 | convolution fusion | flops 269500416 | bytes 4227200 | tf_op jit(solution)/shard_map/dot_general | solution.py:32
  16.3 19.9 %all-gather.7.cloned.1.call-done = bf16[8,8,8192]{2,1,0:T(8,128)(2,1)} async-done(((bf16[1,8,8192]{2,1,0:T(8,128)(2,1)}), bf16[8,8,8192]{2,1,0:T(8,128)(2,1)}) %all-gather.7.cloned.1.call-update) | async-done | bytes 1048592 | tf_op jit(solution)/shard_map/all_gather | solution.py:197
  36.1 2.9 fusion.65
  40.4 3.7 %fusion.43 = bf16[544,128]{1,0:T(8,128)(2,1)} fusion(bf16[544,128]{1,0:T(8,128)(2,1)} %fusion.33, bf16[1,128,8192]{2,1,0:T(8,128)(2,1)} %param.13, bf16[1,128,8192]{2,1,0:T(8,128)(2,1)} %param.10, pred[128]{0:T(512)(128)(4,1)S(1)} %get-tuple-element.36), kind=kOutput, calls=%fused_computation.50 | convolution fusion | flops 269500416 | bytes 4227200 | tf_op jit(solution)/shard_map/dot_general | solution.py:32
  60.3 3.0 all_to_all.68
  65.3 4.2 %all-to-all-start.3 = ((bf16[64,8,400]{2,0,1:T(8,128)(2,1)}), bf16[64,8,400]{2,0,1:T(8,128)(2,1)}, u32[]{:S(2)}, u32[]{:S(2)}) async-start(bf16[64,8,400]{2,0,1:T(8,128)(2,1)} %copy.61), calls=%async_computation.3 | async-start | bytes 1048576 | tf_op jit(solution)/shard_map/all_to_all | solution.py:249
  69.6 4.1 %copy.53 = bf16[1,128,8192]{1,2,0:T(8,128)(2,1)} copy(bf16[1,128,8192]{2,1,0:T(8,128)(2,1)} %param.10) | data formatting | bytes 4194304 | tf_op args[0]
  79.9 4.1 %multiply_reduce_fusion = (f32[128]{0:T(128)S(1)}, bf16[128,8192]{0,1:T(8,128)(2,1)}) fusion(bf16[1,128,8192]{1,2,0:T(8,128)(2,1)} %copy.53, pred[128]{0:T(512)(128)(4,1)S(1)} %get-tuple-element.36), kind=kLoop, calls=%fused_computation.2 | loop fusion | flops 4194176 | bytes 4194944 | tf_op jit(solution)/shard_map/reduce_sum | solution.py:211
  89.3 4.1 %copy.66 = bf16[1,128,8192]{1,2,0:T(8,128)(2,1)} copy(bf16[1,128,8192]{2,1,0:T(8,128)(2,1)} %param.13) | data formatting | bytes 4194304 | tf_op args[3]
  93.4 4.1 %copy.54 = bf16[1,128,8192]{1,2,0:T(8,128)(2,1)} copy(bf16[1,128,8192]{2,1,0:T(8,128)(2,1)} %param.11) | data formatting | bytes 4194304 | tf_op args[1]
  119.8 4.2 %all-to-all-start.4 = ((bf16[16,8,1600]{2,0,1:T(8,128)(2,1)}), bf16[16,8,1600]{2,0,1:T(8,128)(2,1)}, u32[]{:S(2)}, u32[]{:S(2)}) async-start(bf16[16,8,1600]{2,0,1:T(8,128)(2,1)} %fusion.76), calls=%async_computation.4 | async-start | bytes 851968 | tf_op jit(solution)/shard_map/all_to_all | solution.py:250
  127.2 6.3 %all-to-all-done.4 = bf16[16,8,1600]{2,0,1:T(8,128)(2,1)} async-done(((bf16[16,8,1600]{2,0,1:T(8,128)(2,1)}), bf16[16,8,1600]{2,0,1:T(8,128)(2,1)}, u32[]{:S(2)}, u32[]{:S(2)}) %all-to-all-start.4) | async-done | bytes 409632 | tf_op jit(solution)/shard_map/all_to_all | solution.py:250
  133.5 7.1 %all-to-all-start.2 = ((bf16[128,16,512]{0,2,1:T(8,128)(2,1)}), bf16[128,16,512]{0,2,1:T(8,128)(2,1)}, u32[]{:S(2)}, u32[]{:S(2)}) async-start(bf16[128,16,512]{0,2,1:T(8,128)(2,1)} %bitcast.242), calls=%async_computation.2 | async-start | bytes 4194304 | tf_op jit(solution)/shard_map/all_to_all | solution.py:253
  148.8 5.3 %shard_map.145 = (bf16[18,128,128]{2,1,0:T(8,128)(2,1)S(1)}, bf16[3,128,128]{2,1,0:T(8,128)(2,1)S(1)}, bf16[3,128,128]{2,1,0:T(8,128)(2,1)S(1)}) custom-call(s32[1]{0:T(128)} %bitcast.6.place_ref, bf16[128,144,128]{2,1,0:T(8,128)(2,1)S(1)} %copy-done.1, bf16[8,544,128]{2,1,0:T(8,128)(2,1)S(1)} %copy-done.2, f32[128,128]{1,0:T(8,128)S(1)} %fusion.1.cot_ref, ...), custom_call_target="tpu_custom_call" | custom-call | tf_op jit(solution)/shard_map/pallas_call | solution.py:140
  176.0 7.2 %all-to-all-start.1 = ((bf16[16,144,128]{2,1,0:T(8,128)(2,1)}), bf16[16,144,128]{2,1,0:T(8,128)(2,1)}, u32[]{:S(2)}, u32[]{:S(2)}) async-start(bf16[16,144,128]{2,1,0:T(8,128)(2,1)} %bitcast.238), calls=%async_computation.1 | async-start | bytes 1179648 | tf_op jit(solution)/shard_map/all_to_all | solution.py:278
  187.0 10.9 %all-to-all-done.1 = bf16[16,144,128]{2,1,0:T(8,128)(2,1)} async-done(((bf16[16,144,128]{2,1,0:T(8,128)(2,1)}), bf16[16,144,128]{2,1,0:T(8,128)(2,1)}, u32[]{:S(2)}, u32[]{:S(2)}) %all-to-all-start.1) | async-done | bytes 589856 | tf_op jit(solution)/shard_map/all_to_all | solution.py:278
  198.0 4.4 %all-to-all-start = ((bf16[128,16,512]{0,2,1:T(8,128)(2,1)}), bf16[128,16,512]{0,2,1:T(8,128)(2,1)}, u32[]{:S(2)}, u32[]{:S(2)}) async-start(bf16[128,16,512]{0,2,1:T(8,128)(2,1)} %bitcast.241), calls=%async_computation | async-start | bytes 4194304 | tf_op jit(solution)/shard_map/all_to_all | solution.py:252
  222.8 24.5 %all_gather.28 = bf16[2304,128]{1,0:T(8,128)(2,1)S(1)} all-gather(bf16[144,128]{1,0:T(8,128)(2,1)} %reduce_sum.78), channel_id=1, replica_groups=mesh['section'=8,'dp'=16] {'dp'}, dimensions={0}, use_global_device_ids=true | all-gather | bytes 626688 | tf_op jit(solution)/shard_map/all_gather | solution.py:280
  250.2 4.0 %all-to-all-start.6 = ((bf16[8,64,128]{2,1,0:T(8,128)(2,1)}), bf16[8,64,128]{2,1,0:T(8,128)(2,1)}, u32[]{:S(2)}, u32[]{:S(2)}) async-start(bf16[8,64,128]{2,1,0:T(8,128)(2,1)} %bitcast.261), calls=%async_computation.6 | async-start | bytes 262144 | tf_op jit(solution)/shard_map/all_to_all | solution.py:362
  256.5 3.8 %all-to-all-done.6 = bf16[8,64,128]{2,1,0:T(8,128)(2,1)} async-done(((bf16[8,64,128]{2,1,0:T(8,128)(2,1)}), bf16[8,64,128]{2,1,0:T(8,128)(2,1)}, u32[]{:S(2)}, u32[]{:S(2)}) %all-to-all-start.6) | async-done | bytes 131104 | tf_op jit(solution)/shard_map/all_to_all | solution.py:362
  260.4 4.9 %all-to-all-start.5 = ((bf16[16,214,128]{2,1,0:T(8,128)(2,1)}), bf16[16,214,128]{2,1,0:T(8,128)(2,1)}, u32[]{:S(2)}, u32[]{:S(2)}) async-start(bf16[16,214,128]{2,1,0:T(8,128)(2,1)} %pad_maximum_fusion.2), calls=%async_computation.5 | async-start | bytes 1769472 | tf_op jit(solution)/shard_map/all_to_all | solution.py:328
  267.0 3.9 %copy.60 = bf16[16,128,512]{2,1,0:T(8,128)(2,1)} copy(bf16[16,128,512]{1,2,0:T(8,128)(2,1)} %bitcast.36) | data formatting | bytes 4194304 | tf_op jit(solution)/shard_map/all_to_all | solution.py:253
  270.9 3.9 %copy.55 = bf16[16,128,512]{2,1,0:T(8,128)(2,1)} copy(bf16[16,128,512]{1,2,0:T(8,128)(2,1)} %bitcast.4) | data formatting | bytes 4194304 | tf_op jit(solution)/shard_map/all_to_all | solution.py:252
  275.7 5.0 %all-to-all-done.5 = bf16[16,214,128]{2,1,0:T(8,128)(2,1)} async-done(((bf16[16,214,128]{2,1,0:T(8,128)(2,1)}), bf16[16,214,128]{2,1,0:T(8,128)(2,1)}, u32[]{:S(2)}, u32[]{:S(2)}) %all-to-all-start.5) | async-done | bytes 876576 | tf_op jit(solution)/shard_map/all_to_all | solution.py:328
  (191 shorter events, 140.3 us)
Async XLA Ops:
  7.2 45.4 %copy-start = (bf16[12800,128]{1,0:T(8,128)(2,1)S(1)}, bf16[12800,128]{1,0:T(8,128)(2,1)}, u32[]{:S(2)}) copy-start(bf16[12800,128]{1,0:T(8,128)(2,1)} %param.17) | copy-start | bytes 9830404
  7.2 28.9 %all-gather.7.cloned.1.call-start = ((), (), s32[]{:S(2)}) async-start(), calls=%async_computation.7 | async-start | bytes 1179648 | tf_op jit(solution)/shard_map/all_gather | solution.py:197
  9.0 135.5 %all-gather.9.cloned.1.call-start = ((), (), s32[]{:S(2)}) async-start(), calls=%async_computation.8 | async-start | bytes 4755456 | tf_op jit(solution)/shard_map/all_gather | solution.py:247
  36.1 2.9 copy-start.17
  40.4 3.7 %copy-start.7 = (bf16[1,128,8192]{2,1,0:T(8,128)(2,1)S(1)}, bf16[1,128,8192]{2,1,0:T(8,128)(2,1)}, u32[]{:S(2)}) copy-start(bf16[1,128,8192]{2,1,0:T(8,128)(2,1)} %param.13) | copy-start | bytes 6291460
  40.4 3.7 %copy-start.8 = (bf16[1,128,8192]{2,1,0:T(8,128)(2,1)S(1)}, bf16[1,128,8192]{2,1,0:T(8,128)(2,1)}, u32[]{:S(2)}) copy-start(bf16[1,128,8192]{2,1,0:T(8,128)(2,1)} %param.11) | copy-start | bytes 6291460
  55.5 44.5 %collective-permute-start = (bf16[544,128]{1,0:T(8,128)(2,1)}, bf16[544,128]{1,0:T(8,128)(2,1)}, u32[]{:S(2)}, u32[]{:S(2)}) collective-permute-start(bf16[544,128]{1,0:T(8,128)(2,1)} %constant_dynamic-update-slice_fusion), channel_id=1, source_target_pairs={{16,0},{32,16},{48,32},{64,48},{80,64},{96,80},{112,96},{0,112},{1... | collective-permute-start | bytes 417800 | tf_op jit(solution)/shard_map/ppermute | solution.py:170
  56.4 47.2 %collective-permute-start.1 = (bf16[544,128]{1,0:T(8,128)(2,1)}, bf16[544,128]{1,0:T(8,128)(2,1)}, u32[]{:S(2)}, u32[]{:S(2)}) collective-permute-start(bf16[544,128]{1,0:T(8,128)(2,1)} %constant_dynamic-update-slice_fusion), channel_id=1, source_target_pairs={{32,0},{48,16},{64,32},{80,48},{96,64},{112,80},{0,96},{16,112},{3... | collective-permute-start | bytes 417800 | tf_op jit(solution)/shard_map/ppermute | solution.py:170
  57.5 47.7 %collective-permute-start.2 = (bf16[544,128]{1,0:T(8,128)(2,1)}, bf16[544,128]{1,0:T(8,128)(2,1)}, u32[]{:S(2)}, u32[]{:S(2)}) collective-permute-start(bf16[544,128]{1,0:T(8,128)(2,1)} %constant_dynamic-update-slice_fusion), channel_id=1, source_target_pairs={{48,0},{64,16},{80,32},{96,48},{112,64},{0,80},{16,96},{32,112},{4... | collective-permute-start | bytes 417800 | tf_op jit(solution)/shard_map/ppermute | solution.py:170
  57.5 49.3 %collective-permute-start.3 = (bf16[544,128]{1,0:T(8,128)(2,1)}, bf16[544,128]{1,0:T(8,128)(2,1)}, u32[]{:S(2)}, u32[]{:S(2)}) collective-permute-start(bf16[544,128]{1,0:T(8,128)(2,1)} %constant_dynamic-update-slice_fusion), channel_id=1, source_target_pairs={{64,0},{80,16},{96,32},{112,48},{0,64},{16,80},{32,96},{48,112},{6... | collective-permute-start | bytes 417800 | tf_op jit(solution)/shard_map/ppermute | solution.py:170
  59.9 48.5 %collective-permute-start.4 = (bf16[544,128]{1,0:T(8,128)(2,1)}, bf16[544,128]{1,0:T(8,128)(2,1)}, u32[]{:S(2)}, u32[]{:S(2)}) collective-permute-start(bf16[544,128]{1,0:T(8,128)(2,1)} %constant_dynamic-update-slice_fusion), channel_id=1, source_target_pairs={{80,0},{96,16},{112,32},{0,48},{16,64},{32,80},{48,96},{64,112},{8... | collective-permute-start | bytes 417800 | tf_op jit(solution)/shard_map/ppermute | solution.py:170
  65.3 54.5 %all-to-all-start.3 = ((bf16[64,8,400]{2,0,1:T(8,128)(2,1)}), bf16[64,8,400]{2,0,1:T(8,128)(2,1)}, u32[]{:S(2)}, u32[]{:S(2)}) async-start(bf16[64,8,400]{2,0,1:T(8,128)(2,1)} %copy.61), calls=%async_computation.3 | async-start | bytes 1048576 | tf_op jit(solution)/shard_map/all_to_all | solution.py:249
  79.9 4.1 %copy-start.6 = (bf16[128,8192]{1,0:T(8,128)(2,1)S(1)}, bf16[128,8192]{1,0:T(8,128)(2,1)}, u32[]{:S(2)}) copy-start(bf16[128,8192]{1,0:T(8,128)(2,1)} %param.18) | copy-start | bytes 6291460
  100.1 9.9 %collective-permute-start.5 = (bf16[544,128]{1,0:T(8,128)(2,1)}, bf16[544,128]{1,0:T(8,128)(2,1)S(1)}, u32[]{:S(2)}, u32[]{:S(2)}) collective-permute-start(bf16[544,128]{1,0:T(8,128)(2,1)} %constant_dynamic-update-slice_fusion), channel_id=1, source_target_pairs={{96,0},{112,16},{0,32},{16,48},{32,64},{48,80},{64,96},{80,112},{9... | collective-permute-start | bytes 417800 | tf_op jit(solution)/shard_map/ppermute | solution.py:170
  103.6 7.1 %collective-permute-start.6 = (bf16[544,128]{1,0:T(8,128)(2,1)}, bf16[544,128]{1,0:T(8,128)(2,1)S(1)}, u32[]{:S(2)}, u32[]{:S(2)}) collective-permute-start(bf16[544,128]{1,0:T(8,128)(2,1)} %constant_dynamic-update-slice_fusion), channel_id=1, source_target_pairs={{112,0},{0,16},{16,32},{32,48},{48,64},{64,80},{80,96},{96,112},{1... | collective-permute-start | bytes 417800 | tf_op jit(solution)/shard_map/ppermute | solution.py:170
  119.8 13.6 %all-to-all-start.4 = ((bf16[16,8,1600]{2,0,1:T(8,128)(2,1)}), bf16[16,8,1600]{2,0,1:T(8,128)(2,1)}, u32[]{:S(2)}, u32[]{:S(2)}) async-start(bf16[16,8,1600]{2,0,1:T(8,128)(2,1)} %fusion.76), calls=%async_computation.4 | async-start | bytes 851968 | tf_op jit(solution)/shard_map/all_to_all | solution.py:250
  133.5 42.5 %all-to-all-start.2 = ((bf16[128,16,512]{0,2,1:T(8,128)(2,1)}), bf16[128,16,512]{0,2,1:T(8,128)(2,1)}, u32[]{:S(2)}, u32[]{:S(2)}) async-start(bf16[128,16,512]{0,2,1:T(8,128)(2,1)} %bitcast.242), calls=%async_computation.2 | async-start | bytes 4194304 | tf_op jit(solution)/shard_map/all_to_all | solution.py:253
  140.5 143.4 %all-gather.11.cloned.1.call-start = ((), (), s32[]{:S(2)}) async-start(), calls=%async_computation.9 | async-start | bytes 1671168 | tf_op jit(solution)/shard_map/all_gather | solution.py:277
  176.0 22.0 %all-to-all-start.1 = ((bf16[16,144,128]{2,1,0:T(8,128)(2,1)}), bf16[16,144,128]{2,1,0:T(8,128)(2,1)}, u32[]{:S(2)}, u32[]{:S(2)}) async-start(bf16[16,144,128]{2,1,0:T(8,128)(2,1)} %bitcast.238), calls=%async_computation.1 | async-start | bytes 1179648 | tf_op jit(solution)/shard_map/all_to_all | solution.py:278
  198.0 52.2 %all-to-all-start = ((bf16[128,16,512]{0,2,1:T(8,128)(2,1)}), bf16[128,16,512]{0,2,1:T(8,128)(2,1)}, u32[]{:S(2)}, u32[]{:S(2)}) async-start(bf16[128,16,512]{0,2,1:T(8,128)(2,1)} %bitcast.241), calls=%async_computation | async-start | bytes 4194304 | tf_op jit(solution)/shard_map/all_to_all | solution.py:252
  202.4 87.0 %all-gather.13.cloned.1.call-start = ((), (), s32[]{:S(2)}) async-start(), calls=%async_computation.10 | async-start | bytes 2359296 | tf_op jit(solution)/shard_map/all_gather | solution.py:263
  220.9 33.3 %copy-start.21 = (bf16[1024,128]{1,0:T(8,128)(2,1)S(1)}, bf16[1024,128]{1,0:T(8,128)(2,1)}, u32[]{:S(2)}) copy-start(bf16[1024,128]{1,0:T(8,128)(2,1)} %fusion.18) | copy-start | bytes 786436
  250.2 10.1 %all-to-all-start.6 = ((bf16[8,64,128]{2,1,0:T(8,128)(2,1)}), bf16[8,64,128]{2,1,0:T(8,128)(2,1)}, u32[]{:S(2)}, u32[]{:S(2)}) async-start(bf16[8,64,128]{2,1,0:T(8,128)(2,1)} %bitcast.261), calls=%async_computation.6 | async-start | bytes 262144 | tf_op jit(solution)/shard_map/all_to_all | solution.py:362
  260.4 20.4 %all-to-all-start.5 = ((bf16[16,214,128]{2,1,0:T(8,128)(2,1)}), bf16[16,214,128]{2,1,0:T(8,128)(2,1)}, u32[]{:S(2)}, u32[]{:S(2)}) async-start(bf16[16,214,128]{2,1,0:T(8,128)(2,1)} %pad_maximum_fusion.2), calls=%async_computation.5 | async-start | bytes 1769472 | tf_op jit(solution)/shard_map/all_to_all | solution.py:328
  (22 other events, 31.7 us)
Sparse Core Ops, SparseCore 0:
  10.3 25.7 all-gather.6
  40.4 68.0 all-gather.8
  155.8 51.3 all-gather.10
  212.8 26.9 all-gather.12

commit v2 on v1

v2 whole, which is shorter than its diff:
```python
import functools

import jax
import jax.numpy as jnp
from jax import lax
from jax.experimental import pallas as pl
from jax.experimental.pallas import tpu as pltpu
from jax.sharding import PartitionSpec as P

EPS = 1e-06
GELU_C = 0.7978845608028654
BF = jnp.bfloat16
F32 = jnp.float32


def gelu_tanh(value):
    return 0.5 * value * (1.0 + jnp.tanh(GELU_C * (value + 0.044715 * value * value * value)))


def gelu_slope(value):
    inner = jnp.tanh(GELU_C * (value + 0.044715 * value * value * value))
    return 0.5 * (1.0 + inner) + 0.5 * value * (1.0 - inner * inner) * GELU_C * (
        1.0 + 3.0 * 0.044715 * value * value
    )


def norm_scale(rows32):
    return lax.rsqrt(jnp.mean(rows32 * rows32, axis=-1, keepdims=True) + EPS)


def dot(left, right, dims):
    return lax.dot_general(left, right, ((dims[:1], dims[1:]), ((), ())), preferred_element_type=F32)


def dot_nn(left, right):
    return dot(left, right, (1, 0))


def dot_tn(left, right):
    return dot(left, right, (0, 0))


def dot_nt(left, right):
    return dot(left, right, (1, 1))


RANK = 128
VMEM = pl.BlockSpec(memory_space=pltpu.VMEM)
SMEM = pl.BlockSpec(memory_space=pltpu.SMEM)
PARAMS = pltpu.CompilerParams(vmem_limit_bytes=48 * 1024 * 1024)


def scalars(*values):
    return jnp.stack(values).astype(jnp.int32)


def text_kernel(
    steps, kept,
    start_ref, keep_ref, text_ref, cot_ref, down_ref, up_ref, out_ref,
    cols_ref, proj_ref, image_ref, norm_ref, gram_ref,
    proj, image, gram,
):
    step = pl.program_id(0)

    @pl.when(step == 0)
    def _():
        proj[...] = jnp.zeros_like(proj)
        image[...] = jnp.zeros_like(image)
        gram[...] = jnp.zeros_like(gram)
        norm_ref[...] = jnp.zeros_like(norm_ref)

    rows = text_ref.shape[0]
    text32 = text_ref[...].astype(F32) * keep_ref[...]
    text = text32.astype(BF)
    cot = cot_ref[...]
    norm_ref[...] += jnp.sum(text32 * text32, axis=1, keepdims=True)
    proj[:RANK] += dot_nn(text, down_ref[...])
    proj[RANK:2 * RANK] += dot_nt(text, up_ref[...])
    proj[2 * RANK:] += dot_nt(cot, up_ref[...])
    image[...] += dot_nt(cot, out_ref[...])
    gram[...] += dot_nt(out_ref[...], out_ref[...])

    @pl.when(step < kept)
    def _():
        cols_ref[0, :rows, :] = text
        cols_ref[0, rows:, :] = cot

    @pl.when(step == steps - 1)
    def _():
        proj_ref[...] = proj[...].astype(BF)
        image_ref[...] = image[...]
        gram_ref[...] = gram[...].astype(BF)


def text_products(start, keep, text, cot, down, up, out, groups):
    rows, width = text.shape
    share = width // groups
    kept = groups // 2
    across = pl.BlockSpec((rows, share), lambda i, at: (0, (at[0] + i) % groups))
    fixed = pl.BlockSpec((rows, RANK), lambda i, at: (0, 0))
    column = pl.BlockSpec((rows, 1), lambda i, at: (0, 0))
    return pl.pallas_call(
        functools.partial(text_kernel, groups, kept),
        grid_spec=pltpu.PrefetchScalarGridSpec(
            num_scalar_prefetch=1,
            grid=(groups,),
            in_specs=[
                column,
                across,
                across,
                pl.BlockSpec((share, RANK), lambda i, at: ((at[0] + i) % groups, 0)),
                across,
                across,
            ],
            out_specs=[
                pl.BlockSpec(
                    (1, 2 * rows, share), lambda i, at: (jnp.minimum(i, kept - 1), 0, 0)
                ),
                pl.BlockSpec((3 * RANK, RANK), lambda i, at: (0, 0)),
                fixed,
                column,
                fixed,
            ],
            scratch_shapes=[
                pltpu.VMEM((3 * RANK, RANK), F32),
                pltpu.VMEM((rows, RANK), F32),
                pltpu.VMEM((RANK, RANK), F32),
            ],
        ),
        out_shape=[
            jax.ShapeDtypeStruct((kept, 2 * rows, share), BF),
            jax.ShapeDtypeStruct((3 * RANK, RANK), BF),
            jax.ShapeDtypeStruct((rows, RANK), F32),
            jax.ShapeDtypeStruct((rows, 1), F32),
            jax.ShapeDtypeStruct((RANK, RANK), BF),
        ],
        compiler_params=PARAMS,
    )(scalars(start), keep, text, cot, down, up, out)


def two_lanes(column):
    high = column.astype(BF).astype(F32)
    lane = lax.broadcasted_iota(jnp.int32, (column.shape[0], RANK), 1)
    zero = jnp.zeros((column.shape[0], RANK), F32)
    return jnp.where(lane == 0, high, jnp.where(lane == 1, column - high, zero)).astype(BF)


def front_kernel(
    sections, windows, in_windows,
    place_ref, patch_ref, down_ref, up_ref, in_ref,
    pre_ref, cols_ref, cross_ref,
    patch, enc, inner, state, tiles,
):
    rows, width = patch_ref.shape
    count = width // RANK
    quarter = rows // 4

    def keep_tiles(ref, value):
        for m in range(count):
            ref[m] = value[:, m * RANK:(m + 1) * RANK]

    def fourth(ref, k):
        return jnp.concatenate(
            [ref[m, pl.ds(k, quarter, stride=4), :] for m in range(count)], axis=1
        )

    patch32 = patch_ref[...].astype(F32)
    keep_tiles(patch, patch32)
    scale = norm_scale(patch32)
    pre = dot_nn((patch32 * scale).astype(BF), down_ref[...])
    act = gelu_tanh(pre).astype(BF)
    out = (patch32 + dot_nn(act, up_ref[...])).astype(BF)
    keep_tiles(enc, out.astype(F32))
    inner[...] = dot_nt(out, up_ref[...])
    state[...] = pre
    total = jnp.zeros((quarter, 1), F32)
    for k in range(4):
        part = fourth(enc, k)
        total = total + jnp.sum(part * part, axis=1, keepdims=True)
    merged_scale = lax.rsqrt(total * (1.0 / (4 * width)) + EPS)
    proj = jnp.zeros((quarter, RANK), F32)
    for k in range(4):
        normed = (fourth(enc, k) * merged_scale).astype(BF)
        proj = proj + dot_nn(normed, in_ref[k])
        cross_ref[:, k * RANK:(k + 1) * RANK] = dot(in_ref[k], up_ref[...], (0, 1)).astype(BF)
        for m in range(count):
            tiles[k, m] = normed[:, m * RANK:(m + 1) * RANK]
        head = [
            state[pl.ds(k, quarter, stride=4), :].astype(BF),
            inner[pl.ds(k, quarter, stride=4), :].astype(BF),
            two_lanes(norm_scale(fourth(patch, k))),
        ]
        for step in range(sections):
            for at, value in enumerate(head):
                cols_ref[step, at * rows + k * quarter:at * rows + (k + 1) * quarter, :] = value
    merged_lanes = two_lanes(merged_scale)
    for step in range(sections):
        to = lax.rem(place_ref[0] + step, sections)
        base = 3 * rows
        cols_ref[step, base:base + quarter, :] = merged_lanes
        base += quarter
        for m in range(windows[1]):
            for k in range(4):
                tile = patch[to * (windows[0] // RANK) + m, pl.ds(k, quarter, stride=4), :]
                at = base + m * rows + k * quarter
                cols_ref[step, at:at + quarter, :] = tile.astype(BF)
        base += windows[1] * rows
        per = sections // 4
        for m in range(in_windows[1]):
            tile = tiles[to // per, lax.rem(to, per) * (in_windows[0] // RANK) + m]
            cols_ref[step, base + m * quarter:base + (m + 1) * quarter, :] = tile
    pre_ref[...] = proj.astype(BF)


def window(width, count):
    block = width // count
    stride = block // RANK * RANK
    tiles = -(-((count - 1) * (block - stride) + block) // RANK)
    return stride, tiles


def encoder_front(sec, patches, enc_down, enc_up, proj_in, sections):
    rows, width = patches.shape
    windows = window(width, sections)
    in_windows = window(width, sections // 4)
    total = 3 * rows + rows // 4 + windows[1] * rows + in_windows[1] * (rows // 4)
    return pl.pallas_call(
        functools.partial(front_kernel, sections, windows, in_windows),
        in_specs=[SMEM] + [VMEM] * 4,
        out_specs=[VMEM] * 3,
        out_shape=[
            jax.ShapeDtypeStruct((rows // 4, RANK), BF),
            jax.ShapeDtypeStruct((sections, total, RANK), BF),
            jax.ShapeDtypeStruct((RANK, 4 * RANK), BF),
        ],
        scratch_shapes=[
            pltpu.VMEM((width // RANK, rows, RANK), F32),
            pltpu.VMEM((width // RANK, rows, RANK), F32),
            pltpu.VMEM((rows, RANK), F32),
            pltpu.VMEM((rows, RANK), F32),
            pltpu.VMEM((4, width // RANK, rows // 4, RANK), BF),
        ],
        compiler_params=PARAMS,
    )(scalars(sec), patches, enc_down, enc_up, proj_in)


def pack_kernel(layers, core_ref, gram_ref, out_ref, packed):
    at = 0
    for l in range(layers):
        size = (l + 2) * 16
        packed[at:at + size, :] = gram_ref[l, :size, :]
        at += size
    half = at // 2
    value = packed[pl.ds(pl.multiple_of(core_ref[0] * half, 16), half), :]
    for to in range(out_ref.shape[0]):
        out_ref[to] = value


def pack_gram(core, gram, groups):
    layers = gram.shape[0]
    total = sum((l + 2) * 16 for l in range(layers))
    return pl.pallas_call(
        functools.partial(pack_kernel, layers),
        in_specs=[SMEM, VMEM],
        out_specs=VMEM,
        out_shape=jax.ShapeDtypeStruct((groups, total // 2, RANK), BF),
        scratch_shapes=[pltpu.VMEM((total, RANK), BF)],
        compiler_params=PARAMS,
    )(scalars(core), gram)


def rank_kernel(
    layers, width,
    place_ref, own_ref, other_ref, gath_ref, cot_ref, norm_ref, image_gram_ref, sel_ref,
    coef_ref, factor_ref, image_ref,
    weight, acts, act_cat, grads, scaled, back, pre_ref, slope_ref, inner_ref, scale_ref,
):
    rank = RANK
    own = place_ref[0]
    core = place_ref[1]
    at = 0
    for l in range(layers):
        for j in range(l + 2):
            which, place = divmod(at, own_ref.shape[1])
            span = slice(place, place + 16)
            tile = jnp.where(core == which, own_ref[:, span, :], other_ref[:, span, :])
            tile = tile.astype(F32)
            rows = slice(j * rank, (j + 1) * rank)
            weight[l, rows, :rank] = tile[:, :8, :].reshape(rank, rank).astype(BF)
            weight[l, rows, rank:] = tile[:, 8:, :].reshape(rank, rank).astype(BF)
            at += 16

    proj_half = jnp.concatenate(
        [gath_ref[l, 3 * rank:3 * rank + 16, :] for l in range(layers)], axis=0
    )
    proj_pre = proj_half.astype(F32)
    sel = sel_ref[...]
    placed = dot_nn(sel, gelu_tanh(proj_pre).astype(BF))
    placed_half = placed.astype(BF)
    acts[0] = placed_half
    act_cat[:, :rank] = placed_half
    image_inner = dot_nn(placed_half, image_gram_ref[...])
    total = norm_ref[...] + jnp.sum(placed * image_inner, axis=1, keepdims=True)
    for l in range(layers):
        here = (l + 1) * rank
        scale = lax.rsqrt(jnp.maximum(total, 0.0) * (1.0 / width) + EPS)
        both = dot_nn(act_cat[:, :here], weight[l, :here, :])
        pre = scale * (gath_ref[l, :rank, :].astype(F32) + both[:, :rank])
        inner = gath_ref[l, rank:2 * rank, :].astype(F32) + both[:, rank:]
        sig = jax.nn.sigmoid(pre)
        act = (pre * sig).astype(BF)
        acts[l + 1] = act
        act_cat[:, here:here + rank] = act
        after = inner + dot_nn(act, weight[l, here:here + rank, rank:])
        total = total + jnp.sum(act.astype(F32) * (inner + after), axis=1, keepdims=True)
        pre_ref[l] = pre
        slope_ref[l] = sig * (1.0 + pre * (1.0 - sig))
        inner_ref[l] = after
        scale_ref[l] = scale
    back[...] = jnp.zeros_like(back)
    sums = jnp.zeros_like(total)
    for l in reversed(range(layers)):
        here = (l + 1) * rank
        cot = gath_ref[l, 2 * rank:3 * rank, :].astype(F32)
        d_act = cot - sums * inner_ref[l] + back[:, here:here + rank]
        d_pre = (d_act * slope_ref[l]).astype(BF).astype(F32)
        scale = scale_ref[l]
        mean = jnp.sum(d_pre * pre_ref[l], axis=1, keepdims=True) * (1.0 / width)
        grad = (scale * d_pre).astype(BF)
        part = (sums * acts[l + 1].astype(F32)).astype(BF)
        grads[l] = grad
        scaled[l + 1] = part
        pair = jnp.concatenate([grad, -part], axis=1)
        back[:, :here] += dot_nt(pair, weight[l, :here, :])
        sums = sums + scale * scale * mean
    d_image = cot_ref[...] - sums * image_inner + back[:, :rank]
    scaled[0] = (sums * placed).astype(BF)
    d_slot = dot_tn(sel, d_image.astype(BF))
    image_ref[0] = (d_slot * gelu_slope(proj_pre)).astype(BF)
    image_ref[1] = placed_half
    image_ref[2] = scaled[0]
    image_ref[3] = proj_half

    own_act = acts[own + 1]
    own_grad = grads[own]
    own_scaled = scaled[own + 1]
    factor_ref[0] = own_grad
    factor_ref[1] = own_act
    factor_ref[2] = own_scaled
    coef_ref[0] = dot_tn(acts[0], own_grad).astype(BF)
    for l in range(layers):
        low = l < own
        left = jnp.where(low, acts[l + 1], grads[l])
        right = jnp.where(low, own_grad, own_act)
        coef_ref[l + 1] = dot_tn(left, right).astype(BF)
    for l in range(layers + 1):
        low = l <= own + 1
        left = jnp.where(low, acts[l], scaled[l])
        right = jnp.where(low, own_scaled, own_act)
        coef_ref[layers + 1 + l] = dot_tn(left, right).astype(BF)


def rank_space(position, core, gram, other, gath, cot, norms, image_gram, sel, width):
    layers = gath.shape[0]
    rank = RANK
    tall = (layers + 1) * rank
    return pl.pallas_call(
        functools.partial(rank_kernel, layers, width),
        in_specs=[SMEM] + [VMEM] * 7,
        out_specs=[VMEM] * 3,
        out_shape=[
            jax.ShapeDtypeStruct((2 * layers + 2, rank, rank), BF),
            jax.ShapeDtypeStruct((3, rank, rank), BF),
            jax.ShapeDtypeStruct((4, rank, rank), BF),
        ],
        scratch_shapes=[
            pltpu.VMEM((layers, tall, 2 * rank), BF),
            pltpu.VMEM((layers + 1, rank, rank), BF),
            pltpu.VMEM((rank, tall), BF),
            pltpu.VMEM((layers, rank, rank), BF),
            pltpu.VMEM((layers + 1, rank, rank), BF),
            pltpu.VMEM((rank, tall), F32),
            pltpu.VMEM((layers, rank, rank), F32),
            pltpu.VMEM((layers, rank, rank), F32),
            pltpu.VMEM((layers, rank, rank), F32),
            pltpu.VMEM((layers, rank, 1), F32),
        ],
        compiler_params=PARAMS,
    )(scalars(position, core), gram, other, gath, cot, norms, image_gram, sel)


def late_kernel(sections, enc_width, tiles, in_tiles, pieces, shift_ref, *refs):
    cols_refs = refs[:sections]
    image_ref, cross_ref, up_ref, in_ref, cot_ref, out_ref, part_ref = refs[sections:sections + 7]
    down, up, proj, last = refs[sections + 7:]
    few = RANK // sections
    many = 4 * few

    def arrived(index):
        rows = []
        for step in range(sections):
            source = lax.rem(shift_ref[3] + sections - step, sections)
            rows.append(image_ref[index, pl.ds(pl.multiple_of(source * few, few), few), :])
        return jnp.concatenate(rows, axis=0)

    d_proj = arrived(0)
    placed = image_ref[1]
    d_proj32 = d_proj.astype(F32)
    proj_pre = arrived(3).astype(F32)

    def group(start):
        return jnp.concatenate(
            [ref[start:start + few, :] for ref in cols_refs], axis=0
        )

    proj_scale = jnp.sum(group(3 * many).astype(F32), axis=1, keepdims=True)
    mean = jnp.sum(d_proj32 * proj_pre, axis=1, keepdims=True) * (1.0 / (4 * enc_width))
    d_scaled = (d_proj32 * proj_scale).astype(BF)
    pull = mean * proj_scale * proj_scale
    for k in range(4):
        at = k * few
        enc_pre = group(at).astype(F32)
        inner = group(many + at).astype(F32)
        scale = jnp.sum(group(2 * many + at).astype(F32), axis=1, keepdims=True)
        act = gelu_tanh(enc_pre).astype(BF)
        d_enc = dot_nn(d_scaled, cross_ref[:, k * RANK:(k + 1) * RANK]) - pull * inner
        d_enc = (d_enc * gelu_slope(enc_pre)).astype(BF)
        pulled = (pull * act.astype(F32)).astype(BF)
        value = dot_nn(in_ref[k], dot_tn(d_scaled, act).astype(BF))
        if k == 0:
            up[:tiles * RANK, :] = value
        else:
            up[:tiles * RANK, :] += value
        for m in range(tiles):
            rows = slice(m * RANK, (m + 1) * RANK)
            patch = group(3 * many + few + m * many + at).astype(F32)
            out = (patch + dot_nn(act, up_ref[:, rows])).astype(BF)
            up[rows, :] -= dot_tn(out, pulled)
            value = dot_tn((patch * scale).astype(BF), d_enc)
            if k == 0:
                down[rows, :] = value
            else:
                down[rows, :] += value
    base = 3 * many + few + tiles * many
    for m in range(in_tiles):
        proj[m * RANK:(m + 1) * RANK, :] = dot_tn(group(base + m * few), d_proj)
    last[...] = dot_tn(cot_ref[...], placed) - dot_tn(
        out_ref[...], dot_tn(placed, image_ref[2]).astype(BF)
    )
    groups = part_ref.shape[0]
    n_enc, n_in, pad_enc, pad_in = pieces
    n_out = last.shape[0] // groups
    for step in range(groups):
        to = lax.rem(shift_ref[2] + step, groups)
        at = shift_ref[0] + n_enc * to
        part_ref[step, :pad_enc, :] = down[pl.ds(at, pad_enc), :].astype(BF)
        part_ref[step, pad_enc:2 * pad_enc, :] = up[pl.ds(at, pad_enc), :].astype(BF)
        at = shift_ref[1] + n_in * to
        part_ref[step, 2 * pad_enc:2 * pad_enc + pad_in, :] = proj[pl.ds(at, pad_in), :].astype(BF)
        at = pl.multiple_of(to * n_out, n_out)
        part_ref[step, 2 * pad_enc + pad_in:, :] = last[pl.ds(at, n_out), :].astype(BF)


def encoder_late(sec, grp, cols, image, cross, own_up, own_in, cot, out, enc_width, groups):
    sections = len(cols)
    tiles = window(enc_width, sections)[1]
    in_tiles = window(enc_width, sections // 4)[1]
    n_enc = enc_width // sections // groups
    n_in = 4 * n_enc
    pad_enc = -(-n_enc // 16) * 16
    pad_in = -(-n_in // 16) * 16
    block = enc_width // sections
    in_block = 4 * block
    shifts = scalars(
        sec * (block % RANK), (sec % (sections // 4)) * (in_block % RANK), grp, sec
    )
    n_out = out.shape[1] // groups
    total = 2 * pad_enc + pad_in + n_out
    parts = pl.pallas_call(
        functools.partial(
            late_kernel, sections, enc_width, tiles, in_tiles, (n_enc, n_in, pad_enc, pad_in)
        ),
        in_specs=[SMEM] + [VMEM] * (sections + 6),
        out_specs=VMEM,
        out_shape=jax.ShapeDtypeStruct((groups, total, RANK), BF),
        scratch_shapes=[
            pltpu.VMEM((tiles * RANK + 16, RANK), F32),
            pltpu.VMEM((tiles * RANK + 16, RANK), F32),
            pltpu.VMEM((in_tiles * RANK + 16, RANK), F32),
            pltpu.VMEM((out.shape[1], RANK), F32),
        ],
        compiler_params=PARAMS,
    )(shifts, *cols, image, cross, own_up, own_in, cot, out)
    return parts, (n_enc, n_in, pad_enc, pad_in)


def sum_kernel(count, *refs):
    total = refs[0][...].astype(F32)
    for ref in refs[1:count]:
        total = total + ref[...].astype(F32)
    refs[count][...] = total


def sum_parts(parts):
    return pl.pallas_call(
        functools.partial(sum_kernel, len(parts)),
        in_specs=[VMEM] * len(parts),
        out_specs=VMEM,
        out_shape=jax.ShapeDtypeStruct(parts[0].shape, F32),
        compiler_params=PARAMS,
    )(*parts)


def last_kernel(layers, groups, place_ref, *refs):
    blocks = refs[:groups]
    factor_ref, coef_ref, down_ref, up_ref, out_ref, grad_down_ref, grad_up_ref = refs[groups:]
    sec, grp, core = place_ref[0], place_ref[1], place_ref[2]
    rows = blocks[0].shape[0] // 2
    half = groups // 2
    share = blocks[0].shape[1]
    total_down = jnp.zeros((share, RANK), F32)
    total_up = jnp.zeros((RANK, share), F32)
    for at, block in enumerate(blocks):
        part = core if at < half else 1 - core
        source = lax.rem(grp + 2 * groups - half * part - at % half, groups)
        text = block[:rows, :]
        total_down += dot_tn(text, factor_ref[source, 0])
        total_up += dot_tn(factor_ref[source, 1], block[rows:, :])
        total_up -= dot_tn(factor_ref[source, 2], text)
    total_down += dot_tn(out_ref[...], coef_ref[0])
    total_up -= dot_tn(coef_ref[layers + 1], out_ref[...])
    turned = jnp.zeros((share, RANK), F32)
    for l in range(layers):
        coef = coef_ref[l + 1]
        zero = jnp.zeros_like(coef)
        total_down += dot_tn(up_ref[l], jnp.where(l < sec, coef, zero))
        turned += dot_nn(down_ref[l], jnp.where(l > sec, coef, zero))
        total_up -= dot_tn(coef_ref[layers + 2 + l], up_ref[l])
    grad_down_ref[...] = total_down
    grad_up_ref[...] = total_up + turned.T


def last_products(sec, grp, core, blocks, factors, coef, down, up, out):
    layers = down.shape[0]
    share = out.shape[1]
    groups = len(blocks)
    return pl.pallas_call(
        functools.partial(last_kernel, layers, groups),
        in_specs=[SMEM] + [VMEM] * (groups + 5),
        out_specs=[VMEM] * 2,
        out_shape=[
            jax.ShapeDtypeStruct((share, RANK), F32),
            jax.ShapeDtypeStruct((RANK, share), F32),
        ],
        compiler_params=PARAMS,
    )(scalars(sec, grp, core), *blocks, factors, coef, down, up, out)


def spread(value, axis):
    count = lax.axis_size(axis)
    return lax.all_to_all(jnp.broadcast_to(value[None], (count,) + value.shape), axis, 0, 0)


def shards(text, cotangent, dec_down, dec_up, images, enc_down, enc_up, proj_in, proj_out, frame):
    sections = lax.axis_size("section")
    groups = lax.axis_size("dp")
    sec = lax.axis_index("section")
    grp = lax.axis_index("dp")
    core = sec % 2
    both = ("section", "dp")
    slot_count, patch_count, enc_width = images.shape[2:]
    tokens = patch_count // 4
    rows_total, width = text.shape[1:]
    rank = dec_down.shape[2]
    weight_down = dec_down[0]
    weight_up = dec_up[0]
    frames = frame[0]
    text = text[0]
    cot = cotangent[0]
    piece = rank // groups
    share = width // groups
    half = groups // 2
    swap = [(at, at ^ 1) for at in range(sections)]

    up_rows = spread(lax.dynamic_slice_in_dim(weight_up, grp * piece, piece, 0), "section")

    slot_row = jnp.repeat(frames, tokens)[None, :]
    row = jnp.arange(rows_total, dtype=jnp.int32)[:, None]
    column = jnp.arange(rows_total, dtype=jnp.int32)[None, :]
    sel = (slot_row == row // tokens) & (row % tokens == column % tokens)
    keep = 1.0 - jnp.any(sel, axis=1, keepdims=True).astype(F32)
    sel = sel.astype(BF)
    cols, proj, cot_image, text_norm, image_gram = text_products(
        grp + half * core, keep, text, cot, weight_down, weight_up, proj_out, groups
    )

    patches = images[0, 0].reshape(slot_count * patch_count, enc_width)
    quarters = proj_in.reshape(4, enc_width, rank)
    proj_pre, enc_cols, cross = encoder_front(
        sec, patches, enc_down, enc_up, quarters, sections
    )
    gath = lax.all_gather(jnp.concatenate([proj, proj_pre], axis=0), "section", axis=0)

    image_rows = lax.dynamic_slice_in_dim(proj_out, grp * piece, piece, 0)
    up_rows, cols, enc_cols = lax.optimization_barrier((up_rows, cols, enc_cols))
    rows = jnp.concatenate([image_rows[None], up_rows], axis=0).reshape(-1, width)
    gram = jnp.stack(
        [
            dot_nn(rows, weight_down).reshape(sections + 1, piece, rank),
            dot_nt(rows, weight_up).reshape(sections + 1, piece, rank),
        ],
        axis=1,
    ).astype(BF).reshape(-1, rank)
    gram, cols = lax.optimization_barrier((gram, cols))
    packed = pack_gram(core, spread(gram, "section"), groups)

    blocks = []
    for step in range(half):
        pairs = []
        for at in range(sections):
            for source in range(groups):
                to = (source + half * (at % 2) + step) % groups
                pairs.append((at * groups + source, at * groups + to))
        blocks.append(lax.ppermute(cols[step], both, pairs))

    packed, enc_cols = lax.optimization_barrier((packed, enc_cols))
    own_gram = lax.all_to_all(packed, "dp", 0, 0)
    other_gram = lax.ppermute(own_gram, "section", swap)

    window_parts = [enc_cols[0]]
    for step in range(1, sections):
        pairs = [(at, (at + step) % sections) for at in range(sections)]
        window_parts.append(lax.ppermute(enc_cols[step], "section", pairs))

    blocks = blocks + [lax.ppermute(block, "section", swap) for block in blocks]

    own_down = lax.dynamic_slice_in_dim(weight_down, grp * share, share, 0)
    own_up = lax.dynamic_slice_in_dim(weight_up, grp * share, share, 1)
    own_down, own_up, gath = lax.optimization_barrier((own_down, own_up, gath))
    down_slices = lax.all_gather(own_down, "section", axis=0)
    up_slices = lax.all_gather(own_up, "section", axis=0)
    out_slice = lax.dynamic_slice_in_dim(proj_out, grp * share, share, 1)
    stride, tiles = window(enc_width, sections)
    wide = width // sections
    few_cols = width // (sections * groups)
    early = (
        out_slice,
        lax.dynamic_slice_in_dim(enc_up, sec * stride, tiles * rank, 1),
        lax.dynamic_slice_in_dim(quarters, sec * stride, tiles * rank, 1),
        lax.dynamic_slice_in_dim(cot, sec * wide, wide, 1),
        lax.dynamic_slice_in_dim(proj_out, sec * wide, wide, 1),
        lax.dynamic_slice_in_dim(
            weight_down.reshape(sections, -1, rank), grp * few_cols, few_cols, 1
        ).reshape(-1, rank),
        lax.dynamic_slice_in_dim(
            weight_up.reshape(rank, sections, -1), grp * few_cols, few_cols, 2
        ).reshape(rank, -1),
    )
    early, gath = lax.optimization_barrier((early, gath))
    out_slice, up_window, in_window, cot_block, out_block, down_pick, up_pick = early

    coef, factor, image = rank_space(
        sec, core, own_gram, other_gram, gath, cot_image, text_norm, image_gram, sel, width
    )
    coef = lax.all_to_all(coef.reshape(groups, -1, rank), "dp", 0, 0)
    factors = lax.all_gather(factor, "dp", axis=0)

    parts, (n_enc, n_in, pad_enc, pad_in) = encoder_late(
        sec, grp, window_parts, image, cross, up_window, in_window, cot_block, out_block,
        enc_width, groups,
    )
    coef = jnp.sum(coef.astype(F32), axis=0).astype(BF)
    first = 6
    early_parts = [parts[step] for step in range(first)]
    late_parts, coef = lax.optimization_barrier((parts, coef))
    coef = spread(coef, "dp").reshape(-1, rank, rank)
    pieces = early_parts + [late_parts[step] for step in range(first, groups)]
    for step in range(1, groups):
        pairs = [(at, (at + step) % groups) for at in range(groups)]
        pieces[step] = lax.ppermute(pieces[step], "dp", pairs)
    parts = sum_parts(pieces)
    grad_enc_down = parts[:n_enc]
    grad_enc_up = parts[pad_enc:pad_enc + n_enc].T
    grad_proj_in = parts[2 * pad_enc:2 * pad_enc + n_in]
    own_out = parts[2 * pad_enc + pad_in:]

    term = dot_nt(down_pick, coef[0]) - dot(up_pick, coef[sections + 1], (0, 1))
    term = lax.all_to_all(term.astype(BF).reshape(sections, few_cols, rank), "section", 0, 0)

    grad_dec_down, grad_dec_up = last_products(
        sec, grp, core, blocks, factors, coef, down_slices, up_slices, out_slice
    )
    grad_proj_out = (own_out + jnp.sum(term.astype(F32), axis=0)).T
    return (
        grad_dec_down[None],
        grad_dec_up[None],
        grad_enc_down,
        grad_enc_up,
        grad_proj_in,
        grad_proj_out,
    )


def solution(mesh):
    placed = (
        P("dp", None, None),
        P("dp", None, None),
        P("section", None, None),
        P("section", None, None),
        P("dp", "section", None, None, None),
        P(),
        P(),
        P(),
        P(),
        P("dp", None),
    )
    return jax.shard_map(
        shards,
        mesh=mesh,
        in_specs=placed,
        out_specs=(
            P("section", "dp", None),
            P("section", None, "dp"),
            P(("section", "dp"), None),
            P(None, ("section", "dp")),
            P(("section", "dp"), None),
            P(None, ("section", "dp")),
        ),
        check_vma=False,
    )
```

time: 307 us -> 270 us (0.88)
  local copies, waits for them, and re-layouts: 96.9 us -> 30.4 us
  starting transfers between devices: 43 us -> 105 us
  matrix products: 46.7 us -> 6.26 us
  Pallas kernels: 5.29 us -> 35.7 us
  other arithmetic: 27.1 us -> 2.29 us
  blocking collectives: 24.5 us -> 28 us
    ppermute x7 -> x39, starting transfers between devices: 6.79 us -> 76 us  [the longest x7 30.7 us: shards(): window_parts.append(lax.ppermute(enc_cols[step], 'section', pairs))]
    unnamed x75 -> x43, local copies, waits for them, and re-layouts: 46.1 us -> 8.45 us
    dot_general x25 -> x4, matrix products: 42.1 us -> 6.26 us  [dot(): lax.dot_general(left, right, ((dims[:1], dims[1:]), ((), ())), preferred_...]
    pallas_call x1 -> x7, Pallas kernels: 5.29 us -> 35.7 us  [the longest x1 12.9 us: text_products(): pl.pallas_call(functools.partial(text_kernel, groups, kept), grid_spec=pl...]
    all_gather x3 -> x2, waiting for transfers between devices: 19.9 us -> 0.04 us  [the longest x1 0.02 us: shards(): down_slices = lax.all_gather(own_down, 'section', axis=0)]
    ppermute x7 -> x39, waiting for transfers between devices: 0.02 us -> 19.4 us  [the longest x8 11.3 us: shards(): blocks.append(lax.ppermute(cols[step], both, pairs))]
    all_to_all x0 -> x1, blocking collectives: none -> 13.7 us  [spread(): lax.all_to_all(jnp.broadcast_to(value[None], (count,) + value.shape), axi...]
    all_to_all x4 -> x0, local copies, waits for them, and re-layouts: 12.8 us -> none  [the longest x2 5 us: shards(): patch_cols = lax.all_to_all(patches, 'section', 1, 0, tiled=True)]
  transfers between devices with their start and end apart: 18 -> 47, of which waited for: 5 -> 6; matrix products, arithmetic and copies ran while one was open for 48% -> 12% of each run, Pallas kernels for 2% -> 11%
where the time goes in v2:
time: 270 us; the launch traced here: 268 us
  starting transfers between devices  105 us (39%)
  waiting for transfers between devices  46.2 us (17%)
  Pallas kernels  35.7 us (13%)
  local copies, waits for them, and re-layouts  30.4 us (11%)
  blocking collectives  28 us (10%)
  between operations  14.3 us (5%)
  matrix products  6.26 us (2%)
    ppermute x7, starting transfers between devices, shards(): window_parts.append(lax.ppermute(enc_cols[step], 'section', pairs))  30.7 us
    ppermute x15, starting transfers between devices, shards(): pieces[step] = lax.ppermute(pieces[step], 'dp', pairs)  25.8 us
    all_to_all x1, waiting for transfers between devices, shards(): own_gram = lax.all_to_all(packed, 'dp', 0, 0)  22 us
    ppermute x8, starting transfers between devices, shards(): blocks.append(lax.ppermute(cols[step], both, pairs))  17.1 us
    all_gather x1, blocking collectives, shards(): lax.all_gather(jnp.concatenate([proj, proj_pre], axis=0), 'section', axis=0)  14.2 us
    all_to_all x1, blocking collectives, spread(): lax.all_to_all(jnp.broadcast_to(value[None], (count,) + value.shape), axi...  13.7 us
    pallas_call x1, Pallas kernels, text_products(): pl.pallas_call(functools.partial(text_kernel, groups, kept), grid_spec=pl...  12.9 us
    ppermute x8, waiting for transfers between devices, shards(): blocks.append(lax.ppermute(cols[step], both, pairs))  11.3 us
  transfers between devices with their start and end apart: 47, of which 6 were waited for; matrix products, arithmetic and copies ran while one was open for 12% of the time, Pallas kernels for 11%

profile of v2, /device:TPU:0, one launch (start us, length us, event | category | flops | bytes accessed | tf_op | source)
XLA Modules:
  0.0 268.3 jit_solution(7962817944439880583)
XLA Ops:
  9.3 4.4 %all-to-all-start = ((bf16[8,8,8192]{2,1,0:T(8,128)(2,1)}), bf16[8,8,8192]{2,1,0:T(8,128)(2,1)}, u32[]{:S(2)}, u32[]{:S(2)}) async-start(bf16[8,8,8192]{2,1,0:T(8,128)(2,1)} %broadcast_in_dim.18), calls=%async_computation | async-start | bytes 2097152 | tf_op jit(solution)/shard_map/all_to_all | solution.py:561
  14.3 4.5 %shard_map.146 = (bf16[16,128]{1,0:T(8,128)(2,1)S(1)}, bf16[8,672,128]{2,1,0:T(8,128)(2,1)S(1)}, bf16[128,512]{1,0:T(8,128)(2,1)S(1)}) custom-call(s32[1]{0:T(128)} %bitcast.place_ref, bf16[64,3200]{1,0:T(8,128)(2,1)S(1)} %bitcast.139, bf16[3200,128]{1,0:T(8,128)(2,1)S(1)} %copy-done.8, bf16[128,3200]{1,0:T(8,128)(2,1)S(1)} %copy-done.4, ...), custom_call_target="tpu_custom_call" | custom-call | tf_op jit(solution)/shard_map/pallas_call | solution.py:227
  20.0 12.9 %shard_map.145 = (bf16[8,256,512]{2,1,0:T(8,128)(2,1)S(1)}, bf16[384,128]{1,0:T(8,128)(2,1)S(1)}, f32[128,128]{1,0:T(8,128)S(1)}, f32[128,1]{1,0:T(8,128)S(1)}, bf16[128,128]{1,0:T(8,128)(2,1)S(1)}) custom-call(s32[1]{0:T(128)} %bitcast.5.start_ref, f32[128,1]{1,0:T(8,128)S(1)} %copy.20.keep_ref, bf16[128,8192]{1,0:T(8,128)(2,1)S(1)} %bitcast.137, ...), custom_call_target="tpu_custom_call" | custom-call | tf_op jit(solution)/shard_map/pallas_call | solution.py:102
  34.3 14.2 %all-gather = bf16[3200,128]{1,0:T(8,128)(2,1)S(1)} all-gather(bf16[400,128]{1,0:T(8,128)(2,1)S(1)} %pad_maximum_fusion.3), channel_id=2, replica_groups=mesh['section'=8,'dp'=16] {'section'}, dimensions={0}, use_global_device_ids=true | all-gather | bytes 921600 | tf_op jit(solution)/shard_map/all_gather | solution.py:602
  57.9 13.7 %all_to_all.30.gram_ref = bf16[8,144,128]{2,1,0:T(8,128)(2,1)S(1)} all-to-all(bf16[8,144,128]{2,1,0:T(8,128)(2,1)S(1)} %broadcast_in_dim.39), channel_id=1, replica_groups=mesh['section'=8,'dp'=16] {'section'}, dimensions={0} | all-to-all | bytes 589824 | tf_op jit(solution)/shard_map/all_to_all | solution.py:561
  73.0 8.3 %all-to-all-start.2 = ((bf16[16,352,128]{2,1,0:T(8,128)(2,1)}), bf16[16,352,128]{2,1,0:T(8,128)(2,1)S(1)}, u32[]{:S(2)}, u32[]{:S(2)}) async-start(bf16[16,352,128]{2,1,0:T(8,128)(2,1)} %shard_map.147), calls=%async_computation.2 | async-start | bytes 2883584 | tf_op jit(solution)/shard_map/all_to_all | solution.py:627
  82.1 22.0 %all-to-all-done.2.own_ref = bf16[16,352,128]{2,1,0:T(8,128)(2,1)S(1)} async-done(((bf16[16,352,128]{2,1,0:T(8,128)(2,1)}), bf16[16,352,128]{2,1,0:T(8,128)(2,1)S(1)}, u32[]{:S(2)}, u32[]{:S(2)}) %all-to-all-start.2) | async-done | bytes 1441824 | tf_op jit(solution)/shard_map/all_to_all | solution.py:627
  104.1 4.1 %copy.22 = bf16[1,128,8192]{1,2,0:T(8,128)(2,1)} copy(bf16[1,128,8192]{2,1,0:T(8,128)(2,1)} %param.13) | data formatting | bytes 4194304 | tf_op args[3]
  117.6 6.8 %shard_map.148 = (bf16[18,128,128]{2,1,0:T(8,128)(2,1)}, bf16[3,128,128]{2,1,0:T(8,128)(2,1)}, bf16[4,128,128]{2,1,0:T(8,128)(2,1)S(1)}) custom-call(s32[2]{0:T(128)S(1)} %pad_add_fusion.1.place_ref, bf16[16,352,128]{2,1,0:T(8,128)(2,1)S(1)} %all-to-all-done.2.own_ref, bf16[16,352,128]{2,1,0:T(8,128)(2,1)} %collective-permute-done.16.other_ref, ...), custom_call_target="tpu_custom_call" | custom-call | tf_op jit(solution)/shard_map/pallas_call | solution.py:367
  128.4 4.3 %all-to-all-start.3 = ((bf16[16,144,128]{2,1,0:T(8,128)(2,1)}), bf16[16,144,128]{2,1,0:T(8,128)(2,1)}, u32[]{:S(2)}, u32[]{:S(2)}) async-start(bf16[16,144,128]{2,1,0:T(8,128)(2,1)} %bitcast.46), calls=%async_computation.3 | async-start | bytes 1179648 | tf_op jit(solution)/shard_map/all_to_all | solution.py:665
  136.5 8.2 %collective-permute-start.21 = (bf16[672,128]{1,0:T(8,128)(2,1)}, bf16[672,128]{1,0:T(8,128)(2,1)S(1)}, u32[]{:S(2)}, u32[]{:S(2)}) collective-permute-start(bf16[672,128]{1,0:T(8,128)(2,1)} %get-tuple-element.82), channel_id=1, source_target_pairs={{0,80},{16,96},{32,112},{48,0},{64,16},{80,32},{96,48},{112,64},{1... | collective-permute-start | bytes 516104 | tf_op jit(solution)/shard_map/ppermute | solution.py:633
  144.7 8.9 %collective-permute-start.22 = (bf16[672,128]{1,0:T(8,128)(2,1)}, bf16[672,128]{1,0:T(8,128)(2,1)S(1)}, u32[]{:S(2)}, u32[]{:S(2)}) collective-permute-start(bf16[672,128]{1,0:T(8,128)(2,1)} %get-tuple-element.81), channel_id=1, source_target_pairs={{0,96},{16,112},{32,0},{48,16},{64,32},{80,48},{96,64},{112,80},{1... | collective-permute-start | bytes 516104 | tf_op jit(solution)/shard_map/ppermute | solution.py:633
  153.6 9.0 %collective-permute-start.23 = (bf16[672,128]{1,0:T(8,128)(2,1)}, bf16[672,128]{1,0:T(8,128)(2,1)S(1)}, u32[]{:S(2)}, u32[]{:S(2)}) collective-permute-start(bf16[672,128]{1,0:T(8,128)(2,1)} %get-tuple-element.80), channel_id=1, source_target_pairs={{0,112},{16,0},{32,16},{48,32},{64,48},{80,64},{96,80},{112,96},{1... | collective-permute-start | bytes 516104 | tf_op jit(solution)/shard_map/ppermute | solution.py:633
  166.6 4.3 %shard_map.149 = bf16[16,240,128]{2,1,0:T(8,128)(2,1)S(1)} custom-call(s32[4]{0:T(128)S(1)} %pad_add_fusion.2.shift_ref, bf16[672,128]{1,0:T(8,128)(2,1)S(1)} %get-tuple-element.87.refs_0_, bf16[672,128]{1,0:T(8,128)(2,1)S(1)} %collective-permute-done.17.refs_1_, bf16[672,128]{1,0:T(8,128)(2,1)S(1)} %collective-permute-done.18.refs_2_, ...), custom_call_target="tpu_custom_call" | custom-call | tf_op jit(solution)/shard_map/pallas_call | solution.py:479
  173.1 6.4 %all-to-all-start.4 = ((bf16[16,144,128]{2,1,0:T(8,128)(2,1)}), bf16[16,144,128]{2,1,0:T(8,128)(2,1)S(1)}, u32[]{:S(2)}, u32[]{:S(2)}) async-start(bf16[16,144,128]{2,1,0:T(8,128)(2,1)} %broadcast_in_dim.40), calls=%async_computation.4 | async-start | bytes 1179648 | tf_op jit(solution)/shard_map/all_to_all | solution.py:561
  189.3 5.7 %collective-permute-done.24.refs_1_ = bf16[240,128]{1,0:T(8,128)(2,1)S(1)} collective-permute-done((bf16[240,128]{1,0:T(8,128)(2,1)S(1)}, bf16[240,128]{1,0:T(8,128)(2,1)S(1)}, u32[]{:S(2)}, u32[]{:S(2)}) %collective-permute-start.24) | collective-permute-done | bytes 61472 | tf_op jit(solution)/shard_map/ppermute | solution.py:680
  198.7 3.3 %collective-permute-start.32 = (bf16[240,128]{1,0:T(8,128)(2,1)S(1)}, bf16[240,128]{1,0:T(8,128)(2,1)S(1)}, u32[]{:S(2)}, u32[]{:S(2)}) collective-permute-start(bf16[240,128]{1,0:T(8,128)(2,1)S(1)} %get-tuple-element.94), channel_id=1, source_target_pairs={{0,9},{1,10},{2,11},{3,12},{4,13},{5,14},{6,15},{7,0},{8,1},{9,2},... | collective-permute-start | bytes 184328 | tf_op jit(solution)/shard_map/ppermute | solution.py:680
  202.0 4.2 %collective-permute-start.33 = (bf16[240,128]{1,0:T(8,128)(2,1)S(1)}, bf16[240,128]{1,0:T(8,128)(2,1)S(1)}, u32[]{:S(2)}, u32[]{:S(2)}) collective-permute-start(bf16[240,128]{1,0:T(8,128)(2,1)S(1)} %get-tuple-element.93), channel_id=1, source_target_pairs={{0,10},{1,11},{2,12},{3,13},{4,14},{5,15},{6,0},{7,1},{8,2},{9,3},... | collective-permute-start | bytes 184328 | tf_op jit(solution)/shard_map/ppermute | solution.py:680
  223.3 3.4 %collective-permute-done.3.refs_3_ = bf16[256,512]{1,0:T(8,128)(2,1)S(1)} collective-permute-done((bf16[256,512]{1,0:T(8,128)(2,1)}, bf16[256,512]{1,0:T(8,128)(2,1)S(1)}, u32[]{:S(2)}, u32[]{:S(2)}) %collective-permute-start.3) | collective-permute-done | bytes 262176 | tf_op jit(solution)/shard_map/ppermute | solution.py:624
  228.3 7.9 %collective-permute-done.4.refs_4_ = bf16[256,512]{1,0:T(8,128)(2,1)S(1)} collective-permute-done((bf16[256,512]{1,0:T(8,128)(2,1)S(1)}, bf16[256,512]{1,0:T(8,128)(2,1)S(1)}, u32[]{:S(2)}, u32[]{:S(2)}) %collective-permute-start.4) | collective-permute-done | bytes 262176 | tf_op jit(solution)/shard_map/ppermute | solution.py:624
  236.2 4.3 %collective-permute-start.1 = (bf16[256,512]{1,0:T(8,128)(2,1)}, bf16[256,512]{1,0:T(8,128)(2,1)S(1)}, u32[]{:S(2)}, u32[]{:S(2)}) collective-permute-start(bf16[256,512]{1,0:T(8,128)(2,1)} %get-tuple-element.78), channel_id=1, source_target_pairs={{0,1},{1,2},{2,3},{3,4},{4,5},{5,6},{6,7},{7,8},{8,9},{9,10},{10,1... | collective-permute-start | bytes 786440 | tf_op jit(solution)/shard_map/ppermute | solution.py:624
  242.2 5.6 %all-to-all-start.5 = ((bf16[8,64,128]{2,1,0:T(8,128)(2,1)}), bf16[8,64,128]{2,1,0:T(8,128)(2,1)S(1)}, u32[]{:S(2)}, u32[]{:S(2)}) async-start(bf16[8,64,128]{2,1,0:T(8,128)(2,1)} %bitcast.71), calls=%async_computation.5 | async-start | bytes 262144 | tf_op jit(solution)/shard_map/all_to_all | solution.py:688
  250.0 4.0 %all-to-all-done.5 = bf16[8,64,128]{2,1,0:T(8,128)(2,1)S(1)} async-done(((bf16[8,64,128]{2,1,0:T(8,128)(2,1)}), bf16[8,64,128]{2,1,0:T(8,128)(2,1)S(1)}, u32[]{:S(2)}, u32[]{:S(2)}) %all-to-all-start.5) | async-done | bytes 131104 | tf_op jit(solution)/shard_map/all_to_all | solution.py:688
  256.0 5.8 %shard_map.150 = (f32[512,128]{1,0:T(8,128)}, f32[128,512]{1,0:T(8,128)}) custom-call(s32[3]{0:T(128)S(1)} %pad_add_fusion.place_ref, bf16[256,512]{1,0:T(8,128)(2,1)S(1)} %collective-permute-done.refs_0_, bf16[256,512]{1,0:T(8,128)(2,1)S(1)} %collective-permute-done.1.refs_1_, bf16[256,512]{1,0:T(8,128)(2,1)S(1)} %collective-permute-done.2.refs_2_, ...), custom_call_target="tpu_custom_call" | custom-call | tf_op jit(solution)/shard_map/pallas_call | solution.py:547
  (163 shorter events, 77.8 us)
Async XLA Ops:
  9.3 43.2 %all-to-all-start = ((bf16[8,8,8192]{2,1,0:T(8,128)(2,1)}), bf16[8,8,8192]{2,1,0:T(8,128)(2,1)}, u32[]{:S(2)}, u32[]{:S(2)}) async-start(bf16[8,8,8192]{2,1,0:T(8,128)(2,1)} %broadcast_in_dim.18), calls=%async_computation | async-start | bytes 2097152 | tf_op jit(solution)/shard_map/all_to_all | solution.py:561
  13.7 241.0 %all-gather.10.cloned.1.call-start = ((), (), s32[]{:S(2)}) async-start(), calls=%async_computation.7 | async-start | bytes 1179648 | tf_op jit(solution)/shard_map/all_gather | solution.py:640
  73.0 31.2 %all-to-all-start.2 = ((bf16[16,352,128]{2,1,0:T(8,128)(2,1)}), bf16[16,352,128]{2,1,0:T(8,128)(2,1)S(1)}, u32[]{:S(2)}, u32[]{:S(2)}) async-start(bf16[16,352,128]{2,1,0:T(8,128)(2,1)} %shard_map.147), calls=%async_computation.2 | async-start | bytes 2883584 | tf_op jit(solution)/shard_map/all_to_all | solution.py:627
  81.3 173.4 %all-gather.12.cloned.1.call-start = ((), (), s32[]{:S(2)}) async-start(), calls=%async_computation.8 | async-start | bytes 1179648 | tf_op jit(solution)/shard_map/all_gather | solution.py:641
  82.1 172.7 %all-gather.8.cloned.1.call-start = ((), (), s32[]{:S(2)}) async-start(), calls=%async_computation.6 | async-start | bytes 1671168 | tf_op jit(solution)/shard_map/all_gather | solution.py:666
  104.1 13.4 %collective-permute-start.16 = (bf16[16,352,128]{2,1,0:T(8,128)(2,1)S(1)}, bf16[16,352,128]{2,1,0:T(8,128)(2,1)}, u32[]{:S(2)}, u32[]{:S(2)}) collective-permute-start(bf16[16,352,128]{2,1,0:T(8,128)(2,1)S(1)} %all-to-all-done.2.own_ref), channel_id=1, source_target_pairs={{0,16},{16,0},{32,48},{48,32},{64,80},{80,64},{96,112},{112,96},{1... | collective-permute-start | bytes 4325384 | tf_op jit(solution)/shard_map/ppermute | solution.py:628
  127.6 17.1 %collective-permute-start.17 = (bf16[672,128]{1,0:T(8,128)(2,1)}, bf16[672,128]{1,0:T(8,128)(2,1)S(1)}, u32[]{:S(2)}, u32[]{:S(2)}) collective-permute-start(bf16[672,128]{1,0:T(8,128)(2,1)} %get-tuple-element.86), channel_id=1, source_target_pairs={{0,16},{16,32},{32,48},{48,64},{64,80},{80,96},{96,112},{112,0},{1... | collective-permute-start | bytes 516104 | tf_op jit(solution)/shard_map/ppermute | solution.py:633
  128.1 25.5 %collective-permute-start.18 = (bf16[672,128]{1,0:T(8,128)(2,1)}, bf16[672,128]{1,0:T(8,128)(2,1)S(1)}, u32[]{:S(2)}, u32[]{:S(2)}) collective-permute-start(bf16[672,128]{1,0:T(8,128)(2,1)} %get-tuple-element.85), channel_id=1, source_target_pairs={{0,32},{16,48},{32,64},{48,80},{64,96},{80,112},{96,0},{112,16},{1... | collective-permute-start | bytes 516104 | tf_op jit(solution)/shard_map/ppermute | solution.py:633
  128.4 42.6 %all-to-all-start.3 = ((bf16[16,144,128]{2,1,0:T(8,128)(2,1)}), bf16[16,144,128]{2,1,0:T(8,128)(2,1)}, u32[]{:S(2)}, u32[]{:S(2)}) async-start(bf16[16,144,128]{2,1,0:T(8,128)(2,1)} %bitcast.46), calls=%async_computation.3 | async-start | bytes 1179648 | tf_op jit(solution)/shard_map/all_to_all | solution.py:665
  132.6 31.4 %collective-permute-start.19 = (bf16[672,128]{1,0:T(8,128)(2,1)}, bf16[672,128]{1,0:T(8,128)(2,1)S(1)}, u32[]{:S(2)}, u32[]{:S(2)}) collective-permute-start(bf16[672,128]{1,0:T(8,128)(2,1)} %get-tuple-element.84), channel_id=1, source_target_pairs={{0,48},{16,64},{32,80},{48,96},{64,112},{80,0},{96,16},{112,32},{1... | collective-permute-start | bytes 516104 | tf_op jit(solution)/shard_map/ppermute | solution.py:633
  133.7 32.9 %collective-permute-start.20 = (bf16[672,128]{1,0:T(8,128)(2,1)}, bf16[672,128]{1,0:T(8,128)(2,1)S(1)}, u32[]{:S(2)}, u32[]{:S(2)}) collective-permute-start(bf16[672,128]{1,0:T(8,128)(2,1)} %get-tuple-element.83), channel_id=1, source_target_pairs={{0,64},{16,80},{32,96},{48,112},{64,0},{80,16},{96,32},{112,48},{1... | collective-permute-start | bytes 516104 | tf_op jit(solution)/shard_map/ppermute | solution.py:633
  136.5 30.0 %collective-permute-start.21 = (bf16[672,128]{1,0:T(8,128)(2,1)}, bf16[672,128]{1,0:T(8,128)(2,1)S(1)}, u32[]{:S(2)}, u32[]{:S(2)}) collective-permute-start(bf16[672,128]{1,0:T(8,128)(2,1)} %get-tuple-element.82), channel_id=1, source_target_pairs={{0,80},{16,96},{32,112},{48,0},{64,16},{80,32},{96,48},{112,64},{1... | collective-permute-start | bytes 516104 | tf_op jit(solution)/shard_map/ppermute | solution.py:633
  144.7 21.9 %collective-permute-start.22 = (bf16[672,128]{1,0:T(8,128)(2,1)}, bf16[672,128]{1,0:T(8,128)(2,1)S(1)}, u32[]{:S(2)}, u32[]{:S(2)}) collective-permute-start(bf16[672,128]{1,0:T(8,128)(2,1)} %get-tuple-element.81), channel_id=1, source_target_pairs={{0,96},{16,112},{32,0},{48,16},{64,32},{80,48},{96,64},{112,80},{1... | collective-permute-start | bytes 516104 | tf_op jit(solution)/shard_map/ppermute | solution.py:633
  164.1 24.0 %collective-permute-start.2 = (bf16[256,512]{1,0:T(8,128)(2,1)}, bf16[256,512]{1,0:T(8,128)(2,1)S(1)}, u32[]{:S(2)}, u32[]{:S(2)}) collective-permute-start(bf16[256,512]{1,0:T(8,128)(2,1)} %get-tuple-element.77), channel_id=1, source_target_pairs={{0,2},{1,3},{2,4},{3,5},{4,6},{5,7},{6,8},{7,9},{8,10},{9,11},{10,... | collective-permute-start | bytes 786440 | tf_op jit(solution)/shard_map/ppermute | solution.py:624
  173.1 50.1 %all-to-all-start.4 = ((bf16[16,144,128]{2,1,0:T(8,128)(2,1)}), bf16[16,144,128]{2,1,0:T(8,128)(2,1)S(1)}, u32[]{:S(2)}, u32[]{:S(2)}) async-start(bf16[16,144,128]{2,1,0:T(8,128)(2,1)} %broadcast_in_dim.40), calls=%async_computation.4 | async-start | bytes 1179648 | tf_op jit(solution)/shard_map/all_to_all | solution.py:561
  179.6 15.4 %collective-permute-start.24 = (bf16[240,128]{1,0:T(8,128)(2,1)S(1)}, bf16[240,128]{1,0:T(8,128)(2,1)S(1)}, u32[]{:S(2)}, u32[]{:S(2)}) collective-permute-start(bf16[240,128]{1,0:T(8,128)(2,1)S(1)} %get-tuple-element.102), channel_id=1, source_target_pairs={{0,1},{1,2},{2,3},{3,4},{4,5},{5,6},{6,7},{7,8},{8,9},{9,10},{10,1... | collective-permute-start | bytes 184328 | tf_op jit(solution)/shard_map/ppermute | solution.py:680
  181.5 15.8 %collective-permute-start.25 = (bf16[240,128]{1,0:T(8,128)(2,1)S(1)}, bf16[240,128]{1,0:T(8,128)(2,1)S(1)}, u32[]{:S(2)}, u32[]{:S(2)}) collective-permute-start(bf16[240,128]{1,0:T(8,128)(2,1)S(1)} %get-tuple-element.101), channel_id=1, source_target_pairs={{0,2},{1,3},{2,4},{3,5},{4,6},{5,7},{6,8},{7,9},{8,10},{9,11},{10,... | collective-permute-start | bytes 184328 | tf_op jit(solution)/shard_map/ppermute | solution.py:680
  188.0 14.0 %collective-permute-start.28 = (bf16[240,128]{1,0:T(8,128)(2,1)S(1)}, bf16[240,128]{1,0:T(8,128)(2,1)S(1)}, u32[]{:S(2)}, u32[]{:S(2)}) collective-permute-start(bf16[240,128]{1,0:T(8,128)(2,1)S(1)} %get-tuple-element.98), channel_id=1, source_target_pairs={{0,5},{1,6},{2,7},{3,8},{4,9},{5,10},{6,11},{7,12},{8,13},{9,14},{... | collective-permute-start | bytes 184328 | tf_op jit(solution)/shard_map/ppermute | solution.py:680
  213.5 13.2 %collective-permute-start.3 = (bf16[256,512]{1,0:T(8,128)(2,1)}, bf16[256,512]{1,0:T(8,128)(2,1)S(1)}, u32[]{:S(2)}, u32[]{:S(2)}) collective-permute-start(bf16[256,512]{1,0:T(8,128)(2,1)} %get-tuple-element.76), channel_id=1, source_target_pairs={{0,3},{1,4},{2,5},{3,6},{4,7},{5,8},{6,9},{7,10},{8,11},{9,12},{10... | collective-permute-start | bytes 786440 | tf_op jit(solution)/shard_map/ppermute | solution.py:624
  214.6 21.6 %collective-permute-start.4 = (bf16[256,512]{1,0:T(8,128)(2,1)S(1)}, bf16[256,512]{1,0:T(8,128)(2,1)S(1)}, u32[]{:S(2)}, u32[]{:S(2)}) collective-permute-start(bf16[256,512]{1,0:T(8,128)(2,1)S(1)} %copy-done.19), channel_id=1, source_target_pairs={{0,4},{1,5},{2,6},{3,7},{4,8},{5,9},{6,10},{7,11},{8,12},{9,13},{1... | collective-permute-start | bytes 786440 | tf_op jit(solution)/shard_map/ppermute | solution.py:624
  216.5 24.1 %collective-permute-start.5 = (bf16[256,512]{1,0:T(8,128)(2,1)S(1)}, bf16[256,512]{1,0:T(8,128)(2,1)S(1)}, u32[]{:S(2)}, u32[]{:S(2)}) collective-permute-start(bf16[256,512]{1,0:T(8,128)(2,1)S(1)} %copy-done.18), channel_id=1, source_target_pairs={{0,5},{1,6},{2,7},{3,8},{4,9},{5,10},{6,11},{7,12},{8,13},{9,14},{... | collective-permute-start | bytes 786440 | tf_op jit(solution)/shard_map/ppermute | solution.py:624
  216.9 23.7 %collective-permute-start.6 = (bf16[256,512]{1,0:T(8,128)(2,1)}, bf16[256,512]{1,0:T(8,128)(2,1)S(1)}, u32[]{:S(2)}, u32[]{:S(2)}) collective-permute-start(bf16[256,512]{1,0:T(8,128)(2,1)} %get-tuple-element.73), channel_id=1, source_target_pairs={{0,6},{1,7},{2,8},{3,9},{4,10},{5,11},{6,12},{7,13},{8,14},{9,15},... | collective-permute-start | bytes 786440 | tf_op jit(solution)/shard_map/ppermute | solution.py:624
  220.1 20.9 %collective-permute-start.7 = (bf16[256,512]{1,0:T(8,128)(2,1)}, bf16[256,512]{1,0:T(8,128)(2,1)S(1)}, u32[]{:S(2)}, u32[]{:S(2)}) collective-permute-start(bf16[256,512]{1,0:T(8,128)(2,1)} %get-tuple-element.72), channel_id=1, source_target_pairs={{0,7},{1,8},{2,9},{3,10},{4,11},{5,12},{6,13},{7,14},{8,15},{9,0},... | collective-permute-start | bytes 786440 | tf_op jit(solution)/shard_map/ppermute | solution.py:624
  226.7 21.7 %collective-permute-start = (bf16[256,512]{1,0:T(8,128)(2,1)}, bf16[256,512]{1,0:T(8,128)(2,1)S(1)}, u32[]{:S(2)}, u32[]{:S(2)}) collective-permute-start(bf16[256,512]{1,0:T(8,128)(2,1)} %get-tuple-element.79), channel_id=1, source_target_pairs={{0,0},{1,1},{2,2},{3,3},{4,4},{5,5},{6,6},{7,7},{8,8},{9,9},{10,10... | collective-permute-start | bytes 786440 | tf_op jit(solution)/shard_map/ppermute | solution.py:624
  (44 other events, 637.5 us)
Sparse Core Ops, SparseCore 0:
  51.8 25.9 all-gather.9
  83.9 23.4 all-gather.11
  125.1 43.1 all-gather.7

commit v3 on v2

v3 whole, which is shorter than its diff:
```python
import functools

import jax
import jax.numpy as jnp
from jax import lax
from jax.experimental import pallas as pl
from jax.experimental.pallas import tpu as pltpu
from jax.sharding import PartitionSpec as P

EPS = 1e-06
GELU_C = 0.7978845608028654
BF = jnp.bfloat16
F32 = jnp.float32


def gelu_tanh(value):
    return 0.5 * value * (1.0 + jnp.tanh(GELU_C * (value + 0.044715 * value * value * value)))


def gelu_slope(value):
    inner = jnp.tanh(GELU_C * (value + 0.044715 * value * value * value))
    return 0.5 * (1.0 + inner) + 0.5 * value * (1.0 - inner * inner) * GELU_C * (
        1.0 + 3.0 * 0.044715 * value * value
    )


def norm_scale(rows32):
    return lax.rsqrt(jnp.mean(rows32 * rows32, axis=-1, keepdims=True) + EPS)


def dot(left, right, dims):
    return lax.dot_general(left, right, ((dims[:1], dims[1:]), ((), ())), preferred_element_type=F32)


def dot_nn(left, right):
    return dot(left, right, (1, 0))


def dot_tn(left, right):
    return dot(left, right, (0, 0))


def dot_nt(left, right):
    return dot(left, right, (1, 1))


RANK = 128
VMEM = pl.BlockSpec(memory_space=pltpu.VMEM)
SMEM = pl.BlockSpec(memory_space=pltpu.SMEM)
PARAMS = pltpu.CompilerParams(vmem_limit_bytes=48 * 1024 * 1024)


def scalars(*values):
    return jnp.stack(values).astype(jnp.int32)


def text_kernel(
    half, share, few, steps,
    place_ref, keep_ref, text_ref, cot_ref, down_ref, up_ref, out_ref,
    text_cols_ref, cot_cols_ref, proj_ref, image_ref, norm_ref, gram_ref,
    pick_ref, block_ref, slice_ref, out_slice_ref,
    proj, image, gram,
):
    step = pl.program_id(0)
    core, sec, grp = place_ref[0], place_ref[1], place_ref[2]

    @pl.when(step == 0)
    def _():
        proj[...] = jnp.zeros_like(proj)
        image[...] = jnp.zeros_like(image)
        gram[...] = jnp.zeros_like(gram)
        norm_ref[...] = jnp.zeros_like(norm_ref)

    text32 = text_ref[...].astype(F32) * keep_ref[...]
    text = text32.astype(BF)
    cot = cot_ref[...]
    norm_ref[...] += jnp.sum(text32 * text32, axis=1, keepdims=True)
    proj[:RANK] += dot_nn(text, down_ref[...])
    proj[RANK:2 * RANK] += dot_nt(text, up_ref[...])
    proj[2 * RANK:] += dot_nt(cot, up_ref[...])
    image[...] += dot_nt(cot, out_ref[...])
    gram[...] += dot_nt(out_ref[...], out_ref[...])

    own = pl.ds(pl.multiple_of(core * half, half), half)
    keep = keep_ref[own, :]
    pieces = text_cols_ref.shape[0]
    for piece in range(pieces):
        span = slice(piece * share, (piece + 1) * share)
        text_cols_ref[piece] = (text_ref[own, span].astype(F32) * keep).astype(BF)
        cot_cols_ref[piece] = cot_ref[own, span]

    pick_ref[0, 0] = down_ref[pl.ds(pl.multiple_of(grp * few, few), few), :]
    per = RANK // few
    lanes = up_ref[:, pl.ds(pl.multiple_of(grp // per * RANK, RANK), RANK)].astype(F32).T
    picked = lanes[:few]
    for at in range(1, per):
        picked = jnp.where(lax.rem(grp, per) == at, lanes[at * few:(at + 1) * few], picked)
    pick_ref[0, 1] = picked.astype(BF)

    @pl.when(step == sec)
    def _():
        block_ref[0] = cot
        block_ref[1] = out_ref[...]

    @pl.when(step == grp // pieces)
    def _():
        at = pl.multiple_of(lax.rem(grp, pieces) * share, share)
        slice_ref[:share, :] = down_ref[pl.ds(at, share), :]
        up = up_ref[:, pl.ds(at, share)]
        for m in range(share // RANK):
            slice_ref[share + m * RANK:share + (m + 1) * RANK, :] = up[:, m * RANK:(m + 1) * RANK]
        out_slice_ref[...] = out_ref[:, pl.ds(at, share)]

    @pl.when(step == steps - 1)
    def _():
        proj_ref[...] = proj[...].astype(BF)
        image_ref[...] = image[...]
        gram_ref[...] = gram[...].astype(BF)


def text_products(sec, grp, keep, text, cot, down, up, out, sections, groups):
    rows, width = text.shape
    share = width // groups
    steps = sections
    wide = width // steps
    pieces = wide // share
    few = wide // groups
    half = rows // 2
    across = pl.BlockSpec((rows, wide), lambda i: (0, i))
    fixed = pl.BlockSpec((rows, RANK), lambda i: (0, 0))
    column = pl.BlockSpec((rows, 1), lambda i: (0, 0))
    cols = pl.BlockSpec((pieces, half, share), lambda i: (i, 0, 0))
    return pl.pallas_call(
        functools.partial(text_kernel, half, share, few, steps),
        grid=(steps,),
        in_specs=[
            SMEM,
            column,
            across,
            across,
            pl.BlockSpec((wide, RANK), lambda i: (i, 0)),
            across,
            across,
        ],
        out_specs=[
            cols,
            cols,
            pl.BlockSpec((3 * RANK, RANK), lambda i: (0, 0)),
            fixed,
            column,
            fixed,
            pl.BlockSpec((1, 2, few, RANK), lambda i: (i, 0, 0, 0)),
            pl.BlockSpec((2, rows, wide), lambda i: (0, 0, 0)),
            pl.BlockSpec((2 * share, RANK), lambda i: (0, 0)),
            pl.BlockSpec((rows, share), lambda i: (0, 0)),
        ],
        out_shape=[
            jax.ShapeDtypeStruct((groups, half, share), BF),
            jax.ShapeDtypeStruct((groups, half, share), BF),
            jax.ShapeDtypeStruct((3 * RANK, RANK), BF),
            jax.ShapeDtypeStruct((rows, RANK), F32),
            jax.ShapeDtypeStruct((rows, 1), F32),
            jax.ShapeDtypeStruct((RANK, RANK), BF),
            jax.ShapeDtypeStruct((steps, 2, few, RANK), BF),
            jax.ShapeDtypeStruct((2, rows, wide), BF),
            jax.ShapeDtypeStruct((2 * share, RANK), BF),
            jax.ShapeDtypeStruct((rows, share), BF),
        ],
        scratch_shapes=[
            pltpu.VMEM((3 * RANK, RANK), F32),
            pltpu.VMEM((rows, RANK), F32),
            pltpu.VMEM((RANK, RANK), F32),
        ],
        compiler_params=PARAMS,
    )(scalars(sec % 2, sec, grp), keep, text, cot, down, up, out)


def window(width, count):
    block = width // count
    stride = block // RANK * RANK
    tiles = -(-((count - 1) * (block - stride) + block) // RANK)
    return stride, tiles


def front_kernel(
    sections, windows, in_windows,
    place_ref, image_ref, down_ref, up_ref, in_ref,
    state_ref, wide_ref, in_window_ref,
    normed_buf, out_buf,
):
    sec = place_ref[0]
    width = down_ref.shape[0]
    span = windows[1] * RANK
    own = pl.ds(pl.multiple_of(sec * windows[0], RANK), span)
    total = jnp.zeros((RANK, 1), F32)
    for k in range(4):
        patch = jnp.concatenate([image_ref[l, k] for l in range(sections)], axis=0).astype(F32)
        normed = (patch * norm_scale(patch)).astype(BF)
        normed_buf[...] = normed
        pre = dot_nn(normed, down_ref[...])
        act = gelu_tanh(pre).astype(BF)
        out = (patch + dot_nn(act, up_ref[...])).astype(BF)
        out_buf[k] = out
        out32 = out.astype(F32)
        total = total + jnp.sum(out32 * out32, axis=1, keepdims=True)
        state_ref[k] = gelu_slope(pre)
        state_ref[4 + k] = dot_nt(out, up_ref[...])
        wide_ref[:, k * RANK:(k + 1) * RANK] = act
        cross = dot(in_ref[k], up_ref[...], (0, 1))
        wide_ref[:, (4 + k) * RANK:(5 + k) * RANK] = cross.astype(BF)
        at = 8 * RANK + k * span
        wide_ref[:, at:at + span] = normed_buf[:, own]
        at += 4 * span
        wide_ref[:, at:at + span] = out_buf[k, :, own]
        in_window_ref[k * span:(k + 1) * span, :] = in_ref[k, own, :]
    scale = lax.rsqrt(total * (1.0 / (4 * width)) + EPS)
    proj = jnp.zeros((RANK, RANK), F32)
    for k in range(4):
        proj = proj + dot_nn((out_buf[k].astype(F32) * scale).astype(BF), in_ref[k])
    state_ref[8] = proj
    state_ref[9] = jnp.broadcast_to(scale, (RANK, RANK))
    per = sections // 4
    own = pl.ds(
        pl.multiple_of(lax.rem(sec, per) * in_windows[0], RANK), in_windows[1] * RANK
    )
    out = out_buf[sec // per, :, own].astype(F32)
    wide_ref[:, 8 * RANK + 8 * span:] = (out * scale).astype(BF)


def encoder_front(sec, images, enc_down, enc_up, proj_in):
    sections = images.shape[0]
    width = images.shape[3]
    windows = window(width, sections)
    in_windows = window(width, sections // 4)
    span = windows[1] * RANK
    total = 8 * RANK + 8 * span + in_windows[1] * RANK
    return pl.pallas_call(
        functools.partial(front_kernel, sections, windows, in_windows),
        in_specs=[SMEM] + [VMEM] * 4,
        out_specs=[VMEM] * 3,
        out_shape=[
            jax.ShapeDtypeStruct((10, RANK, RANK), F32),
            jax.ShapeDtypeStruct((RANK, total), BF),
            jax.ShapeDtypeStruct((4 * span, RANK), BF),
        ],
        scratch_shapes=[
            pltpu.VMEM((RANK, width), BF),
            pltpu.VMEM((4, RANK, width), BF),
        ],
        compiler_params=PARAMS,
    )(scalars(sec), images, enc_down, enc_up, proj_in)


def pack_kernel(layers, core_ref, gram_ref, out_ref, packed):
    at = 0
    for l in range(layers):
        size = (l + 2) * 16
        packed[at:at + size, :] = gram_ref[l, :size, :]
        at += size
    half = at // 2
    value = packed[pl.ds(pl.multiple_of(core_ref[0] * half, 16), half), :]
    for to in range(out_ref.shape[0]):
        out_ref[to] = value


def pack_gram(core, gram, groups):
    layers = gram.shape[0]
    total = sum((l + 2) * 16 for l in range(layers))
    return pl.pallas_call(
        functools.partial(pack_kernel, layers),
        in_specs=[SMEM, VMEM],
        out_specs=VMEM,
        out_shape=jax.ShapeDtypeStruct((groups, total // 2, RANK), BF),
        scratch_shapes=[pltpu.VMEM((total, RANK), BF)],
        compiler_params=PARAMS,
    )(scalars(core), gram)


def rank_kernel(
    layers, width,
    place_ref, own_ref, other_ref, gath_ref, state_ref, cot_ref, norm_ref, image_gram_ref, sel_ref,
    coef_ref, factor_ref, image_ref,
    weight, acts, act_cat, grads, scaled, back, pre_ref, slope_ref, inner_ref, scale_ref,
):
    rank = RANK
    own = place_ref[0]
    core = place_ref[1]
    at = 0
    for l in range(layers):
        for j in range(l + 2):
            which, place = divmod(at, own_ref.shape[1])
            span = slice(place, place + 16)
            tile = jnp.where(core == which, own_ref[:, span, :], other_ref[:, span, :])
            tile = tile.astype(F32)
            rows = slice(j * rank, (j + 1) * rank)
            weight[l, rows, :rank] = tile[:, :8, :].reshape(rank, rank).astype(BF)
            weight[l, rows, rank:] = tile[:, 8:, :].reshape(rank, rank).astype(BF)
            at += 16

    proj_pre = state_ref[8]
    sel = sel_ref[...]
    placed = dot_nn(sel, gelu_tanh(proj_pre).astype(BF))
    placed_half = placed.astype(BF)
    acts[0] = placed_half
    act_cat[:, :rank] = placed_half
    image_inner = dot_nn(placed_half, image_gram_ref[...])
    total = norm_ref[...] + jnp.sum(placed * image_inner, axis=1, keepdims=True)
    for l in range(layers):
        here = (l + 1) * rank
        scale = lax.rsqrt(jnp.maximum(total, 0.0) * (1.0 / width) + EPS)
        both = dot_nn(act_cat[:, :here], weight[l, :here, :])
        pre = scale * (gath_ref[l, :rank, :].astype(F32) + both[:, :rank])
        inner = gath_ref[l, rank:2 * rank, :].astype(F32) + both[:, rank:]
        sig = jax.nn.sigmoid(pre)
        act = (pre * sig).astype(BF)
        acts[l + 1] = act
        act_cat[:, here:here + rank] = act
        after = inner + dot_nn(act, weight[l, here:here + rank, rank:])
        total = total + jnp.sum(act.astype(F32) * (inner + after), axis=1, keepdims=True)
        pre_ref[l] = pre
        slope_ref[l] = sig * (1.0 + pre * (1.0 - sig))
        inner_ref[l] = after
        scale_ref[l] = scale
    back[...] = jnp.zeros_like(back)
    sums = jnp.zeros_like(total)
    for l in reversed(range(layers)):
        here = (l + 1) * rank
        cot = gath_ref[l, 2 * rank:3 * rank, :].astype(F32)
        d_act = cot - sums * inner_ref[l] + back[:, here:here + rank]
        d_pre = (d_act * slope_ref[l]).astype(BF).astype(F32)
        scale = scale_ref[l]
        mean = jnp.sum(d_pre * pre_ref[l], axis=1, keepdims=True) * (1.0 / width)
        grad = (scale * d_pre).astype(BF)
        part = (sums * acts[l + 1].astype(F32)).astype(BF)
        grads[l] = grad
        scaled[l + 1] = part
        pair = jnp.concatenate([grad, -part], axis=1)
        back[:, :here] += dot_nt(pair, weight[l, :here, :])
        sums = sums + scale * scale * mean
    d_image = cot_ref[...] - sums * image_inner + back[:, :rank]
    scaled[0] = (sums * placed).astype(BF)
    d_slot = dot_tn(sel, d_image.astype(BF))
    image_ref[0] = (d_slot * gelu_slope(proj_pre)).astype(BF)
    image_ref[1] = placed_half
    image_ref[2] = scaled[0]

    own_act = acts[own + 1]
    own_grad = grads[own]
    own_scaled = scaled[own + 1]
    factor_ref[0] = own_grad
    factor_ref[1] = own_act
    factor_ref[2] = own_scaled
    coef_ref[0] = dot_tn(acts[0], own_grad).astype(BF)
    for l in range(layers):
        low = l < own
        left = jnp.where(low, acts[l + 1], grads[l])
        right = jnp.where(low, own_grad, own_act)
        coef_ref[l + 1] = dot_tn(left, right).astype(BF)
    for l in range(layers + 1):
        low = l <= own + 1
        left = jnp.where(low, acts[l], scaled[l])
        right = jnp.where(low, own_scaled, own_act)
        coef_ref[layers + 1 + l] = dot_tn(left, right).astype(BF)


def rank_space(position, core, gram, other, gath, state, cot, norms, image_gram, sel, width):
    layers = gath.shape[0]
    rank = RANK
    tall = (layers + 1) * rank
    return pl.pallas_call(
        functools.partial(rank_kernel, layers, width),
        in_specs=[SMEM] + [VMEM] * 8,
        out_specs=[VMEM] * 3,
        out_shape=[
            jax.ShapeDtypeStruct((2 * layers + 2, rank, rank), BF),
            jax.ShapeDtypeStruct((3, rank, rank), BF),
            jax.ShapeDtypeStruct((3, rank, rank), BF),
        ],
        scratch_shapes=[
            pltpu.VMEM((layers, tall, 2 * rank), BF),
            pltpu.VMEM((layers + 1, rank, rank), BF),
            pltpu.VMEM((rank, tall), BF),
            pltpu.VMEM((layers, rank, rank), BF),
            pltpu.VMEM((layers + 1, rank, rank), BF),
            pltpu.VMEM((rank, tall), F32),
            pltpu.VMEM((layers, rank, rank), F32),
            pltpu.VMEM((layers, rank, rank), F32),
            pltpu.VMEM((layers, rank, rank), F32),
            pltpu.VMEM((layers, rank, 1), F32),
        ],
        compiler_params=PARAMS,
    )(scalars(position, core), gram, other, gath, state, cot, norms, image_gram, sel)


def late_kernel(
    enc_width, tiles, in_tiles, pieces,
    shift_ref, image_ref, state_ref, wide_ref, in_ref, block_ref,
    part_ref,
    down, up, proj, last,
):
    span = tiles * RANK
    d_proj = image_ref[0]
    placed = image_ref[1]
    d_proj32 = d_proj.astype(F32)
    proj_scale = state_ref[9]
    mean = jnp.sum(d_proj32 * state_ref[8], axis=1, keepdims=True) * (1.0 / (4 * enc_width))
    d_scaled = (d_proj32 * proj_scale).astype(BF)
    pull = mean * proj_scale * proj_scale
    total_down = jnp.zeros((span, RANK), F32)
    total_up = jnp.zeros((span, RANK), F32)
    for k in range(4):
        act = wide_ref[:, k * RANK:(k + 1) * RANK]
        cross = wide_ref[:, (4 + k) * RANK:(5 + k) * RANK]
        at = 8 * RANK + k * span
        normed = wide_ref[:, at:at + span]
        at += 4 * span
        out = wide_ref[:, at:at + span]
        d_enc = (dot_nn(d_scaled, cross) - pull * state_ref[4 + k]) * state_ref[k]
        total_down += dot_tn(normed, d_enc.astype(BF))
        inner = dot_tn(d_scaled, act).astype(BF)
        total_up += dot_nn(in_ref[k * span:(k + 1) * span, :], inner)
        total_up -= dot_tn(out, (pull * act.astype(F32)).astype(BF))
    down[:span, :] = total_down
    up[:span, :] = total_up
    proj[:in_tiles * RANK, :] = dot_tn(wide_ref[:, 8 * RANK + 8 * span:], d_proj)
    last[...] = dot_tn(block_ref[0], placed) - dot_tn(
        block_ref[1], dot_tn(placed, image_ref[2]).astype(BF)
    )
    groups = part_ref.shape[0]
    n_enc, n_in, pad_enc, pad_in = pieces
    n_out = last.shape[0] // groups
    for to in range(groups):
        at = shift_ref[0] + n_enc * to
        part_ref[to, :pad_enc, :] = down[pl.ds(at, pad_enc), :].astype(BF)
        part_ref[to, pad_enc:2 * pad_enc, :] = up[pl.ds(at, pad_enc), :].astype(BF)
        at = shift_ref[1] + n_in * to
        part_ref[to, 2 * pad_enc:2 * pad_enc + pad_in, :] = proj[pl.ds(at, pad_in), :].astype(BF)
        part_ref[to, 2 * pad_enc + pad_in:, :] = last[to * n_out:(to + 1) * n_out, :].astype(BF)


def encoder_late(sec, image, state, wide, in_window, blocks, enc_width, sections, groups):
    tiles = window(enc_width, sections)[1]
    in_tiles = window(enc_width, sections // 4)[1]
    block = enc_width // sections
    in_block = 4 * block
    n_enc = block // groups
    n_in = in_block // groups
    pad_enc = -(-n_enc // 16) * 16
    pad_in = -(-n_in // 16) * 16
    shifts = scalars(
        sec * (block % RANK), (sec % (sections // 4)) * (in_block % RANK)
    )
    columns = blocks.shape[2]
    total = 2 * pad_enc + pad_in + columns // groups
    pieces = (n_enc, n_in, pad_enc, pad_in)
    parts = pl.pallas_call(
        functools.partial(late_kernel, enc_width, tiles, in_tiles, pieces),
        in_specs=[SMEM] + [VMEM] * 5,
        out_specs=VMEM,
        out_shape=jax.ShapeDtypeStruct((groups, total, RANK), BF),
        scratch_shapes=[
            pltpu.VMEM((tiles * RANK + 16, RANK), F32),
            pltpu.VMEM((tiles * RANK + 16, RANK), F32),
            pltpu.VMEM((in_tiles * RANK + 16, RANK), F32),
            pltpu.VMEM((columns, RANK), F32),
        ],
        compiler_params=PARAMS,
    )(shifts, image, state, wide, in_window, blocks)
    return parts, pieces


def last_kernel(
    layers,
    place_ref, text_ref, cot_ref, other_text_ref, other_cot_ref,
    factor_ref, mixed_ref, slice_ref, out_ref,
    grad_down_ref, grad_up_ref,
    coef,
):
    sec = place_ref[0]
    core = place_ref[1]
    groups, half, share = text_ref.shape
    chunk = coef.shape[0] // groups
    for at in range(groups):
        coef[at * chunk:(at + 1) * chunk, :] = mixed_ref[at, :chunk, :]

    def block(index):
        return coef[index * RANK:(index + 1) * RANK, :]

    def flat(value):
        return value.reshape(groups * half, value.shape[-1])

    total_down = jnp.zeros((share, RANK), F32)
    total_up = jnp.zeros((RANK, share), F32)
    for first, second, which in (
        (text_ref, cot_ref, core), (other_text_ref, other_cot_ref, 1 - core)
    ):
        span = pl.ds(pl.multiple_of(which * half, half), half)
        text = flat(first[...])
        total_down += dot_tn(text, flat(factor_ref[:, 0, span, :]))
        total_up += dot_tn(flat(factor_ref[:, 1, span, :]), flat(second[...]))
        total_up -= dot_tn(flat(factor_ref[:, 2, span, :]), text)
    total_down += dot_tn(out_ref[...], block(0))
    total_up -= dot_tn(block(layers + 1), out_ref[...])
    turned = jnp.zeros((share, RANK), F32)
    for l in range(layers):
        pair = block(l + 1)
        zero = jnp.zeros_like(pair)
        up = jnp.concatenate(
            [
                slice_ref[l, share + m * RANK:share + (m + 1) * RANK, :]
                for m in range(share // RANK)
            ],
            axis=1,
        )
        total_down += dot_tn(up, jnp.where(l < sec, pair, zero))
        turned += dot_nn(slice_ref[l, :share, :], jnp.where(l > sec, pair, zero))
        total_up -= dot_tn(block(layers + 2 + l), up)
    grad_down_ref[...] = total_down
    grad_up_ref[...] = total_up + turned.T


def last_products(sec, own, other, factors, mixed, slices, out):
    layers = slices.shape[0]
    share = out.shape[1]
    return pl.pallas_call(
        functools.partial(last_kernel, layers),
        in_specs=[SMEM] + [VMEM] * 8,
        out_specs=[VMEM] * 2,
        out_shape=[
            jax.ShapeDtypeStruct((share, RANK), F32),
            jax.ShapeDtypeStruct((RANK, share), F32),
        ],
        scratch_shapes=[pltpu.VMEM(((2 * layers + 2) * RANK, RANK), BF)],
        compiler_params=PARAMS,
    )(scalars(sec, sec % 2), *own, *other, factors, mixed, slices, out)


def spread(value, axis):
    count = lax.axis_size(axis)
    return lax.all_to_all(jnp.broadcast_to(value[None], (count,) + value.shape), axis, 0, 0)


def shards(text, cotangent, dec_down, dec_up, images, enc_down, enc_up, proj_in, proj_out, frame):
    sections = lax.axis_size("section")
    groups = lax.axis_size("dp")
    sec = lax.axis_index("section")
    grp = lax.axis_index("dp")
    core = sec % 2
    slot_count, patch_count, enc_width = images.shape[2:]
    tokens = patch_count // 4
    rows_total, width = text.shape[1:]
    rank = dec_down.shape[2]
    weight_down = dec_down[0]
    weight_up = dec_up[0]
    frames = frame[0]
    text = text[0]
    cot = cotangent[0]
    piece = rank // groups
    swap = [(at, at ^ 1) for at in range(sections)]

    up_rows = lax.all_gather(
        lax.dynamic_slice_in_dim(weight_up, grp * piece, piece, 0), "section", axis=0
    )

    slot_row = jnp.repeat(frames, tokens)[None, :]
    row = jnp.arange(rows_total, dtype=jnp.int32)[:, None]
    column = jnp.arange(rows_total, dtype=jnp.int32)[None, :]
    sel = (slot_row == row // tokens) & (row % tokens == column % tokens)
    keep = 1.0 - jnp.any(sel, axis=1, keepdims=True).astype(F32)
    sel = sel.astype(BF)
    text_cols, cot_cols, proj, cot_image, text_norm, image_gram, picks, blocks, own_slices, out_slice = (
        text_products(
            sec, grp, keep, text, cot, weight_down, weight_up, proj_out, sections, groups
        )
    )
    text_cols = lax.all_to_all(text_cols, "dp", 0, 0)
    own_images = images[0, 0].reshape(slot_count * tokens, 4, enc_width).transpose(1, 0, 2)

    image_rows = lax.dynamic_slice_in_dim(proj_out, grp * piece, piece, 0)
    up_rows, text_cols, cot_cols, own_images, image_rows = lax.optimization_barrier(
        (up_rows, text_cols, cot_cols, own_images, image_rows)
    )
    cot_cols = lax.all_to_all(cot_cols, "dp", 0, 0)
    group_images = lax.all_gather(own_images, "section", axis=0)
    rows = jnp.concatenate([image_rows[None], up_rows], axis=0).reshape(-1, width)
    gram = jnp.stack(
        [
            dot_nn(rows, weight_down).reshape(sections + 1, piece, rank),
            dot_nt(rows, weight_up).reshape(sections + 1, piece, rank),
        ],
        axis=1,
    ).astype(BF).reshape(-1, rank)
    packed = pack_gram(core, lax.all_gather(gram, "section", axis=0), groups)
    packed, cot_cols, proj = lax.optimization_barrier((packed, cot_cols, proj))
    own_gram = lax.all_to_all(packed, "dp", 0, 0)

    gath = lax.all_gather(proj, "section", axis=0)
    quarters = proj_in.reshape(4, enc_width, rank)
    state, wide, in_window = encoder_front(sec, group_images, enc_down, enc_up, quarters)
    own_gram, gath, state, wide, in_window = lax.optimization_barrier(
        (own_gram, gath, state, wide, in_window)
    )
    other_gram = lax.ppermute(own_gram, "section", swap)
    own_cols = (text_cols, cot_cols)
    other_cols = tuple(lax.ppermute(cols, "section", swap) for cols in own_cols)
    own_slices, state = lax.optimization_barrier((own_slices, state))
    slices = lax.all_gather(own_slices, "section", axis=0)

    coef, factor, image = rank_space(
        sec, core, own_gram, other_gram, gath, state, cot_image, text_norm, image_gram, sel, width
    )
    coef = lax.all_to_all(coef.reshape(groups, -1, rank), "dp", 0, 0)
    factors = lax.all_gather(factor, "dp", axis=0)

    parts, (n_enc, n_in, pad_enc, pad_in) = encoder_late(
        sec, image, state, wide, in_window, blocks, enc_width, sections, groups
    )
    coef = jnp.sum(coef.astype(F32), axis=0).astype(BF)
    chunk = coef.shape[0]
    mixed = jnp.concatenate(
        [jnp.broadcast_to(coef[None], (groups,) + coef.shape), parts], axis=1
    )
    mixed = lax.all_to_all(mixed, "dp", 0, 0)

    first_coef = mixed[0, :rank]
    at = (sections + 1) * rank
    last_coef = mixed[at // chunk, at % chunk:at % chunk + rank]
    few = picks.shape[2]
    term = dot_nt(picks[:, 0].reshape(-1, rank), first_coef)
    term = term - dot_nt(picks[:, 1].reshape(-1, rank), last_coef)
    term = lax.all_to_all(term.astype(BF).reshape(sections, few, rank), "section", 0, 0)

    grad_dec_down, grad_dec_up = last_products(
        sec, own_cols, other_cols, factors, mixed, slices, out_slice
    )
    parts = jnp.sum(mixed[:, chunk:].astype(F32), axis=0)
    grad_enc_down = parts[:n_enc]
    grad_enc_up = parts[pad_enc:pad_enc + n_enc].T
    grad_proj_in = parts[2 * pad_enc:2 * pad_enc + n_in]
    own_out = parts[2 * pad_enc + pad_in:]
    grad_proj_out = (own_out + jnp.sum(term.astype(F32), axis=0)).T
    return (
        grad_dec_down[None],
        grad_dec_up[None],
        grad_enc_down,
        grad_enc_up,
        grad_proj_in,
        grad_proj_out,
    )


def solution(mesh):
    placed = (
        P("dp", None, None),
        P("dp", None, None),
        P("section", None, None),
        P("section", None, None),
        P("dp", "section", None, None, None),
        P(),
        P(),
        P(),
        P(),
        P("dp", None),
    )
    return jax.shard_map(
        shards,
        mesh=mesh,
        in_specs=placed,
        out_specs=(
            P("section", "dp", None),
            P("section", None, "dp"),
            P(("section", "dp"), None),
            P(None, ("section", "dp")),
            P(("section", "dp"), None),
            P(None, ("section", "dp")),
        ),
        check_vma=False,
    )
```

time: 270 us -> 208 us (0.77)
  starting transfers between devices: 105 us -> 36.1 us
  waiting for transfers between devices: 46.2 us -> 54.6 us
  Pallas kernels: 35.7 us -> 32.4 us
  other arithmetic: 2.29 us -> 5.43 us
    ppermute x38 -> x2, starting transfers between devices: 76 us -> 0.58 us  [shards(): lax.ppermute(cols, 'section', swap)]
    all_to_all x3 -> x4, waiting for transfers between devices: 3.98 us -> 43.6 us  [the longest x1 23.6 us: shards(): mixed = lax.all_to_all(mixed, 'dp', 0, 0)]
    all_to_all x1, waiting for transfers between devices: 22 us -> 0.01 us  [shards(): own_gram = lax.all_to_all(packed, 'dp', 0, 0)]
    ppermute x38 -> x2, waiting for transfers between devices: 19.4 us -> 0.01 us  [shards(): lax.ppermute(cols, 'section', swap)]
    unnamed x43 -> x68, local copies, waits for them, and re-layouts: 8.45 us -> 24.1 us
    all_gather x1 -> x2, blocking collectives: 14.2 us -> 28.3 us  [the longest x1 14.7 us: shards(): gath = lax.all_gather(proj, 'section', axis=0)]
    all_to_all x1 -> x0, blocking collectives: 13.7 us -> none  [spread(): lax.all_to_all(jnp.broadcast_to(value[None], (count,) + value.shape), axi...]
    dynamic_slice x8 -> x2, local copies, waits for them, and re-layouts: 12.4 us -> 2.47 us  [the longest x1 1.55 us: shards(): lax.dynamic_slice_in_dim(weight_up, grp * piece, piece, 0)]
  transfers between devices with their start and end apart: 47 -> 13, of which waited for: 6 -> 6; matrix products, arithmetic and copies ran while one was open for 12% -> 7% of each run, Pallas kernels for 11% -> 13%
where the time goes in v3:
time: 208 us; the launch traced here: 206 us
  waiting for transfers between devices  54.6 us (26%)
  starting transfers between devices  36.1 us (17%)
  Pallas kernels  32.4 us (16%)
  local copies, waits for them, and re-layouts  29.7 us (14%)
  blocking collectives  28.3 us (14%)
  between operations  14.1 us (7%)
  matrix products  5.68 us (3%)
  other arithmetic  5.43 us (3%)
    unnamed x68, local copies, waits for them, and re-layouts  24.1 us
    all_to_all x1, waiting for transfers between devices, shards(): mixed = lax.all_to_all(mixed, 'dp', 0, 0)  23.6 us
    all_to_all x1, waiting for transfers between devices, shards(): text_cols = lax.all_to_all(text_cols, 'dp', 0, 0)  16.5 us
    all_gather x1, blocking collectives, shards(): gath = lax.all_gather(proj, 'section', axis=0)  14.7 us
    all_gather x1, blocking collectives, shards(): packed = pack_gram(core, lax.all_gather(gram, 'section', axis=0), groups)  13.6 us
    pallas_call x1, Pallas kernels, text_products(): pl.pallas_call(functools.partial(text_kernel, half, share, few, steps), g...  9.39 us
    pallas_call x1, Pallas kernels, encoder_front(): pl.pallas_call(functools.partial(front_kernel, sections, windows, in_wind...  9.24 us
    all_to_all x1, starting transfers between devices, shards(): text_cols = lax.all_to_all(text_cols, 'dp', 0, 0)  8.31 us
  transfers between devices with their start and end apart: 13, of which 6 were waited for; matrix products, arithmetic and copies ran while one was open for 7% of the time, Pallas kernels for 13%

profile of v3, /device:TPU:0, one launch (start us, length us, event | category | flops | bytes accessed | tf_op | source)
XLA Modules:
  0.0 206.3 jit_solution(5148412061807005119)
XLA Ops:
  7.2 1.6 constant_dynamic-slice_fusion.1
  10.6 1.6 copy-done.4
  12.2 9.4 %shard_map.145 = (bf16[16,64,512]{2,1,0:T(8,128)(2,1)}, bf16[16,64,512]{2,1,0:T(8,128)(2,1)}, bf16[384,128]{1,0:T(8,128)(2,1)S(1)}, f32[128,128]{1,0:T(8,128)S(1...) custom-call(s32[3]{0:T(128)S(1)} %pad_add_fusion.1.place_ref, ...), custom_call_target="tpu_custom_call" | custom-call | tf_op jit(solution)/shard_map/pallas_call | solution.py:133
  24.4 8.3 %all-to-all-start = ((bf16[16,64,512]{2,1,0:T(8,128)(2,1)}), bf16[16,64,512]{2,1,0:T(8,128)(2,1)S(1)}, u32[]{:S(2)}, u32[]{:S(2)}) async-start(bf16[16,64,512]{2,1,0:T(8,128)(2,1)} %get-tuple-element.39), calls=%async_computation | async-start | bytes 2097152 | tf_op jit(solution)/shard_map/all_to_all | solution.py:576
  33.8 16.5 %all-to-all-done.text_ref = bf16[16,64,512]{2,1,0:T(8,128)(2,1)S(1)} async-done(((bf16[16,64,512]{2,1,0:T(8,128)(2,1)}), bf16[16,64,512]{2,1,0:T(8,128)(2,1)S(1)}, u32[]{:S(2)}, u32[]{:S(2)}) %all-to-all-start) | async-done | bytes 1048608 | tf_op jit(solution)/shard_map/all_to_all | solution.py:576
  51.2 3.7 %all-to-all-start.1 = ((bf16[16,64,512]{2,1,0:T(8,128)(2,1)}), bf16[16,64,512]{2,1,0:T(8,128)(2,1)S(1)}, u32[]{:S(2)}, u32[]{:S(2)}) async-start(bf16[16,64,512]{2,1,0:T(8,128)(2,1)} %get-tuple-element.44), calls=%async_computation.1 | async-start | bytes 2097152 | tf_op jit(solution)/shard_map/all_to_all | solution.py:583
  54.9 2.3 %fusion.14 = bf16[9,1,8,128]{3,2,0,1:T(8,128)(2,1)S(1)} fusion(bf16[1,8192,128]{2,1,0:T(8,128)(2,1)} %param.12, bf16[8,8,8192]{2,1,0:T(8,128)(2,1)S(1)} %copy-done.32, bf16[1,8,8192]{2,1,0:T(8,128)(2,1)S(1)} %bitcast.69), kind=kOutput, calls=%fused_computation.12 | convolution fusion | flops 151593984 | bytes 3295232 | tf_op jit(solution)/shard_map/dot_general | solution.py:32
  58.1 13.6 %all_gather.32.gram_ref = bf16[8,144,128]{2,1,0:T(8,128)(2,1)S(1)} all-gather(bf16[1,144,128]{2,1,0:T(8,128)(2,1)S(1)} %bitcast.73), channel_id=1, replica_groups=mesh['section'=8,'dp'=16] {'section'}, dimensions={0}, use_global_device_ids=true | all-gather | bytes 331776 | tf_op jit(solution)/shard_map/all_gather | solution.py:593
  73.0 7.2 %all-to-all-start.2 = ((bf16[16,352,128]{2,1,0:T(8,128)(2,1)}), bf16[16,352,128]{2,1,0:T(8,128)(2,1)S(1)}, u32[]{:S(2)}, u32[]{:S(2)}) async-start(bf16[16,352,128]{2,1,0:T(8,128)(2,1)} %shard_map.146), calls=%async_computation.2 | async-start | bytes 2883584 | tf_op jit(solution)/shard_map/all_to_all | solution.py:595
  80.3 14.7 %all-gather = bf16[3072,128]{1,0:T(8,128)(2,1)} all-gather(bf16[384,128]{1,0:T(8,128)(2,1)} %copy-done.21), channel_id=2, replica_groups=mesh['section'=8,'dp'=16] {'section'}, dimensions={0}, use_global_device_ids=true | all-gather | bytes 884736 | tf_op jit(solution)/shard_map/all_gather | solution.py:597
  97.3 9.2 %shard_map.147 = (f32[10,128,128]{2,1,0:T(8,128)S(1)}, bf16[128,6784]{1,0:T(8,128)(2,1)S(1)}, bf16[2048,128]{1,0:T(8,128)(2,1)S(1)}) custom-call(s32[1]{0:T(128)} %bitcast.place_ref, bf16[8,4,16,3200]{3,2,1,0:T(8,128)(2,1)} %bitcast.65, bf16[3200,128]{1,0:T(8,128)(2,1)S(1)} %copy-done.8, bf16[128,3200]{1,0:T(8,128)(2,1)S(1)} %copy-done.9, ...), custom_call_target="tpu_custom_call" | custom-call | tf_op jit(solution)/shard_map/pallas_call | solution.py:237
  110.2 2.8 %collective-permute-done.2.other_ref = bf16[16,352,128]{2,1,0:T(8,128)(2,1)S(1)} collective-permute-done((bf16[16,352,128]{2,1,0:T(8,128)(2,1)S(1)}, bf16[16,352,128]{2,1,0:T(8,128)(2,1)S(1)}, u32[]{:S(2)}, u32[]{:S(2)}) %collective-permute-start.2) | collective-permute-done | bytes 1441824 | tf_op jit(solution)/shard_map/ppermute | solution.py:603
  118.4 5.1 %shard_map.148 = (bf16[18,128,128]{2,1,0:T(8,128)(2,1)S(1)}, bf16[3,128,128]{2,1,0:T(8,128)(2,1)S(1)}, bf16[3,128,128]{2,1,0:T(8,128)(2,1)S(1)}) custom-call(s32[2]{0:T(128)S(1)} %pad_add_fusion.place_ref, bf16[16,352,128]{2,1,0:T(8,128)(2,1)S(1)} %all-to-all-done.2.own_ref, bf16[16,352,128]{2,1,0:T(8,128)(2,1)S(1)} %collective-permute-done.2.other_ref, ...), custom_call_target="tpu_custom_call" | custom-call | tf_op jit(solution)/shard_map/pallas_call | solution.py:370
  125.6 7.3 %all-to-all-start.3 = ((bf16[16,144,128]{2,1,0:T(8,128)(2,1)}), bf16[16,144,128]{2,1,0:T(8,128)(2,1)}, u32[]{:S(2)}, u32[]{:S(2)}) async-start(bf16[16,144,128]{2,1,0:T(8,128)(2,1)} %bitcast.61), calls=%async_computation.3 | async-start | bytes 1179648 | tf_op jit(solution)/shard_map/all_to_all | solution.py:612
  134.6 1.5 copy-done.6
  139.1 1.9 shard_map.149
  141.0 4.7 %all-to-all-done.3 = bf16[16,144,128]{2,1,0:T(8,128)(2,1)} async-done(((bf16[16,144,128]{2,1,0:T(8,128)(2,1)}), bf16[16,144,128]{2,1,0:T(8,128)(2,1)}, u32[]{:S(2)}, u32[]{:S(2)}) %all-to-all-start.3) | async-done | bytes 589856 | tf_op jit(solution)/shard_map/all_to_all | solution.py:612
  148.2 4.5 %all-to-all-start.4 = ((bf16[16,384,128]{2,1,0:T(8,128)(2,1)}), bf16[16,384,128]{2,1,0:T(8,128)(2,1)}, u32[]{:S(2)}, u32[]{:S(2)}) async-start(bf16[16,384,128]{2,1,0:T(8,128)(2,1)} %pad_maximum_fusion), calls=%async_computation.4 | async-start | bytes 3145728 | tf_op jit(solution)/shard_map/all_to_all | solution.py:623
  153.4 23.6 %all-to-all-done.4.mixed_ref = bf16[16,384,128]{2,1,0:T(8,128)(2,1)} async-done(((bf16[16,384,128]{2,1,0:T(8,128)(2,1)}), bf16[16,384,128]{2,1,0:T(8,128)(2,1)}, u32[]{:S(2)}, u32[]{:S(2)}) %all-to-all-start.4) | async-done | bytes 1572896 | tf_op jit(solution)/shard_map/all_to_all | solution.py:623
  177.9 1.6 fusion.4
  179.5 3.7 %all-to-all-start.5 = ((bf16[8,64,128]{2,1,0:T(8,128)(2,1)}), bf16[8,64,128]{2,1,0:T(8,128)(2,1)S(1)}, u32[]{:S(2)}, u32[]{:S(2)}) async-start(bf16[8,64,128]{2,1,0:T(8,128)(2,1)} %bitcast.31), calls=%async_computation.5 | async-start | bytes 262144 | tf_op jit(solution)/shard_map/all_to_all | solution.py:631
  185.8 3.5 %all-to-all-done.5 = bf16[8,64,128]{2,1,0:T(8,128)(2,1)S(1)} async-done(((bf16[8,64,128]{2,1,0:T(8,128)(2,1)}), bf16[8,64,128]{2,1,0:T(8,128)(2,1)S(1)}, u32[]{:S(2)}, u32[]{:S(2)}) %all-to-all-start.5) | async-done | bytes 131104 | tf_op jit(solution)/shard_map/all_to_all | solution.py:631
  190.0 3.0 %all-gather.13.cloned.1.call-done = bf16[48,128,128]{2,1,0:T(8,128)(2,1)} async-done(((bf16[3,128,128]{2,1,0:T(8,128)(2,1)}), bf16[48,128,128]{2,1,0:T(8,128)(2,1)}) %all-gather.13.cloned.1.call-update) | async-done | bytes 1572880 | tf_op jit(solution)/shard_map/all_gather | solution.py:613
  194.4 5.4 %shard_map.150 = (f32[512,128]{1,0:T(8,128)}, f32[128,512]{1,0:T(8,128)}) custom-call(s32[2]{0:T(128)S(1)} %pad_add_fusion.place_ref, bf16[16,64,512]{2,1,0:T(8,128)(2,1)S(1)} %all-to-all-done.text_ref, bf16[16,64,512]{2,1,0:T(8,128)(2,1)S(1)} %all-to-all-done.1.cot_ref, bf16[16,64,512]{2,1,0:T(8,128)(2,1)S(1)} %collective-permute-done.other_text_ref, ...), custom_call_target="tpu_custom_call" | custom-call | tf_op jit(solution)/shard_map/pallas_call | solution.py:525
  (110 shorter events, 35.7 us)
Async XLA Ops:
  7.2 43.2 %all-gather.9.cloned.1.call-start = ((), (), s32[]{:S(2)}) async-start(), calls=%async_computation.6 | async-start | bytes 1179648 | tf_op jit(solution)/shard_map/all_gather | solution.py:561
  10.6 1.6 copy-start.4
  24.3 9.4 %copy-start.16 = (bf16[8,2,64,128]{3,2,1,0:T(8,128)(2,1)}, bf16[8,2,64,128]{3,2,1,0:T(8,128)(2,1)S(1)}, u32[]{:S(2)}) copy-start(bf16[8,2,64,128]{3,2,1,0:T(8,128)(2,1)S(1)} %get-tuple-element.71) | copy-start | bytes 786436
  24.3 9.4 %copy-start.18 = (bf16[128,512]{1,0:T(8,128)(2,1)}, bf16[128,512]{1,0:T(8,128)(2,1)S(1)}, u32[]{:S(2)}) copy-start(bf16[128,512]{1,0:T(8,128)(2,1)S(1)} %get-tuple-element.68.out_ref) | copy-start | bytes 393220
  24.3 9.5 %copy-start.21 = (bf16[384,128]{1,0:T(8,128)(2,1)}, bf16[384,128]{1,0:T(8,128)(2,1)S(1)}, u32[]{:S(2)}) copy-start(bf16[384,128]{1,0:T(8,128)(2,1)S(1)} %get-tuple-element.48) | copy-start | bytes 294916
  24.4 9.5 %copy-start.29 = (bf16[128,128]{1,0:T(8,128)(2,1)}, bf16[128,128]{1,0:T(8,128)(2,1)S(1)}, u32[]{:S(2)}) copy-start(bf16[128,128]{1,0:T(8,128)(2,1)S(1)} %get-tuple-element.60.image_gram_ref) | copy-start | bytes 98308
  24.4 8.4 %copy-start.33 = (bf16[1,1,2,32,3200]{4,3,2,1,0:T(8,128)(2,1)S(1)}, bf16[1,1,2,32,3200]{4,3,2,1,0:T(8,128)(2,1)}, u32[]{:S(2)}) copy-start(bf16[1,1,2,32,3200]{4,3,2,1,0:T(8,128)(2,1)} %param.14) | copy-start | bytes 1228804
  24.4 26.0 %all-to-all-start = ((bf16[16,64,512]{2,1,0:T(8,128)(2,1)}), bf16[16,64,512]{2,1,0:T(8,128)(2,1)S(1)}, u32[]{:S(2)}, u32[]{:S(2)}) async-start(bf16[16,64,512]{2,1,0:T(8,128)(2,1)} %get-tuple-element.39), calls=%async_computation | async-start | bytes 2097152 | tf_op jit(solution)/shard_map/all_to_all | solution.py:576
  32.7 62.3 %all-gather.11.cloned.1.call-start = ((), (), s32[]{:S(2)}) async-start(), calls=%async_computation.7 | async-start | bytes 3686400 | tf_op jit(solution)/shard_map/all_gather | solution.py:584
  50.3 4.5 %copy-start.32 = (bf16[8,8,8192]{2,1,0:T(8,128)(2,1)S(1)}, bf16[8,8,8192]{2,1,0:T(8,128)(2,1)}, u32[]{:S(2)}) copy-start(bf16[8,8,8192]{2,1,0:T(8,128)(2,1)} %all-gather.9.cloned.1.call-done) | copy-start | bytes 3145732
  51.2 21.9 %all-to-all-start.1 = ((bf16[16,64,512]{2,1,0:T(8,128)(2,1)}), bf16[16,64,512]{2,1,0:T(8,128)(2,1)S(1)}, u32[]{:S(2)}, u32[]{:S(2)}) async-start(bf16[16,64,512]{2,1,0:T(8,128)(2,1)} %get-tuple-element.44), calls=%async_computation.1 | async-start | bytes 2097152 | tf_op jit(solution)/shard_map/all_to_all | solution.py:583
  54.9 2.3 %copy-start.31 = (bf16[1,128,8192]{2,1,0:T(8,128)(2,1)S(1)}, bf16[1,128,8192]{2,1,0:T(8,128)(2,1)}, u32[]{:S(2)}) copy-start(bf16[1,128,8192]{2,1,0:T(8,128)(2,1)} %param.13) | copy-start | bytes 6291460
  73.0 36.4 %all-to-all-start.2 = ((bf16[16,352,128]{2,1,0:T(8,128)(2,1)}), bf16[16,352,128]{2,1,0:T(8,128)(2,1)S(1)}, u32[]{:S(2)}, u32[]{:S(2)}) async-start(bf16[16,352,128]{2,1,0:T(8,128)(2,1)} %shard_map.146), calls=%async_computation.2 | async-start | bytes 2883584 | tf_op jit(solution)/shard_map/all_to_all | solution.py:595
  80.2 109.7 %all-gather.15.cloned.1.call-start = ((), (), s32[]{:S(2)}) async-start(), calls=%async_computation.9 | async-start | bytes 2359296 | tf_op jit(solution)/shard_map/all_gather | solution.py:607
  109.4 3.6 %collective-permute-start.2 = (bf16[16,352,128]{2,1,0:T(8,128)(2,1)S(1)}, bf16[16,352,128]{2,1,0:T(8,128)(2,1)S(1)}, u32[]{:S(2)}, u32[]{:S(2)}) collective-permute-start(bf16[16,352,128]{2,1,0:T(8,128)(2,1)S(1)} %all-to-all-done.2.own_ref), channel_id=1, source_target_pairs={{0,16},{16,0},{32,48},{48,32},{64,80},{80,64},{96,112},{112,96},{1... | collective-permute-start | bytes 4325384 | tf_op jit(solution)/shard_map/ppermute | solution.py:603
  125.6 20.1 %all-to-all-start.3 = ((bf16[16,144,128]{2,1,0:T(8,128)(2,1)}), bf16[16,144,128]{2,1,0:T(8,128)(2,1)}, u32[]{:S(2)}, u32[]{:S(2)}) async-start(bf16[16,144,128]{2,1,0:T(8,128)(2,1)} %bitcast.61), calls=%async_computation.3 | async-start | bytes 1179648 | tf_op jit(solution)/shard_map/all_to_all | solution.py:612
  132.9 60.1 %all-gather.13.cloned.1.call-start = ((), (), s32[]{:S(2)}) async-start(), calls=%async_computation.8 | async-start | bytes 1671168 | tf_op jit(solution)/shard_map/all_gather | solution.py:613
  134.6 1.5 copy-start.6
  148.2 4.5 %copy-start.17 = (bf16[8,2,64,128]{3,2,1,0:T(8,128)(2,1)S(1)}, bf16[8,2,64,128]{3,2,1,0:T(8,128)(2,1)}, u32[]{:S(2)}) copy-start(bf16[8,2,64,128]{3,2,1,0:T(8,128)(2,1)} %copy-done.16) | copy-start | bytes 786436
  148.2 28.7 %all-to-all-start.4 = ((bf16[16,384,128]{2,1,0:T(8,128)(2,1)}), bf16[16,384,128]{2,1,0:T(8,128)(2,1)}, u32[]{:S(2)}, u32[]{:S(2)}) async-start(bf16[16,384,128]{2,1,0:T(8,128)(2,1)} %pad_maximum_fusion), calls=%async_computation.4 | async-start | bytes 3145728 | tf_op jit(solution)/shard_map/all_to_all | solution.py:623
  152.8 40.2 %copy-start.19 = (bf16[128,512]{1,0:T(8,128)(2,1)S(1)}, bf16[128,512]{1,0:T(8,128)(2,1)}, u32[]{:S(2)}) copy-start(bf16[128,512]{1,0:T(8,128)(2,1)} %copy-done.18) | copy-start | bytes 393220
  152.8 37.1 %collective-permute-start = (bf16[16,64,512]{2,1,0:T(8,128)(2,1)S(1)}, bf16[16,64,512]{2,1,0:T(8,128)(2,1)S(1)}, u32[]{:S(2)}, u32[]{:S(2)}) collective-permute-start(bf16[16,64,512]{2,1,0:T(8,128)(2,1)S(1)} %all-to-all-done.text_ref), channel_id=1, source_target_pairs={{0,16},{16,0},{32,48},{48,32},{64,80},{80,64},{96,112},{112,96},{1... | collective-permute-start | bytes 3145736 | tf_op jit(solution)/shard_map/ppermute | solution.py:605
  152.9 37.1 %collective-permute-start.1 = (bf16[16,64,512]{2,1,0:T(8,128)(2,1)S(1)}, bf16[16,64,512]{2,1,0:T(8,128)(2,1)}, u32[]{:S(2)}, u32[]{:S(2)}) collective-permute-start(bf16[16,64,512]{2,1,0:T(8,128)(2,1)S(1)} %all-to-all-done.1.cot_ref), channel_id=1, source_target_pairs={{0,16},{16,0},{32,48},{48,32},{64,80},{80,64},{96,112},{112,96},{1... | collective-permute-start | bytes 3145736 | tf_op jit(solution)/shard_map/ppermute | solution.py:605
  179.5 9.8 %all-to-all-start.5 = ((bf16[8,64,128]{2,1,0:T(8,128)(2,1)}), bf16[8,64,128]{2,1,0:T(8,128)(2,1)S(1)}, u32[]{:S(2)}, u32[]{:S(2)}) async-start(bf16[8,64,128]{2,1,0:T(8,128)(2,1)} %bitcast.31), calls=%async_computation.5 | async-start | bytes 262144 | tf_op jit(solution)/shard_map/all_to_all | solution.py:631
  (23 other events, 21.0 us)
Sparse Core Ops, SparseCore 0:
  9.7 25.7 all-gather.8
  51.3 26.5 all-gather.10
  109.6 26.1 all-gather.14
  137.8 55.1 all-gather.12

commit v4 on v3

--- a/solution.py
+++ b/solution.py
@@ -55,14 +55,14 @@
 
 
 def text_kernel(
-    half, share, few, steps,
+    part, share, few, steps,
     place_ref, keep_ref, text_ref, cot_ref, down_ref, up_ref, out_ref,
-    text_cols_ref, cot_cols_ref, proj_ref, image_ref, norm_ref, gram_ref,
+    cols_ref, proj_ref, image_ref, norm_ref, gram_ref,
     pick_ref, block_ref, slice_ref, out_slice_ref,
     proj, image, gram,
 ):
     step = pl.program_id(0)
-    core, sec, grp = place_ref[0], place_ref[1], place_ref[2]
+    sec, grp = place_ref[0], place_ref[1]
 
     @pl.when(step == 0)
     def _():
@@ -81,13 +81,13 @@
     image[...] += dot_nt(cot, out_ref[...])
     gram[...] += dot_nt(out_ref[...], out_ref[...])
 
-    own = pl.ds(pl.multiple_of(core * half, half), half)
+    own = pl.ds(pl.multiple_of(lax.rem(sec, 4) * part, part), part)
     keep = keep_ref[own, :]
-    pieces = text_cols_ref.shape[0]
+    pieces = cols_ref.shape[0]
     for piece in range(pieces):
         span = slice(piece * share, (piece + 1) * share)
-        text_cols_ref[piece] = (text_ref[own, span].astype(F32) * keep).astype(BF)
-        cot_cols_ref[piece] = cot_ref[own, span]
+        cols_ref[piece, :part, :] = (text_ref[own, span].astype(F32) * keep).astype(BF)
+        cols_ref[piece, part:, :] = cot_ref[own, span]
 
     pick_ref[0, 0] = down_ref[pl.ds(pl.multiple_of(grp * few, few), few), :]
     per = RANK // few
@@ -125,13 +125,12 @@
     wide = width // steps
     pieces = wide // share
     few = wide // groups
-    half = rows // 2
+    part = rows // 4
     across = pl.BlockSpec((rows, wide), lambda i: (0, i))
     fixed = pl.BlockSpec((rows, RANK), lambda i: (0, 0))
     column = pl.BlockSpec((rows, 1), lambda i: (0, 0))
-    cols = pl.BlockSpec((pieces, half, share), lambda i: (i, 0, 0))
     return pl.pallas_call(
-        functools.partial(text_kernel, half, share, few, steps),
+        functools.partial(text_kernel, part, share, few, steps),
         grid=(steps,),
         in_specs=[
             SMEM,
@@ -143,8 +142,7 @@
             across,
         ],
         out_specs=[
-            cols,
-            cols,
+            pl.BlockSpec((pieces, 2 * part, share), lambda i: (i, 0, 0)),
             pl.BlockSpec((3 * RANK, RANK), lambda i: (0, 0)),
             fixed,
             column,
@@ -155,8 +153,7 @@
             pl.BlockSpec((rows, share), lambda i: (0, 0)),
         ],
         out_shape=[
-            jax.ShapeDtypeStruct((groups, half, share), BF),
-            jax.ShapeDtypeStruct((groups, half, share), BF),
+            jax.ShapeDtypeStruct((groups, 2 * part, share), BF),
             jax.ShapeDtypeStruct((3 * RANK, RANK), BF),
             jax.ShapeDtypeStruct((rows, RANK), F32),
             jax.ShapeDtypeStruct((rows, 1), F32),
@@ -172,7 +169,7 @@
             pltpu.VMEM((RANK, RANK), F32),
         ],
         compiler_params=PARAMS,
-    )(scalars(sec % 2, sec, grp), keep, text, cot, down, up, out)
+    )(scalars(sec, grp), keep, text, cot, down, up, out)
 
 
 def window(width, count):
@@ -251,6 +248,13 @@
     )(scalars(sec), images, enc_down, enc_up, proj_in)
 
 
+def two_lanes(column):
+    high = column.astype(BF).astype(F32)
+    lane = lax.broadcasted_iota(jnp.int32, (column.shape[0], RANK), 1)
+    zero = jnp.zeros((column.shape[0], RANK), F32)
+    return jnp.where(lane == 0, high, jnp.where(lane == 1, column - high, zero))
+
+
 def pack_kernel(layers, core_ref, gram_ref, out_ref, packed):
     at = 0
     for l in range(layers):
@@ -280,7 +284,7 @@
     layers, width,
     place_ref, own_ref, other_ref, gath_ref, state_ref, cot_ref, norm_ref, image_gram_ref, sel_ref,
     coef_ref, factor_ref, image_ref,
-    weight, acts, act_cat, grads, scaled, back, pre_ref, slope_ref, inner_ref, scale_ref,
+    weight, acts, act_cat, grads, scaled, back, pre_ref, slope_ref, inner_ref, scale_ref, sums_ref,
 ):
     rank = RANK
     own = place_ref[0]
@@ -334,6 +338,7 @@
         part = (sums * acts[l + 1].astype(F32)).astype(BF)
         grads[l] = grad
         scaled[l + 1] = part
+        sums_ref[l] = sums
         pair = jnp.concatenate([grad, -part], axis=1)
         back[:, :here] += dot_nt(pair, weight[l, :here, :])
         sums = sums + scale * scale * mean
@@ -347,9 +352,9 @@
     own_act = acts[own + 1]
     own_grad = grads[own]
     own_scaled = scaled[own + 1]
-    factor_ref[0] = own_grad
-    factor_ref[1] = own_act
-    factor_ref[2] = own_scaled
+    factor_ref[:rank, :] = own_grad
+    factor_ref[rank:2 * rank, :] = own_act
+    factor_ref[2 * rank:, :] = two_lanes(sums_ref[own]).T[:16].astype(BF)
     coef_ref[0] = dot_tn(acts[0], own_grad).astype(BF)
     for l in range(layers):
         low = l < own
@@ -367,15 +372,18 @@
     layers = gath.shape[0]
     rank = RANK
     tall = (layers + 1) * rank
+    operands = (gram, other, gath, state, cot, norms, image_gram, sel)
+
+    def whole(shape):
+        return pl.BlockSpec(shape, lambda i: (0,) * len(shape))
+
+    outs = ((2 * layers + 2, rank, rank), (2 * rank + 16, rank), (3, rank, rank))
     return pl.pallas_call(
         functools.partial(rank_kernel, layers, width),
-        in_specs=[SMEM] + [VMEM] * 8,
-        out_specs=[VMEM] * 3,
-        out_shape=[
-            jax.ShapeDtypeStruct((2 * layers + 2, rank, rank), BF),
-            jax.ShapeDtypeStruct((3, rank, rank), BF),
-            jax.ShapeDtypeStruct((3, rank, rank), BF),
-        ],
+        grid=(1,),
+        in_specs=[SMEM] + [whole(value.shape) for value in operands],
+        out_specs=[whole(shape) for shape in outs],
+        out_shape=[jax.ShapeDtypeStruct(shape, BF) for shape in outs],
         scratch_shapes=[
             pltpu.VMEM((layers, tall, 2 * rank), BF),
             pltpu.VMEM((layers + 1, rank, rank), BF),
@@ -387,9 +395,10 @@
             pltpu.VMEM((layers, rank, rank), F32),
             pltpu.VMEM((layers, rank, rank), F32),
             pltpu.VMEM((layers, rank, 1), F32),
+            pltpu.VMEM((layers, rank, 1), F32),
         ],
         compiler_params=PARAMS,
-    )(scalars(position, core), gram, other, gath, state, cot, norms, image_gram, sel)
+    )(scalars(position, core), *operands)
 
 
 def late_kernel(
@@ -469,16 +478,67 @@
     return parts, pieces
 
 
+def row_kernel(
+    place_ref, first_ref, second_ref, third_ref, fourth_ref, factor_ref,
+    down_ref, up_ref,
+    acts, scaled,
+):
+    groups, rows, share = first_ref.shape
+    part = rows // 2
+    for at in range(groups):
+        act = factor_ref[at, RANK:2 * RANK, :]
+        weights = factor_ref[at, 2 * RANK:2 * RANK + 8, :].astype(F32)
+        weights = jnp.sum(weights, axis=0, keepdims=True)
+        weights = jnp.broadcast_to(weights, (RANK, RANK)).T
+        acts[at] = act
+        scaled[at] = (act.astype(F32) * weights).astype(BF)
+
+    def flat(value):
+        return value.reshape(groups * part, value.shape[-1])
+
+    total_down = jnp.zeros((share, RANK), F32)
+    total_up = jnp.zeros((RANK, share), F32)
+    own = place_ref[0]
+    for at, cols_ref in enumerate((first_ref, second_ref, third_ref, fourth_ref)):
+        which = lax.rem(own, 2) if at % 2 == 0 else 1 - lax.rem(own, 2)
+        which = which + 2 * (own // 2 if at < 2 else 1 - own // 2)
+        start = pl.multiple_of(which * part, part)
+        text = flat(cols_ref[:, :part, :])
+        cot = flat(cols_ref[:, part:, :])
+        total_down += dot_tn(text, flat(factor_ref[:, pl.ds(start, part), :]))
+        total_up += dot_tn(flat(acts[:, pl.ds(start, part), :]), cot)
+        total_up -= dot_tn(flat(scaled[:, pl.ds(start, part), :]), text)
+    down_ref[...] = total_down
+    up_ref[...] = total_up
+
+
+def row_products(sec, cols, factors):
+    groups, _, share = cols[0].shape
+    return pl.pallas_call(
+        row_kernel,
+        in_specs=[SMEM] + [VMEM] * 5,
+        out_specs=[VMEM] * 2,
+        out_shape=[
+            jax.ShapeDtypeStruct((share, RANK), F32),
+            jax.ShapeDtypeStruct((RANK, share), F32),
+        ],
+        scratch_shapes=[
+            pltpu.VMEM((groups, RANK, RANK), BF),
+            pltpu.VMEM((groups, RANK, RANK), BF),
+        ],
+        compiler_params=PARAMS,
+    )(scalars(sec % 4), *cols, factors)
+
+
 def last_kernel(
     layers,
-    place_ref, text_ref, cot_ref, other_text_ref, other_cot_ref,
-    factor_ref, mixed_ref, slice_ref, out_ref,
+    place_ref, down_ref, up_ref, mixed_ref, slice_ref, out_ref,
     grad_down_ref, grad_up_ref,
     coef,
 ):
     sec = place_ref[0]
-    core = place_ref[1]
-    groups, half, share = text_ref.shape
+    groups = mixed_ref.shape[0]
+    share = out_ref.shape[1]
     chunk = coef.shape[0] // groups
     for at in range(groups):
         coef[at * chunk:(at + 1) * chunk, :] = mixed_ref[at, :chunk, :]
@@ -486,21 +546,8 @@
     def block(index):
         return coef[index * RANK:(index + 1) * RANK, :]
 
-    def flat(value):
-        return value.reshape(groups * half, value.shape[-1])
-
-    total_down = jnp.zeros((share, RANK), F32)
-    total_up = jnp.zeros((RANK, share), F32)
-    for first, second, which in (
-        (text_ref, cot_ref, core), (other_text_ref, other_cot_ref, 1 - core)
-    ):
-        span = pl.ds(pl.multiple_of(which * half, half), half)
-        text = flat(first[...])
-        total_down += dot_tn(text, flat(factor_ref[:, 0, span, :]))
-        total_up += dot_tn(flat(factor_ref[:, 1, span, :]), flat(second[...]))
-        total_up -= dot_tn(flat(factor_ref[:, 2, span, :]), text)
-    total_down += dot_tn(out_ref[...], block(0))
-    total_up -= dot_tn(block(layers + 1), out_ref[...])
+    total_down = down_ref[...] + dot_tn(out_ref[...], block(0))
+    total_up = up_ref[...] - dot_tn(block(layers + 1), out_ref[...])
     turned = jnp.zeros((share, RANK), F32)
     for l in range(layers):
         pair = block(l + 1)
@@ -519,12 +566,12 @@
     grad_up_ref[...] = total_up + turned.T
 
 
-def last_products(sec, own, other, factors, mixed, slices, out):
+def last_products(sec, down, up, mixed, slices, out):
     layers = slices.shape[0]
     share = out.shape[1]
     return pl.pallas_call(
         functools.partial(last_kernel, layers),
-        in_specs=[SMEM] + [VMEM] * 8,
+        in_specs=[SMEM] + [VMEM] * 5,
         out_specs=[VMEM] * 2,
         out_shape=[
             jax.ShapeDtypeStruct((share, RANK), F32),
@@ -532,7 +579,7 @@
         ],
         scratch_shapes=[pltpu.VMEM(((2 * layers + 2) * RANK, RANK), BF)],
         compiler_params=PARAMS,
-    )(scalars(sec, sec % 2), *own, *other, factors, mixed, slices, out)
+    )(scalars(sec), down, up, mixed, slices, out)
 
 
 def spread(value, axis):
@@ -558,9 +605,7 @@
     piece = rank // groups
     swap = [(at, at ^ 1) for at in range(sections)]
 
-    up_rows = lax.all_gather(
-        lax.dynamic_slice_in_dim(weight_up, grp * piece, piece, 0), "section", axis=0
-    )
+    up_rows = spread(lax.dynamic_slice_in_dim(weight_up, grp * piece, piece, 0), "section")
 
     slot_row = jnp.repeat(frames, tokens)[None, :]
     row = jnp.arange(rows_total, dtype=jnp.int32)[:, None]
@@ -568,20 +613,21 @@
     sel = (slot_row == row // tokens) & (row % tokens == column % tokens)
     keep = 1.0 - jnp.any(sel, axis=1, keepdims=True).astype(F32)
     sel = sel.astype(BF)
-    text_cols, cot_cols, proj, cot_image, text_norm, image_gram, picks, blocks, own_slices, out_slice = (
+    cols, proj, cot_image, text_norm, image_gram, picks, blocks, own_slices, out_slice = (
         text_products(
             sec, grp, keep, text, cot, weight_down, weight_up, proj_out, sections, groups
         )
     )
-    text_cols = lax.all_to_all(text_cols, "dp", 0, 0)
     own_images = images[0, 0].reshape(slot_count * tokens, 4, enc_width).transpose(1, 0, 2)
 
     image_rows = lax.dynamic_slice_in_dim(proj_out, grp * piece, piece, 0)
-    up_rows, text_cols, cot_cols, own_images, image_rows = lax.optimization_barrier(
-        (up_rows, text_cols, cot_cols, own_images, image_rows)
-    )
-    cot_cols = lax.all_to_all(cot_cols, "dp", 0, 0)
+    up_rows, cols, own_images, image_rows = lax.optimization_barrier(
+        (up_rows, cols, own_images, image_rows)
+    )
+    cols = lax.all_to_all(cols, "dp", 0, 0)
     group_images = lax.all_gather(own_images, "section", axis=0)
+    own_slices, group_images = lax.optimization_barrier((own_slices, group_images))
+    slices = lax.all_gather(own_slices, "section", axis=0)
     rows = jnp.concatenate([image_rows[None], up_rows], axis=0).reshape(-1, width)
     gram = jnp.stack(
         [
@@ -591,31 +637,31 @@
         axis=1,
     ).astype(BF).reshape(-1, rank)
     packed = pack_gram(core, lax.all_gather(gram, "section", axis=0), groups)
-    packed, cot_cols, proj = lax.optimization_barrier((packed, cot_cols, proj))
+    packed, cols, proj = lax.optimization_barrier((packed, cols, proj))
     own_gram = lax.all_to_all(packed, "dp", 0, 0)
 
     gath = lax.all_gather(proj, "section", axis=0)
     quarters = proj_in.reshape(4, enc_width, rank)
     state, wide, in_window = encoder_front(sec, group_images, enc_down, enc_up, quarters)
-    own_gram, gath, state, wide, in_window = lax.optimization_barrier(
-        (own_gram, gath, state, wide, in_window)
+    own_gram, gath, state, wide, in_window, cols = lax.optimization_barrier(
+        (own_gram, gath, state, wide, in_window, cols)
     )
     other_gram = lax.ppermute(own_gram, "section", swap)
-    own_cols = (text_cols, cot_cols)
-    other_cols = tuple(lax.ppermute(cols, "section", swap) for cols in own_cols)
-    own_slices, state = lax.optimization_barrier((own_slices, state))
-    slices = lax.all_gather(own_slices, "section", axis=0)
+    far = [(at, at ^ 2) for at in range(sections)]
+    far_cols = lax.ppermute(cols, "section", far)
 
     coef, factor, image = rank_space(
         sec, core, own_gram, other_gram, gath, state, cot_image, text_norm, image_gram, sel, width
     )
     coef = lax.all_to_all(coef.reshape(groups, -1, rank), "dp", 0, 0)
+    factor, slices = lax.optimization_barrier((factor, slices))
     factors = lax.all_gather(factor, "dp", axis=0)
 
     parts, (n_enc, n_in, pad_enc, pad_in) = encoder_late(
         sec, image, state, wide, in_window, blocks, enc_width, sections, groups
     )
     coef = jnp.sum(coef.astype(F32), axis=0).astype(BF)
+    coef, far_cols = lax.optimization_barrier((coef, far_cols))
     chunk = coef.shape[0]
     mixed = jnp.concatenate(
         [jnp.broadcast_to(coef[None], (groups,) + coef.shape), parts], axis=1
@@ -630,8 +676,13 @@
     term = term - dot_nt(picks[:, 1].reshape(-1, rank), last_coef)
     term = lax.all_to_all(term.astype(BF).reshape(sections, few, rank), "section", 0, 0)
 
+    every_cols = (
+        cols, lax.ppermute(cols, "section", swap),
+        far_cols, lax.ppermute(far_cols, "section", swap),
+    )
+    row_down, row_up = row_products(sec, every_cols, factors)
     grad_dec_down, grad_dec_up = last_products(
-        sec, own_cols, other_cols, factors, mixed, slices, out_slice
+        sec, row_down, row_up, mixed, slices, out_slice
     )
     parts = jnp.sum(mixed[:, chunk:].astype(F32), axis=0)
     grad_enc_down = parts[:n_enc]

time: 208 us -> 199 us (0.957)
  waiting for transfers between devices: 54.6 us -> 49.1 us
  other arithmetic: 5.43 us -> 3.15 us
    all_to_all x2, waiting for transfers between devices: 16.5 us -> 0.01 us  [the longest x1 0.01 us: spread(): lax.all_to_all(jnp.broadcast_to(value[None], (count,) + value.shape), axi...]
    all_gather x1, waiting for transfers between devices: 2.97 us -> 13.3 us  [shards(): factors = lax.all_gather(factor, 'dp', axis=0)]
    pallas_call x2 -> x3, Pallas kernels: 14.5 us -> 18.5 us  [the longest x1 9.15 us: text_products(): pl.pallas_call(functools.partial(text_kernel, part, share, few, steps), g...]
    pallas_call x1, Pallas kernels: 5.43 us -> 1.91 us  [last_products(): pl.pallas_call(functools.partial(last_kernel, layers), in_specs=[SMEM] +...]
    unnamed x68 -> x64, local copies, waits for them, and re-layouts: 24.1 us -> 20.6 us
  transfers between devices with their start and end apart: 13 -> 13, of which waited for: 6 -> 5; matrix products, arithmetic and copies ran while one was open for 7% -> 6% of each run, Pallas kernels for 13% -> 14%
where the time goes in v4:
time: 199 us; the launch traced here: 197 us
  waiting for transfers between devices  49.1 us (25%)
  starting transfers between devices  37.3 us (19%)
  Pallas kernels  33 us (17%)
  local copies, waits for them, and re-layouts  28.1 us (14%)
  blocking collectives  27.7 us (14%)
  between operations  14.1 us (7%)
  matrix products  5.03 us (3%)
  other arithmetic  3.15 us (2%)
    all_to_all x1, waiting for transfers between devices, shards(): mixed = lax.all_to_all(mixed, 'dp', 0, 0)  22 us
    unnamed x64, local copies, waits for them, and re-layouts  20.6 us
    all_gather x1, blocking collectives, shards(): packed = pack_gram(core, lax.all_gather(gram, 'section', axis=0), groups)  14.1 us
    all_gather x1, blocking collectives, shards(): gath = lax.all_gather(proj, 'section', axis=0)  13.6 us
    all_gather x1, waiting for transfers between devices, shards(): factors = lax.all_gather(factor, 'dp', axis=0)  13.3 us
    pallas_call x1, Pallas kernels, encoder_front(): pl.pallas_call(functools.partial(front_kernel, sections, windows, in_wind...  9.25 us
    pallas_call x1, Pallas kernels, text_products(): pl.pallas_call(functools.partial(text_kernel, part, share, few, steps), g...  9.15 us
    all_to_all x1, starting transfers between devices, shards(): cols = lax.all_to_all(cols, 'dp', 0, 0)  8.06 us
  transfers between devices with their start and end apart: 13, of which 5 were waited for; matrix products, arithmetic and copies ran while one was open for 6% of the time, Pallas kernels for 14%

profile of v4, /device:TPU:0, one launch (start us, length us, event | category | flops | bytes accessed | tf_op | source)
XLA Modules:
  0.0 197.4 jit_solution(18326612376342772749)
XLA Ops:
  9.2 4.5 %all-to-all-start = ((bf16[8,8,8192]{2,1,0:T(8,128)(2,1)}), bf16[8,8,8192]{2,1,0:T(8,128)(2,1)}, u32[]{:S(2)}, u32[]{:S(2)}) async-start(bf16[8,8,8192]{2,1,0:T(8,128)(2,1)} %broadcast_in_dim.30), calls=%async_computation | async-start | bytes 2097152 | tf_op jit(solution)/shard_map/all_to_all | solution.py:587
  15.7 9.2 %shard_map.145 = (bf16[16,64,512]{2,1,0:T(8,128)(2,1)S(1)}, bf16[384,128]{1,0:T(8,128)(2,1)S(1)}, f32[128,128]{1,0:T(8,128)S(1)}, f32[128,1]{1,0:T(8,128)S(1)}, ...) custom-call(s32[2]{0:T(128)S(1)} %pad_add_fusion.place_ref, ...), custom_call_target="tpu_custom_call" | custom-call | tf_op jit(solution)/shard_map/pallas_call | solution.py:132
  29.9 2.0 %copy.25 = bf16[4,16,3200]{2,1,0:T(8,128)(2,1)} copy(bf16[4,16,3200]{2,0,1:T(4,128)(2,1)} %bitcast.71) | data formatting | bytes 819200 | tf_op jit(solution)/shard_map/optimization_barrier | solution.py:624
  31.9 8.1 %all-to-all-start.1 = ((bf16[16,64,512]{2,1,0:T(8,128)(2,1)}), bf16[16,64,512]{2,1,0:T(8,128)(2,1)S(1)}, u32[]{:S(2)}, u32[]{:S(2)}) async-start(bf16[16,64,512]{2,1,0:T(8,128)(2,1)} %copy-done.8), calls=%async_computation.1 | async-start | bytes 2097152 | tf_op jit(solution)/shard_map/all_to_all | solution.py:627
  40.0 1.9 fusion.14
  42.0 2.1 %fusion.11 = bf16[9,1,8,128]{3,2,0,1:T(8,128)(2,1)S(1)} fusion(bf16[1,128,8192]{2,1,0:T(8,128)(2,1)S(1)} %copy-done.28, bf16[8,8,8192]{2,1,0:T(8,128)(2,1)} %all-to-all-done, bf16[1,8,8192]{2,1,0:T(8,128)(2,1)S(1)} %bitcast.73), kind=kOutput, calls=%fused_computation.11 | convolution fusion | flops 151593984 | bytes 3295232 | tf_op jit(solution)/shard_map/dot_general | solution.py:32
  44.0 14.1 %all_gather.27.gram_ref = bf16[8,144,128]{2,1,0:T(8,128)(2,1)S(1)} all-gather(bf16[1,144,128]{2,1,0:T(8,128)(2,1)S(1)} %bitcast.76), channel_id=1, replica_groups=mesh['section'=8,'dp'=16] {'section'}, dimensions={0}, use_global_device_ids=true | all-gather | bytes 331776 | tf_op jit(solution)/shard_map/all_gather | solution.py:639
  59.5 7.3 %all-to-all-start.2 = ((bf16[16,352,128]{2,1,0:T(8,128)(2,1)}), bf16[16,352,128]{2,1,0:T(8,128)(2,1)S(1)}, u32[]{:S(2)}, u32[]{:S(2)}) async-start(bf16[16,352,128]{2,1,0:T(8,128)(2,1)} %shard_map.146), calls=%async_computation.2 | async-start | bytes 2883584 | tf_op jit(solution)/shard_map/all_to_all | solution.py:641
  67.5 13.6 %all-gather = bf16[3072,128]{1,0:T(8,128)(2,1)S(1)} all-gather(bf16[384,128]{1,0:T(8,128)(2,1)} %copy-done.19), channel_id=2, replica_groups=mesh['section'=8,'dp'=16] {'section'}, dimensions={0}, use_global_device_ids=true | all-gather | bytes 884736 | tf_op jit(solution)/shard_map/all_gather | solution.py:643
  83.4 9.2 %shard_map.147 = (f32[10,128,128]{2,1,0:T(8,128)S(1)}, bf16[128,6784]{1,0:T(8,128)(2,1)S(1)}, bf16[2048,128]{1,0:T(8,128)(2,1)S(1)}) custom-call(s32[1]{0:T(128)} %bitcast.place_ref, bf16[8,4,16,3200]{3,2,1,0:T(8,128)(2,1)} %bitcast.69, bf16[3200,128]{1,0:T(8,128)(2,1)S(1)} %copy-done.9, bf16[128,3200]{1,0:T(8,128)(2,1)S(1)} %copy-done.10, ...), custom_call_target="tpu_custom_call" | custom-call | tf_op jit(solution)/shard_map/pallas_call | solution.py:234
  96.1 1.4 collective-permute-start.2
  97.5 1.4 collective-permute-done.1.other_ref
  103.2 5.6 %shard_map.148 = (bf16[18,128,128]{2,1,0:T(8,128)(2,1)S(1)}, bf16[272,128]{1,0:T(8,128)(2,1)}, bf16[3,128,128]{2,1,0:T(8,128)(2,1)S(1)}) custom-call(s32[2]{0:T(128)S(1)} %pad_add_fusion.1.place_ref, bf16[16,352,128]{2,1,0:T(8,128)(2,1)S(1)} %all-to-all-done.2.own_ref, bf16[16,352,128]{2,1,0:T(8,128)(2,1)S(1)} %collective-permute-done.1.other_ref, ...), custom_call_target="tpu_custom_call" | custom-call | tf_op jit(solution)/shard_map/pallas_call | solution.py:381
  110.3 7.4 %all-to-all-start.3 = ((bf16[16,144,128]{2,1,0:T(8,128)(2,1)}), bf16[16,144,128]{2,1,0:T(8,128)(2,1)S(1)}, u32[]{:S(2)}, u32[]{:S(2)}) async-start(bf16[16,144,128]{2,1,0:T(8,128)(2,1)} %bitcast.65), calls=%async_computation.3 | async-start | bytes 1179648 | tf_op jit(solution)/shard_map/all_to_all | solution.py:656
  117.8 1.5 copy-done.6
  122.2 1.9 shard_map.150
  124.1 6.3 %all-to-all-done.3 = bf16[16,144,128]{2,1,0:T(8,128)(2,1)S(1)} async-done(((bf16[16,144,128]{2,1,0:T(8,128)(2,1)}), bf16[16,144,128]{2,1,0:T(8,128)(2,1)S(1)}, u32[]{:S(2)}, u32[]{:S(2)}) %all-to-all-start.3) | async-done | bytes 589856 | tf_op jit(solution)/shard_map/all_to_all | solution.py:656
  131.9 3.7 %all-to-all-start.4 = ((bf16[16,384,128]{2,1,0:T(8,128)(2,1)}), bf16[16,384,128]{2,1,0:T(8,128)(2,1)S(1)}, u32[]{:S(2)}, u32[]{:S(2)}) async-start(bf16[16,384,128]{2,1,0:T(8,128)(2,1)} %pad_maximum_fusion), calls=%async_computation.4 | async-start | bytes 3145728 | tf_op jit(solution)/shard_map/all_to_all | solution.py:669
  137.0 22.0 %all-to-all-done.4.mixed_ref = bf16[16,384,128]{2,1,0:T(8,128)(2,1)S(1)} async-done(((bf16[16,384,128]{2,1,0:T(8,128)(2,1)}), bf16[16,384,128]{2,1,0:T(8,128)(2,1)S(1)}, u32[]{:S(2)}, u32[]{:S(2)}) %all-to-all-start.4) | async-done | bytes 1572896 | tf_op jit(solution)/shard_map/all_to_all | solution.py:669
  160.0 3.8 %all-to-all-start.5 = ((bf16[8,64,128]{2,1,0:T(8,128)(2,1)}), bf16[8,64,128]{2,1,0:T(8,128)(2,1)S(1)}, u32[]{:S(2)}, u32[]{:S(2)}) async-start(bf16[8,64,128]{2,1,0:T(8,128)(2,1)} %bitcast.33), calls=%async_computation.5 | async-start | bytes 262144 | tf_op jit(solution)/shard_map/all_to_all | solution.py:677
  165.2 4.8 %all-to-all-done.5 = bf16[8,64,128]{2,1,0:T(8,128)(2,1)S(1)} async-done(((bf16[8,64,128]{2,1,0:T(8,128)(2,1)}), bf16[8,64,128]{2,1,0:T(8,128)(2,1)S(1)}, u32[]{:S(2)}, u32[]{:S(2)}) %all-to-all-start.5) | async-done | bytes 131104 | tf_op jit(solution)/shard_map/all_to_all | solution.py:677
  170.6 13.3 %all-gather.12.cloned.1.call-done = bf16[4352,128]{1,0:T(8,128)(2,1)} async-done(((bf16[272,128]{1,0:T(8,128)(2,1)}), bf16[4352,128]{1,0:T(8,128)(2,1)}) %all-gather.12.cloned.1.call-update) | async-done | bytes 1114128 | tf_op jit(solution)/shard_map/all_gather | solution.py:658
  185.2 3.8 %shard_map.149 = (f32[512,128]{1,0:T(8,128)S(1)}, f32[128,512]{1,0:T(8,128)S(1)}) custom-call(s32[1]{0:T(128)} %bitcast.1.place_ref, bf16[16,64,512]{2,1,0:T(8,128)(2,1)S(1)} %all-to-all-done.1.first_ref, bf16[16,64,512]{2,1,0:T(8,128)(2,1)} %collective-permute-done.second_ref, bf16[16,64,512]{2,1,0:T(8,128)(2,1)} %collective-permute-done.2.third_ref, ...), custom_call_target="tpu_custom_call" | custom-call | tf_op jit(solution)/shard_map/pallas_call | solution.py:517
  189.0 1.9 shard_map.151
  (107 shorter events, 32.7 us)
Async XLA Ops:
  8.1 5.7 %copy-start.31 = (s32[1,16]{1,0:T(1,128)S(1)}, s32[1,16]{1,0:T(1,128)}, u32[]{:S(2)}) copy-start(s32[1,16]{1,0:T(1,128)} %param.19) | copy-start | bytes 196
  8.1 6.7 %copy-start.30 = (bf16[1,1,2,32,3200]{4,3,2,1,0:T(8,128)(2,1)S(1)}, bf16[1,1,2,32,3200]{4,3,2,1,0:T(8,128)(2,1)}, u32[]{:S(2)}) copy-start(bf16[1,1,2,32,3200]{4,3,2,1,0:T(8,128)(2,1)} %param.14) | copy-start | bytes 1228804
  9.2 6.6 %copy-start.4 = (bf16[1,128,8192]{2,1,0:T(8,128)(2,1)S(1)}, bf16[1,128,8192]{2,1,0:T(8,128)(2,1)}, u32[]{:S(2)}) copy-start(bf16[1,128,8192]{2,1,0:T(8,128)(2,1)} %param.10) | copy-start | bytes 6291460
  9.2 20.7 %all-to-all-start = ((bf16[8,8,8192]{2,1,0:T(8,128)(2,1)}), bf16[8,8,8192]{2,1,0:T(8,128)(2,1)}, u32[]{:S(2)}, u32[]{:S(2)}) async-start(bf16[8,8,8192]{2,1,0:T(8,128)(2,1)} %broadcast_in_dim.30), calls=%async_computation | async-start | bytes 2097152 | tf_op jit(solution)/shard_map/all_to_all | solution.py:587
  13.7 53.1 %all-gather.8.cloned.1.call-start = ((), (), s32[]{:S(2)}) async-start(), calls=%async_computation.6 | async-start | bytes 3686400 | tf_op jit(solution)/shard_map/all_gather | solution.py:628
  28.8 3.1 %copy-start.8 = (bf16[16,64,512]{2,1,0:T(8,128)(2,1)}, bf16[16,64,512]{2,1,0:T(8,128)(2,1)S(1)}, u32[]{:S(2)}) copy-start(bf16[16,64,512]{2,1,0:T(8,128)(2,1)S(1)} %get-tuple-element.47) | copy-start | bytes 3145732
  29.9 10.1 %copy-start.29 = (bf16[1,8192,128]{2,1,0:T(8,128)(2,1)S(1)}, bf16[1,8192,128]{2,1,0:T(8,128)(2,1)}, u32[]{:S(2)}) copy-start(bf16[1,8192,128]{2,1,0:T(8,128)(2,1)} %param.12) | copy-start | bytes 6291460
  31.9 27.6 %all-to-all-start.1 = ((bf16[16,64,512]{2,1,0:T(8,128)(2,1)}), bf16[16,64,512]{2,1,0:T(8,128)(2,1)S(1)}, u32[]{:S(2)}, u32[]{:S(2)}) async-start(bf16[16,64,512]{2,1,0:T(8,128)(2,1)} %copy-done.8), calls=%async_computation.1 | async-start | bytes 2097152 | tf_op jit(solution)/shard_map/all_to_all | solution.py:627
  40.0 2.0 copy-start.28
  59.5 36.1 %all-to-all-start.2 = ((bf16[16,352,128]{2,1,0:T(8,128)(2,1)}), bf16[16,352,128]{2,1,0:T(8,128)(2,1)S(1)}, u32[]{:S(2)}, u32[]{:S(2)}) async-start(bf16[16,352,128]{2,1,0:T(8,128)(2,1)} %shard_map.146), calls=%async_computation.2 | async-start | bytes 2883584 | tf_op jit(solution)/shard_map/all_to_all | solution.py:641
  66.7 69.0 %all-gather.10.cloned.1.call-start = ((), (), s32[]{:S(2)}) async-start(), calls=%async_computation.7 | async-start | bytes 2359296 | tf_op jit(solution)/shard_map/all_gather | solution.py:630
  93.5 1.3 copy-start.5
  95.6 3.3 %collective-permute-start.1 = (bf16[16,352,128]{2,1,0:T(8,128)(2,1)S(1)}, bf16[16,352,128]{2,1,0:T(8,128)(2,1)S(1)}, u32[]{:S(2)}, u32[]{:S(2)}) collective-permute-start(bf16[16,352,128]{2,1,0:T(8,128)(2,1)S(1)} %all-to-all-done.2.own_ref), channel_id=1, source_target_pairs={{0,16},{16,0},{32,48},{48,32},{64,80},{80,64},{96,112},{112,96},{1... | collective-permute-start | bytes 4325384 | tf_op jit(solution)/shard_map/ppermute | solution.py:649
  96.1 34.5 %collective-permute-start.2 = (bf16[16,64,512]{2,1,0:T(8,128)(2,1)S(1)}, bf16[16,64,512]{2,1,0:T(8,128)(2,1)}, u32[]{:S(2)}, u32[]{:S(2)}) collective-permute-start(bf16[16,64,512]{2,1,0:T(8,128)(2,1)S(1)} %all-to-all-done.1.first_ref), channel_id=1, source_target_pairs={{0,32},{16,48},{32,0},{48,16},{64,96},{80,112},{96,64},{112,80},{1... | collective-permute-start | bytes 3145736 | tf_op jit(solution)/shard_map/ppermute | solution.py:651
  110.3 7.5 %copy-start.2 = (f32[10,128,128]{2,1,0:T(8,128)S(1)}, f32[10,128,128]{2,1,0:T(8,128)}, u32[]{:S(2)}) copy-start(f32[10,128,128]{2,1,0:T(8,128)} %copy-done) | copy-start | bytes 1966084
  110.3 20.1 %all-to-all-start.3 = ((bf16[16,144,128]{2,1,0:T(8,128)(2,1)}), bf16[16,144,128]{2,1,0:T(8,128)(2,1)S(1)}, u32[]{:S(2)}, u32[]{:S(2)}) async-start(bf16[16,144,128]{2,1,0:T(8,128)(2,1)} %bitcast.65), calls=%async_computation.3 | async-start | bytes 1179648 | tf_op jit(solution)/shard_map/all_to_all | solution.py:656
  117.8 1.5 copy-start.6
  131.9 27.1 %all-to-all-start.4 = ((bf16[16,384,128]{2,1,0:T(8,128)(2,1)}), bf16[16,384,128]{2,1,0:T(8,128)(2,1)S(1)}, u32[]{:S(2)}, u32[]{:S(2)}) async-start(bf16[16,384,128]{2,1,0:T(8,128)(2,1)} %pad_maximum_fusion), calls=%async_computation.4 | async-start | bytes 3145728 | tf_op jit(solution)/shard_map/all_to_all | solution.py:669
  135.6 48.3 %all-gather.12.cloned.1.call-start = ((), (), s32[]{:S(2)}) async-start(), calls=%async_computation.8 | async-start | bytes 1183744 | tf_op jit(solution)/shard_map/all_gather | solution.py:658
  136.4 34.2 %collective-permute-start = (bf16[16,64,512]{2,1,0:T(8,128)(2,1)S(1)}, bf16[16,64,512]{2,1,0:T(8,128)(2,1)}, u32[]{:S(2)}, u32[]{:S(2)}) collective-permute-start(bf16[16,64,512]{2,1,0:T(8,128)(2,1)S(1)} %all-to-all-done.1.first_ref), channel_id=1, source_target_pairs={{0,16},{16,0},{32,48},{48,32},{64,80},{80,64},{96,112},{112,96},{1... | collective-permute-start | bytes 3145736 | tf_op jit(solution)/shard_map/ppermute | solution.py:680
  136.5 34.1 %collective-permute-start.3 = (bf16[16,64,512]{2,1,0:T(8,128)(2,1)}, bf16[16,64,512]{2,1,0:T(8,128)(2,1)}, u32[]{:S(2)}, u32[]{:S(2)}) collective-permute-start(bf16[16,64,512]{2,1,0:T(8,128)(2,1)} %collective-permute-done.2.third_ref), channel_id=1, source_target_pairs={{0,16},{16,0},{32,48},{48,32},{64,80},{80,64},{96,112},{112,96},{1... | collective-permute-start | bytes 3145736 | tf_op jit(solution)/shard_map/ppermute | solution.py:681
  160.0 10.0 %all-to-all-start.5 = ((bf16[8,64,128]{2,1,0:T(8,128)(2,1)}), bf16[8,64,128]{2,1,0:T(8,128)(2,1)S(1)}, u32[]{:S(2)}, u32[]{:S(2)}) async-start(bf16[8,64,128]{2,1,0:T(8,128)(2,1)} %bitcast.33), calls=%async_computation.5 | async-start | bytes 262144 | tf_op jit(solution)/shard_map/all_to_all | solution.py:677
  185.2 3.8 %copy-start.3 = (bf16[8192,128]{1,0:T(8,128)(2,1)S(1)}, bf16[8192,128]{1,0:T(8,128)(2,1)}, u32[]{:S(2)}) copy-start(bf16[8192,128]{1,0:T(8,128)(2,1)} %all-gather.10.cloned.1.call-done) | copy-start | bytes 6291460
  185.2 3.8 %copy-start.18 = (bf16[128,512]{1,0:T(8,128)(2,1)S(1)}, bf16[128,512]{1,0:T(8,128)(2,1)}, u32[]{:S(2)}) copy-start(bf16[128,512]{1,0:T(8,128)(2,1)} %copy-done.17) | copy-start | bytes 393220
  (21 other events, 17.9 us)
Sparse Core Ops, SparseCore 0:
  32.0 32.2 all-gather.7
  69.9 26.0 all-gather.9
  138.7 45.2 all-gather.11

commit v5 on v4

--- a/solution.py
+++ b/solution.py
@@ -57,9 +57,9 @@
 def text_kernel(
     part, share, few, steps,
     place_ref, keep_ref, text_ref, cot_ref, down_ref, up_ref, out_ref,
-    cols_ref, proj_ref, image_ref, norm_ref, gram_ref,
+    cols_ref, proj_ref, base_ref,
     pick_ref, block_ref, slice_ref, out_slice_ref,
-    proj, image, gram,
+    proj, image, gram, norm,
 ):
     step = pl.program_id(0)
     sec, grp = place_ref[0], place_ref[1]
@@ -69,12 +69,12 @@
         proj[...] = jnp.zeros_like(proj)
         image[...] = jnp.zeros_like(image)
         gram[...] = jnp.zeros_like(gram)
-        norm_ref[...] = jnp.zeros_like(norm_ref)
+        norm[...] = jnp.zeros_like(norm)
 
     text32 = text_ref[...].astype(F32) * keep_ref[...]
     text = text32.astype(BF)
     cot = cot_ref[...]
-    norm_ref[...] += jnp.sum(text32 * text32, axis=1, keepdims=True)
+    norm[...] += jnp.sum(text32 * text32, axis=1, keepdims=True)
     proj[:RANK] += dot_nn(text, down_ref[...])
     proj[RANK:2 * RANK] += dot_nt(text, up_ref[...])
     proj[2 * RANK:] += dot_nt(cot, up_ref[...])
@@ -113,9 +113,11 @@
 
     @pl.when(step == steps - 1)
     def _():
-        proj_ref[...] = proj[...].astype(BF)
-        image_ref[...] = image[...]
-        gram_ref[...] = gram[...].astype(BF)
+        proj_ref[:3 * RANK, :] = proj[...].astype(BF)
+        proj_ref[3 * RANK:, :] = jnp.zeros((RANK, RANK), BF)
+        base_ref[0] = image[...]
+        base_ref[1] = gram[...]
+        base_ref[2] = jnp.broadcast_to(norm[...], (RANK, RANK))
 
 
 def text_products(sec, grp, keep, text, cot, down, up, out, sections, groups):
@@ -127,7 +129,6 @@
     few = wide // groups
     part = rows // 4
     across = pl.BlockSpec((rows, wide), lambda i: (0, i))
-    fixed = pl.BlockSpec((rows, RANK), lambda i: (0, 0))
     column = pl.BlockSpec((rows, 1), lambda i: (0, 0))
     return pl.pallas_call(
         functools.partial(text_kernel, part, share, few, steps),
@@ -143,10 +144,8 @@
         ],
         out_specs=[
             pl.BlockSpec((pieces, 2 * part, share), lambda i: (i, 0, 0)),
-            pl.BlockSpec((3 * RANK, RANK), lambda i: (0, 0)),
-            fixed,
-            column,
-            fixed,
+            pl.BlockSpec((4 * RANK, RANK), lambda i: (0, 0)),
+            pl.BlockSpec((3, RANK, RANK), lambda i: (0, 0, 0)),
             pl.BlockSpec((1, 2, few, RANK), lambda i: (i, 0, 0, 0)),
             pl.BlockSpec((2, rows, wide), lambda i: (0, 0, 0)),
             pl.BlockSpec((2 * share, RANK), lambda i: (0, 0)),
@@ -154,10 +153,8 @@
         ],
         out_shape=[
             jax.ShapeDtypeStruct((groups, 2 * part, share), BF),
-            jax.ShapeDtypeStruct((3 * RANK, RANK), BF),
-            jax.ShapeDtypeStruct((rows, RANK), F32),
-            jax.ShapeDtypeStruct((rows, 1), F32),
-            jax.ShapeDtypeStruct((RANK, RANK), BF),
+            jax.ShapeDtypeStruct((4 * RANK, RANK), BF),
+            jax.ShapeDtypeStruct((3, RANK, RANK), F32),
             jax.ShapeDtypeStruct((steps, 2, few, RANK), BF),
             jax.ShapeDtypeStruct((2, rows, wide), BF),
             jax.ShapeDtypeStruct((2 * share, RANK), BF),
@@ -167,6 +164,7 @@
             pltpu.VMEM((3 * RANK, RANK), F32),
             pltpu.VMEM((rows, RANK), F32),
             pltpu.VMEM((RANK, RANK), F32),
+            pltpu.VMEM((rows, 1), F32),
         ],
         compiler_params=PARAMS,
     )(scalars(sec, grp), keep, text, cot, down, up, out)
@@ -182,7 +180,7 @@
 def front_kernel(
     sections, windows, in_windows,
     place_ref, image_ref, down_ref, up_ref, in_ref,
-    state_ref, wide_ref, in_window_ref,
+    state_ref, pre_ref, wide_ref, in_window_ref,
     normed_buf, out_buf,
 ):
     sec = place_ref[0]
@@ -215,6 +213,7 @@
     for k in range(4):
         proj = proj + dot_nn((out_buf[k].astype(F32) * scale).astype(BF), in_ref[k])
     state_ref[8] = proj
+    pre_ref[...] = proj
     state_ref[9] = jnp.broadcast_to(scale, (RANK, RANK))
     per = sections // 4
     own = pl.ds(
@@ -234,9 +233,10 @@
     return pl.pallas_call(
         functools.partial(front_kernel, sections, windows, in_windows),
         in_specs=[SMEM] + [VMEM] * 4,
-        out_specs=[VMEM] * 3,
+        out_specs=[VMEM] * 4,
         out_shape=[
             jax.ShapeDtypeStruct((10, RANK, RANK), F32),
+            jax.ShapeDtypeStruct((RANK, RANK), F32),
             jax.ShapeDtypeStruct((RANK, total), BF),
             jax.ShapeDtypeStruct((4 * span, RANK), BF),
         ],
@@ -282,7 +282,7 @@
 
 def rank_kernel(
     layers, width,
-    place_ref, own_ref, other_ref, gath_ref, state_ref, cot_ref, norm_ref, image_gram_ref, sel_ref,
+    place_ref, own_ref, other_ref, gath_ref, proj_pre_ref, base_ref, sel_ref,
     coef_ref, factor_ref, image_ref,
     weight, acts, act_cat, grads, scaled, back, pre_ref, slope_ref, inner_ref, scale_ref, sums_ref,
 ):
@@ -301,14 +301,14 @@
             weight[l, rows, rank:] = tile[:, 8:, :].reshape(rank, rank).astype(BF)
             at += 16
 
-    proj_pre = state_ref[8]
+    proj_pre = proj_pre_ref[...]
     sel = sel_ref[...]
     placed = dot_nn(sel, gelu_tanh(proj_pre).astype(BF))
     placed_half = placed.astype(BF)
     acts[0] = placed_half
     act_cat[:, :rank] = placed_half
-    image_inner = dot_nn(placed_half, image_gram_ref[...])
-    total = norm_ref[...] + jnp.sum(placed * image_inner, axis=1, keepdims=True)
+    image_inner = dot_nn(placed_half, base_ref[1].astype(BF))
+    total = base_ref[2][:, :1] + jnp.sum(placed * image_inner, axis=1, keepdims=True)
     for l in range(layers):
         here = (l + 1) * rank
         scale = lax.rsqrt(jnp.maximum(total, 0.0) * (1.0 / width) + EPS)
@@ -342,7 +342,7 @@
         pair = jnp.concatenate([grad, -part], axis=1)
         back[:, :here] += dot_nt(pair, weight[l, :here, :])
         sums = sums + scale * scale * mean
-    d_image = cot_ref[...] - sums * image_inner + back[:, :rank]
+    d_image = base_ref[0] - sums * image_inner + back[:, :rank]
     scaled[0] = (sums * placed).astype(BF)
     d_slot = dot_tn(sel, d_image.astype(BF))
     image_ref[0] = (d_slot * gelu_slope(proj_pre)).astype(BF)
@@ -368,11 +368,11 @@
         coef_ref[layers + 1 + l] = dot_tn(left, right).astype(BF)
 
 
-def rank_space(position, core, gram, other, gath, state, cot, norms, image_gram, sel, width):
+def rank_space(position, core, gram, other, gath, proj_pre, base, sel, width):
     layers = gath.shape[0]
     rank = RANK
     tall = (layers + 1) * rank
-    operands = (gram, other, gath, state, cot, norms, image_gram, sel)
+    operands = (gram, other, gath, proj_pre, base, sel)
 
     def whole(shape):
         return pl.BlockSpec(shape, lambda i: (0,) * len(shape))
@@ -397,7 +397,7 @@
             pltpu.VMEM((layers, rank, 1), F32),
             pltpu.VMEM((layers, rank, 1), F32),
         ],
-        compiler_params=PARAMS,
+        compiler_params=pltpu.CompilerParams(vmem_limit_bytes=60 * 1024 * 1024),
     )(scalars(position, core), *operands)
 
 
@@ -605,7 +605,9 @@
     piece = rank // groups
     swap = [(at, at ^ 1) for at in range(sections)]
 
-    up_rows = spread(lax.dynamic_slice_in_dim(weight_up, grp * piece, piece, 0), "section")
+    own_rows = lax.dynamic_slice_in_dim(weight_up, grp * piece, piece, 0)
+    own_rows, frames = lax.optimization_barrier((own_rows, frames))
+    up_rows = spread(own_rows, "section")
 
     slot_row = jnp.repeat(frames, tokens)[None, :]
     row = jnp.arange(rows_total, dtype=jnp.int32)[:, None]
@@ -613,18 +615,18 @@
     sel = (slot_row == row // tokens) & (row % tokens == column % tokens)
     keep = 1.0 - jnp.any(sel, axis=1, keepdims=True).astype(F32)
     sel = sel.astype(BF)
-    cols, proj, cot_image, text_norm, image_gram, picks, blocks, own_slices, out_slice = (
+    cols, proj, base, picks, blocks, own_slices, out_slice = (
         text_products(
             sec, grp, keep, text, cot, weight_down, weight_up, proj_out, sections, groups
         )
     )
+    gath = lax.all_gather(proj, "section", axis=0)
     own_images = images[0, 0].reshape(slot_count * tokens, 4, enc_width).transpose(1, 0, 2)
 
     image_rows = lax.dynamic_slice_in_dim(proj_out, grp * piece, piece, 0)
-    up_rows, cols, own_images, image_rows = lax.optimization_barrier(
-        (up_rows, cols, own_images, image_rows)
-    )
+    up_rows, cols, image_rows = lax.optimization_barrier((up_rows, cols, image_rows))
     cols = lax.all_to_all(cols, "dp", 0, 0)
+    gath, own_images = lax.optimization_barrier((gath, own_images))
     group_images = lax.all_gather(own_images, "section", axis=0)
     own_slices, group_images = lax.optimization_barrier((own_slices, group_images))
     slices = lax.all_gather(own_slices, "section", axis=0)
@@ -637,24 +639,25 @@
         axis=1,
     ).astype(BF).reshape(-1, rank)
     packed = pack_gram(core, lax.all_gather(gram, "section", axis=0), groups)
-    packed, cols, proj = lax.optimization_barrier((packed, cols, proj))
+    packed, cols = lax.optimization_barrier((packed, cols))
     own_gram = lax.all_to_all(packed, "dp", 0, 0)
 
-    gath = lax.all_gather(proj, "section", axis=0)
     quarters = proj_in.reshape(4, enc_width, rank)
-    state, wide, in_window = encoder_front(sec, group_images, enc_down, enc_up, quarters)
-    own_gram, gath, state, wide, in_window, cols = lax.optimization_barrier(
-        (own_gram, gath, state, wide, in_window, cols)
+    state, proj_pre, wide, in_window = encoder_front(
+        sec, group_images, enc_down, enc_up, quarters
+    )
+    own_gram, gath, state, proj_pre, wide, in_window, cols = lax.optimization_barrier(
+        (own_gram, gath, state, proj_pre, wide, in_window, cols)
     )
     other_gram = lax.ppermute(own_gram, "section", swap)
     far = [(at, at ^ 2) for at in range(sections)]
     far_cols = lax.ppermute(cols, "section", far)
 
+    gath, slices = lax.optimization_barrier((gath, slices))
     coef, factor, image = rank_space(
-        sec, core, own_gram, other_gram, gath, state, cot_image, text_norm, image_gram, sel, width
+        sec, core, own_gram, other_gram, gath, proj_pre, base, sel, width
     )
     coef = lax.all_to_all(coef.reshape(groups, -1, rank), "dp", 0, 0)
-    factor, slices = lax.optimization_barrier((factor, slices))
     factors = lax.all_gather(factor, "dp", axis=0)
 
     parts, (n_enc, n_in, pad_enc, pad_in) = encoder_late(

time: 199 us -> 231 us (1.16)
  waiting for transfers between devices: 49.1 us -> 110 us
  blocking collectives: 27.7 us -> 12.9 us
  local copies, waits for them, and re-layouts: 28.1 us -> 20 us
  starting transfers between devices: 37.3 us -> 29.6 us
    all_gather x0 -> x1, waiting for transfers between devices: none -> 25.8 us  [shards(): gath = lax.all_gather(proj, 'section', axis=0)]
    all_to_all x1, waiting for transfers between devices: 0.01 us -> 21.3 us  [spread(): lax.all_to_all(jnp.broadcast_to(value[None], (count,) + value.shape), axi...]
    all_gather x1 -> x0, blocking collectives: 13.6 us -> none  [shards(): gath = lax.all_gather(proj, 'section', axis=0)]
    all_to_all x1, waiting for transfers between devices: 0.01 us -> 11.9 us  [shards(): own_gram = lax.all_to_all(packed, 'dp', 0, 0)]
    unnamed x64 -> x46, local copies, waits for them, and re-layouts: 20.6 us -> 13.9 us
    all_gather x1, waiting for transfers between devices: 13.3 us -> 18.1 us  [shards(): factors = lax.all_gather(factor, 'dp', axis=0)]
    all_to_all x1, waiting for transfers between devices: 4.76 us -> 0.01 us  [shards(): lax.all_to_all(term.astype(BF).reshape(sections, few, rank), 'section', 0...]
    all_to_all x1, starting transfers between devices: 7.38 us -> 3.73 us  [shards(): coef = lax.all_to_all(coef.reshape(groups, -1, rank), 'dp', 0, 0)]
  transfers between devices with their start and end apart: 13 -> 14, of which waited for: 5 -> 8; matrix products, arithmetic and copies ran while one was open for 6% -> 4% of each run, Pallas kernels for 14% -> 11%
where the time goes in v5:
time: 231 us; the launch traced here: 229 us
  waiting for transfers between devices  110 us (48%)
  Pallas kernels  35.3 us (15%)
  starting transfers between devices  29.6 us (13%)
  local copies, waits for them, and re-layouts  20 us (9%)
  between operations  14.1 us (6%)
  blocking collectives  12.9 us (6%)
  matrix products  4.17 us (2%)
  other arithmetic  3.67 us (2%)
    all_gather x1, waiting for transfers between devices, shards(): gath = lax.all_gather(proj, 'section', axis=0)  25.8 us
    all_to_all x1, waiting for transfers between devices, shards(): mixed = lax.all_to_all(mixed, 'dp', 0, 0)  22.2 us
    all_to_all x1, waiting for transfers between devices, spread(): lax.all_to_all(jnp.broadcast_to(value[None], (count,) + value.shape), axi...  21.3 us
    all_gather x1, waiting for transfers between devices, shards(): factors = lax.all_gather(factor, 'dp', axis=0)  18.1 us
    unnamed x46, local copies, waits for them, and re-layouts  13.9 us
    all_gather x1, blocking collectives, shards(): packed = pack_gram(core, lax.all_gather(gram, 'section', axis=0), groups)  12.9 us
    all_to_all x1, waiting for transfers between devices, shards(): own_gram = lax.all_to_all(packed, 'dp', 0, 0)  11.9 us
    pallas_call x1, Pallas kernels, text_products(): pl.pallas_call(functools.partial(text_kernel, part, share, few, steps), g...  9.41 us
  transfers between devices with their start and end apart: 14, of which 8 were waited for; matrix products, arithmetic and copies ran while one was open for 4% of the time, Pallas kernels for 11%

profile of v5, /device:TPU:0, one launch (start us, length us, event | category | flops | bytes accessed | tf_op | source)
XLA Modules:
  0.0 229.5 jit_solution(18263624621826534951)
XLA Ops:
  9.9 1.6 copy-done.1
  11.5 9.4 %shard_map.145 = (bf16[16,64,512]{2,1,0:T(8,128)(2,1)}, bf16[512,128]{1,0:T(8,128)(2,1)}, f32[3,128,128]{2,1,0:T(8,128)S(1)}, bf16[8,2,64,128]{3,2,1,0:T(8,128)(...) custom-call(s32[2]{0:T(128)S(1)} %pad_add_fusion.place_ref, ...), custom_call_target="tpu_custom_call" | custom-call | tf_op jit(solution)/shard_map/pallas_call | solution.py:133
  23.9 25.8 %all-gather.9.cloned.1.call-done = bf16[4096,128]{1,0:T(8,128)(2,1)} async-done(((bf16[512,128]{1,0:T(8,128)(2,1)}), bf16[4096,128]{1,0:T(8,128)(2,1)}) %all-gather.9.cloned.1.call-update) | async-done | bytes 1048592 | tf_op jit(solution)/shard_map/all_gather | solution.py:623
  51.6 3.6 %all-to-all-start = ((bf16[8,8,8192]{2,1,0:T(8,128)(2,1)}), bf16[8,8,8192]{2,1,0:T(8,128)(2,1)S(1)}, u32[]{:S(2)}, u32[]{:S(2)}) async-start(bf16[8,8,8192]{2,1,0:T(8,128)(2,1)} %broadcast_in_dim.12), calls=%async_computation | async-start | bytes 2097152 | tf_op jit(solution)/shard_map/all_to_all | solution.py:587
  56.1 21.3 %all-to-all-done = bf16[8,8,8192]{2,1,0:T(8,128)(2,1)S(1)} async-done(((bf16[8,8,8192]{2,1,0:T(8,128)(2,1)}), bf16[8,8,8192]{2,1,0:T(8,128)(2,1)S(1)}, u32[]{:S(2)}, u32[]{:S(2)}) %all-to-all-start) | async-done | bytes 1048608 | tf_op jit(solution)/shard_map/all_to_all | solution.py:587
  77.4 7.0 %all-to-all-start.1 = ((bf16[16,64,512]{2,1,0:T(8,128)(2,1)}), bf16[16,64,512]{2,1,0:T(8,128)(2,1)S(1)}, u32[]{:S(2)}, u32[]{:S(2)}) async-start(bf16[16,64,512]{2,1,0:T(8,128)(2,1)} %get-tuple-element.51), calls=%async_computation.1 | async-start | bytes 2097152 | tf_op jit(solution)/shard_map/all_to_all | solution.py:628
  85.7 2.3 %fusion.14 = bf16[9,1,8,128]{3,2,0,1:T(8,128)(2,1)S(1)} fusion(bf16[1,8192,128]{2,1,0:T(8,128)(2,1)} %param.12, bf16[8,8,8192]{2,1,0:T(8,128)(2,1)S(1)} %all-to-all-done, bf16[1,8,8192]{2,1,0:T(8,128)(2,1)S(1)} %bitcast.70), kind=kOutput, calls=%fused_computation.12 | convolution fusion | flops 151593984 | bytes 3295232 | tf_op jit(solution)/shard_map/dot_general | solution.py:32
  88.8 12.9 %all_gather.27.gram_ref = bf16[8,144,128]{2,1,0:T(8,128)(2,1)S(1)} all-gather(bf16[1,144,128]{2,1,0:T(8,128)(2,1)S(1)} %bitcast.76), channel_id=1, replica_groups=mesh['section'=8,'dp'=16] {'section'}, dimensions={0}, use_global_device_ids=true | all-gather | bytes 331776 | tf_op jit(solution)/shard_map/all_gather | solution.py:641
  101.7 1.4 shard_map.146
  103.1 7.2 %all-to-all-start.2 = ((bf16[16,352,128]{2,1,0:T(8,128)(2,1)}), bf16[16,352,128]{2,1,0:T(8,128)(2,1)}, u32[]{:S(2)}, u32[]{:S(2)}) async-start(bf16[16,352,128]{2,1,0:T(8,128)(2,1)} %shard_map.146), calls=%async_computation.2 | async-start | bytes 2883584 | tf_op jit(solution)/shard_map/all_to_all | solution.py:643
  110.3 9.3 %shard_map.147 = (f32[10,128,128]{2,1,0:T(8,128)S(1)}, f32[128,128]{1,0:T(8,128)S(1)}, bf16[128,6784]{1,0:T(8,128)(2,1)S(1)}, bf16[2048,128]{1,0:T(8,128)(2,1)S(1)}) custom-call(s32[1]{0:T(128)} %bitcast.place_ref, bf16[8,4,16,3200]{3,2,1,0:T(8,128)(2,1)} %bitcast.67, bf16[3200,128]{1,0:T(8,128)(2,1)S(1)} %copy-done.5, bf16[128,3200]{1,0:T(8,128)(2,1)S(1)} %copy-done.6, ...), custom_call_target="tpu_custom_call" | custom-call | tf_op jit(solution)/shard_map/pallas_call | solution.py:233
  122.3 11.9 %all-to-all-done.2.own_ref = bf16[16,352,128]{2,1,0:T(8,128)(2,1)} async-done(((bf16[16,352,128]{2,1,0:T(8,128)(2,1)}), bf16[16,352,128]{2,1,0:T(8,128)(2,1)}, u32[]{:S(2)}, u32[]{:S(2)}) %all-to-all-start.2) | async-done | bytes 1441824 | tf_op jit(solution)/shard_map/all_to_all | solution.py:643
  135.0 2.6 %collective-permute-done.1.other_ref = bf16[16,352,128]{2,1,0:T(8,128)(2,1)S(1)} collective-permute-done((bf16[16,352,128]{2,1,0:T(8,128)(2,1)}, bf16[16,352,128]{2,1,0:T(8,128)(2,1)S(1)}, u32[]{:S(2)}, u32[]{:S(2)}) %collective-permute-start.1) | collective-permute-done | bytes 1441824 | tf_op jit(solution)/shard_map/ppermute | solution.py:652
  138.7 7.5 %shard_map.148 = (bf16[18,128,128]{2,1,0:T(8,128)(2,1)}, bf16[272,128]{1,0:T(8,128)(2,1)}, bf16[3,128,128]{2,1,0:T(8,128)(2,1)}) custom-call(s32[2]{0:T(128)} %pad_add_fusion.1.place_ref, bf16[16,352,128]{2,1,0:T(8,128)(2,1)} %all-to-all-done.2.own_ref, bf16[16,352,128]{2,1,0:T(8,128)(2,1)} %copy-done.21, bf16[8,512,128]{2,1,0:T(8,128)(2,1)} %bitcast.72, ...), custom_call_target="tpu_custom_call" | custom-call | tf_op jit(solution)/shard_map/pallas_call | solution.py:381
  146.2 3.7 %all-to-all-start.3 = ((bf16[16,144,128]{2,1,0:T(8,128)(2,1)}), bf16[16,144,128]{2,1,0:T(8,128)(2,1)S(1)}, u32[]{:S(2)}, u32[]{:S(2)}) async-start(bf16[16,144,128]{2,1,0:T(8,128)(2,1)} %bitcast.73), calls=%async_computation.3 | async-start | bytes 1179648 | tf_op jit(solution)/shard_map/all_to_all | solution.py:660
  150.0 1.5 copy-done.3
  154.5 1.9 shard_map.150
  156.4 6.3 %all-to-all-done.3 = bf16[16,144,128]{2,1,0:T(8,128)(2,1)S(1)} async-done(((bf16[16,144,128]{2,1,0:T(8,128)(2,1)}), bf16[16,144,128]{2,1,0:T(8,128)(2,1)S(1)}, u32[]{:S(2)}, u32[]{:S(2)}) %all-to-all-start.3) | async-done | bytes 589856 | tf_op jit(solution)/shard_map/all_to_all | solution.py:660
  164.2 3.8 %all-to-all-start.4 = ((bf16[16,384,128]{2,1,0:T(8,128)(2,1)}), bf16[16,384,128]{2,1,0:T(8,128)(2,1)S(1)}, u32[]{:S(2)}, u32[]{:S(2)}) async-start(bf16[16,384,128]{2,1,0:T(8,128)(2,1)} %pad_maximum_fusion), calls=%async_computation.4 | async-start | bytes 3145728 | tf_op jit(solution)/shard_map/all_to_all | solution.py:672
  169.3 22.2 %all-to-all-done.4.mixed_ref = bf16[16,384,128]{2,1,0:T(8,128)(2,1)S(1)} async-done(((bf16[16,384,128]{2,1,0:T(8,128)(2,1)}), bf16[16,384,128]{2,1,0:T(8,128)(2,1)S(1)}, u32[]{:S(2)}, u32[]{:S(2)}) %all-to-all-start.4) | async-done | bytes 1572896 | tf_op jit(solution)/shard_map/all_to_all | solution.py:672
  192.5 3.4 %all-to-all-start.5 = ((bf16[8,64,128]{2,1,0:T(8,128)(2,1)}), bf16[8,64,128]{2,1,0:T(8,128)(2,1)S(1)}, u32[]{:S(2)}, u32[]{:S(2)}) async-start(bf16[8,64,128]{2,1,0:T(8,128)(2,1)} %bitcast.33), calls=%async_computation.5 | async-start | bytes 262144 | tf_op jit(solution)/shard_map/all_to_all | solution.py:680
  197.2 18.1 %all-gather.15.cloned.1.call-done = bf16[4352,128]{1,0:T(8,128)(2,1)} async-done(((bf16[272,128]{1,0:T(8,128)(2,1)}), bf16[4352,128]{1,0:T(8,128)(2,1)}) %all-gather.15.cloned.1.call-update) | async-done | bytes 1114128 | tf_op jit(solution)/shard_map/all_gather | solution.py:661
  216.6 3.8 %shard_map.149 = (f32[512,128]{1,0:T(8,128)S(1)}, f32[128,512]{1,0:T(8,128)S(1)}) custom-call(s32[1]{0:T(128)} %bitcast.1.place_ref, bf16[16,64,512]{2,1,0:T(8,128)(2,1)S(1)} %all-to-all-done.1.first_ref, bf16[16,64,512]{2,1,0:T(8,128)(2,1)} %collective-permute-done.second_ref, bf16[16,64,512]{2,1,0:T(8,128)(2,1)} %collective-permute-done.2.third_ref, ...), custom_call_target="tpu_custom_call" | custom-call | tf_op jit(solution)/shard_map/pallas_call | solution.py:517
  220.4 1.9 shard_map.151
  (91 shorter events, 25.2 us)
Async XLA Ops:
  7.2 42.5 %all-gather.9.cloned.1.call-start = ((), (), s32[]{:S(2)}) async-start(), calls=%async_computation.6 | async-start | bytes 1179648 | tf_op jit(solution)/shard_map/all_gather | solution.py:623
  9.9 1.6 copy-start.1
  11.5 12.3 %copy-start.22 = (bf16[1,1,2,32,3200]{4,3,2,1,0:T(8,128)(2,1)S(1)}, bf16[1,1,2,32,3200]{4,3,2,1,0:T(8,128)(2,1)}, u32[]{:S(2)}) copy-start(bf16[1,1,2,32,3200]{4,3,2,1,0:T(8,128)(2,1)} %param.14) | copy-start | bytes 1228804
  23.8 61.8 %all-gather.11.cloned.1.call-start = ((), (), s32[]{:S(2)}) async-start(), calls=%async_computation.7 | async-start | bytes 3686400 | tf_op jit(solution)/shard_map/all_gather | solution.py:630
  51.6 25.8 %all-to-all-start = ((bf16[8,8,8192]{2,1,0:T(8,128)(2,1)}), bf16[8,8,8192]{2,1,0:T(8,128)(2,1)S(1)}, u32[]{:S(2)}, u32[]{:S(2)}) async-start(bf16[8,8,8192]{2,1,0:T(8,128)(2,1)} %broadcast_in_dim.12), calls=%async_computation | async-start | bytes 2097152 | tf_op jit(solution)/shard_map/all_to_all | solution.py:587
  77.4 25.7 %all-to-all-start.1 = ((bf16[16,64,512]{2,1,0:T(8,128)(2,1)}), bf16[16,64,512]{2,1,0:T(8,128)(2,1)S(1)}, u32[]{:S(2)}, u32[]{:S(2)}) async-start(bf16[16,64,512]{2,1,0:T(8,128)(2,1)} %get-tuple-element.51), calls=%async_computation.1 | async-start | bytes 2097152 | tf_op jit(solution)/shard_map/all_to_all | solution.py:628
  84.4 50.5 %all-gather.13.cloned.1.call-start = ((), (), s32[]{:S(2)}) async-start(), calls=%async_computation.8 | async-start | bytes 2359296 | tf_op jit(solution)/shard_map/all_gather | solution.py:632
  85.6 2.3 %copy-start.20 = (bf16[1,128,8192]{2,1,0:T(8,128)(2,1)S(1)}, bf16[1,128,8192]{2,1,0:T(8,128)(2,1)}, u32[]{:S(2)}) copy-start(bf16[1,128,8192]{2,1,0:T(8,128)(2,1)} %param.13) | copy-start | bytes 6291460
  103.1 7.2 %copy-start.5 = (bf16[3200,128]{1,0:T(8,128)(2,1)S(1)}, bf16[3200,128]{1,0:T(8,128)(2,1)}, u32[]{:S(2)}) copy-start(bf16[3200,128]{1,0:T(8,128)(2,1)} %down_ref.1) | copy-start | bytes 2457604
  103.1 7.2 %copy-start.6 = (bf16[128,3200]{1,0:T(8,128)(2,1)S(1)}, bf16[128,3200]{1,0:T(8,128)(2,1)}, u32[]{:S(2)}) copy-start(bf16[128,3200]{1,0:T(8,128)(2,1)} %up_ref.1) | copy-start | bytes 2457604
  103.1 31.0 %all-to-all-start.2 = ((bf16[16,352,128]{2,1,0:T(8,128)(2,1)}), bf16[16,352,128]{2,1,0:T(8,128)(2,1)}, u32[]{:S(2)}, u32[]{:S(2)}) async-start(bf16[16,352,128]{2,1,0:T(8,128)(2,1)} %shard_map.146), calls=%async_computation.2 | async-start | bytes 2883584 | tf_op jit(solution)/shard_map/all_to_all | solution.py:643
  122.3 23.9 %copy-start.7 = (f32[10,128,128]{2,1,0:T(8,128)}, f32[10,128,128]{2,1,0:T(8,128)S(1)}, u32[]{:S(2)}) copy-start(f32[10,128,128]{2,1,0:T(8,128)S(1)} %get-tuple-element.77.state_ref) | copy-start | bytes 1966084
  134.2 3.4 %collective-permute-start.1 = (bf16[16,352,128]{2,1,0:T(8,128)(2,1)}, bf16[16,352,128]{2,1,0:T(8,128)(2,1)S(1)}, u32[]{:S(2)}, u32[]{:S(2)}) collective-permute-start(bf16[16,352,128]{2,1,0:T(8,128)(2,1)} %all-to-all-done.2.own_ref), channel_id=1, source_target_pairs={{0,16},{16,0},{32,48},{48,32},{64,80},{80,64},{96,112},{112,96},{1... | collective-permute-start | bytes 4325384 | tf_op jit(solution)/shard_map/ppermute | solution.py:652
  134.2 28.6 %collective-permute-start.2 = (bf16[16,64,512]{2,1,0:T(8,128)(2,1)S(1)}, bf16[16,64,512]{2,1,0:T(8,128)(2,1)}, u32[]{:S(2)}, u32[]{:S(2)}) collective-permute-start(bf16[16,64,512]{2,1,0:T(8,128)(2,1)S(1)} %all-to-all-done.1.first_ref), channel_id=1, source_target_pairs={{0,32},{16,48},{32,0},{48,16},{64,96},{80,112},{96,64},{112,80},{1... | collective-permute-start | bytes 3145736 | tf_op jit(solution)/shard_map/ppermute | solution.py:654
  146.2 3.8 %copy-start.8 = (f32[10,128,128]{2,1,0:T(8,128)S(1)}, f32[10,128,128]{2,1,0:T(8,128)}, u32[]{:S(2)}) copy-start(f32[10,128,128]{2,1,0:T(8,128)} %copy-done.7) | copy-start | bytes 1966084
  146.2 16.5 %all-to-all-start.3 = ((bf16[16,144,128]{2,1,0:T(8,128)(2,1)}), bf16[16,144,128]{2,1,0:T(8,128)(2,1)S(1)}, u32[]{:S(2)}, u32[]{:S(2)}) async-start(bf16[16,144,128]{2,1,0:T(8,128)(2,1)} %bitcast.73), calls=%async_computation.3 | async-start | bytes 1179648 | tf_op jit(solution)/shard_map/all_to_all | solution.py:660
  164.2 5.0 %copy-start.14 = (bf16[8,2,64,128]{3,2,1,0:T(8,128)(2,1)S(1)}, bf16[8,2,64,128]{3,2,1,0:T(8,128)(2,1)}, u32[]{:S(2)}) copy-start(bf16[8,2,64,128]{3,2,1,0:T(8,128)(2,1)} %copy-done.13) | copy-start | bytes 786436
  164.2 27.2 %all-to-all-start.4 = ((bf16[16,384,128]{2,1,0:T(8,128)(2,1)}), bf16[16,384,128]{2,1,0:T(8,128)(2,1)S(1)}, u32[]{:S(2)}, u32[]{:S(2)}) async-start(bf16[16,384,128]{2,1,0:T(8,128)(2,1)} %pad_maximum_fusion), calls=%async_computation.4 | async-start | bytes 3145728 | tf_op jit(solution)/shard_map/all_to_all | solution.py:672
  168.1 47.3 %all-gather.15.cloned.1.call-start = ((), (), s32[]{:S(2)}) async-start(), calls=%async_computation.9 | async-start | bytes 1183744 | tf_op jit(solution)/shard_map/all_gather | solution.py:661
  168.7 28.6 %collective-permute-start = (bf16[16,64,512]{2,1,0:T(8,128)(2,1)S(1)}, bf16[16,64,512]{2,1,0:T(8,128)(2,1)}, u32[]{:S(2)}, u32[]{:S(2)}) collective-permute-start(bf16[16,64,512]{2,1,0:T(8,128)(2,1)S(1)} %all-to-all-done.1.first_ref), channel_id=1, source_target_pairs={{0,16},{16,0},{32,48},{48,32},{64,80},{80,64},{96,112},{112,96},{1... | collective-permute-start | bytes 3145736 | tf_op jit(solution)/shard_map/ppermute | solution.py:683
  168.8 28.5 %collective-permute-start.3 = (bf16[16,64,512]{2,1,0:T(8,128)(2,1)}, bf16[16,64,512]{2,1,0:T(8,128)(2,1)}, u32[]{:S(2)}, u32[]{:S(2)}) collective-permute-start(bf16[16,64,512]{2,1,0:T(8,128)(2,1)} %collective-permute-done.2.third_ref), channel_id=1, source_target_pairs={{0,16},{16,0},{32,48},{48,32},{64,80},{80,64},{96,112},{112,96},{1... | collective-permute-start | bytes 3145736 | tf_op jit(solution)/shard_map/ppermute | solution.py:684
  192.5 29.8 %all-to-all-start.5 = ((bf16[8,64,128]{2,1,0:T(8,128)(2,1)}), bf16[8,64,128]{2,1,0:T(8,128)(2,1)S(1)}, u32[]{:S(2)}, u32[]{:S(2)}) async-start(bf16[8,64,128]{2,1,0:T(8,128)(2,1)} %bitcast.33), calls=%async_computation.5 | async-start | bytes 262144 | tf_op jit(solution)/shard_map/all_to_all | solution.py:680
  216.6 3.8 %copy-start = (bf16[8192,128]{1,0:T(8,128)(2,1)S(1)}, bf16[8192,128]{1,0:T(8,128)(2,1)}, u32[]{:S(2)}) copy-start(bf16[8192,128]{1,0:T(8,128)(2,1)} %all-gather.13.cloned.1.call-done) | copy-start | bytes 6291460
  216.6 3.8 %copy-start.17 = (bf16[128,512]{1,0:T(8,128)(2,1)S(1)}, bf16[128,512]{1,0:T(8,128)(2,1)}, u32[]{:S(2)}) copy-start(bf16[128,512]{1,0:T(8,128)(2,1)} %copy-done.16) | copy-start | bytes 393220
  (13 other events, 12.3 us)
Sparse Core Ops, SparseCore 0:
  23.9 25.7 all-gather.8
  51.4 34.1 all-gather.10
  87.9 24.7 all-gather.12
  170.8 44.4 all-gather.14

commit v6 on v5

--- a/solution.py
+++ b/solution.py
@@ -248,13 +248,6 @@
     )(scalars(sec), images, enc_down, enc_up, proj_in)
 
 
-def two_lanes(column):
-    high = column.astype(BF).astype(F32)
-    lane = lax.broadcasted_iota(jnp.int32, (column.shape[0], RANK), 1)
-    zero = jnp.zeros((column.shape[0], RANK), F32)
-    return jnp.where(lane == 0, high, jnp.where(lane == 1, column - high, zero))
-
-
 def pack_kernel(layers, core_ref, gram_ref, out_ref, packed):
     at = 0
     for l in range(layers):
@@ -284,7 +277,7 @@
     layers, width,
     place_ref, own_ref, other_ref, gath_ref, proj_pre_ref, base_ref, sel_ref,
     coef_ref, factor_ref, image_ref,
-    weight, acts, act_cat, grads, scaled, back, pre_ref, slope_ref, inner_ref, scale_ref, sums_ref,
+    weight, acts, act_cat, grads, scaled, back, pre_ref, slope_ref, inner_ref, scale_ref,
 ):
     rank = RANK
     own = place_ref[0]
@@ -338,7 +331,6 @@
         part = (sums * acts[l + 1].astype(F32)).astype(BF)
         grads[l] = grad
         scaled[l + 1] = part
-        sums_ref[l] = sums
         pair = jnp.concatenate([grad, -part], axis=1)
         back[:, :here] += dot_nt(pair, weight[l, :here, :])
         sums = sums + scale * scale * mean
@@ -352,9 +344,9 @@
     own_act = acts[own + 1]
     own_grad = grads[own]
     own_scaled = scaled[own + 1]
-    factor_ref[:rank, :] = own_grad
-    factor_ref[rank:2 * rank, :] = own_act
-    factor_ref[2 * rank:, :] = two_lanes(sums_ref[own]).T[:16].astype(BF)
+    factor_ref[0] = own_grad
+    factor_ref[1] = own_act
+    factor_ref[2] = own_scaled
     coef_ref[0] = dot_tn(acts[0], own_grad).astype(BF)
     for l in range(layers):
         low = l < own
@@ -377,7 +369,7 @@
     def whole(shape):
         return pl.BlockSpec(shape, lambda i: (0,) * len(shape))
 
-    outs = ((2 * layers + 2, rank, rank), (2 * rank + 16, rank), (3, rank, rank))
+    outs = ((2 * layers + 2, rank, rank), (3, rank, rank), (3, rank, rank))
     return pl.pallas_call(
         functools.partial(rank_kernel, layers, width),
         grid=(1,),
@@ -394,7 +386,6 @@
             pltpu.VMEM((layers, rank, rank), F32),
             pltpu.VMEM((layers, rank, rank), F32),
             pltpu.VMEM((layers, rank, rank), F32),
-            pltpu.VMEM((layers, rank, 1), F32),
             pltpu.VMEM((layers, rank, 1), F32),
         ],
         compiler_params=pltpu.CompilerParams(vmem_limit_bytes=60 * 1024 * 1024),
@@ -481,17 +472,9 @@
 def row_kernel(
     place_ref, first_ref, second_ref, third_ref, fourth_ref, factor_ref,
     down_ref, up_ref,
-    acts, scaled,
 ):
     groups, rows, share = first_ref.shape
     part = rows // 2
-    for at in range(groups):
-        act = factor_ref[at, RANK:2 * RANK, :]
-        weights = factor_ref[at, 2 * RANK:2 * RANK + 8, :].astype(F32)
-        weights = jnp.sum(weights, axis=0, keepdims=True)
-        weights = jnp.broadcast_to(weights, (RANK, RANK)).T
-        acts[at] = act
-        scaled[at] = (act.astype(F32) * weights).astype(BF)
 
     def flat(value):
         return value.reshape(groups * part, value.shape[-1])
@@ -505,15 +488,16 @@
         start = pl.multiple_of(which * part, part)
         text = flat(cols_ref[:, :part, :])
         cot = flat(cols_ref[:, part:, :])
-        total_down += dot_tn(text, flat(factor_ref[:, pl.ds(start, part), :]))
-        total_up += dot_tn(flat(acts[:, pl.ds(start, part), :]), cot)
-        total_up -= dot_tn(flat(scaled[:, pl.ds(start, part), :]), text)
+        span = pl.ds(start, part)
+        total_down += dot_tn(text, flat(factor_ref[:, 0, span, :]))
+        total_up += dot_tn(flat(factor_ref[:, 1, span, :]), cot)
+        total_up -= dot_tn(flat(factor_ref[:, 2, span, :]), text)
     down_ref[...] = total_down
     up_ref[...] = total_up
 
 
 def row_products(sec, cols, factors):
-    groups, _, share = cols[0].shape
+    share = cols[0].shape[2]
     return pl.pallas_call(
         row_kernel,
         in_specs=[SMEM] + [VMEM] * 5,
@@ -521,10 +505,6 @@
         out_shape=[
             jax.ShapeDtypeStruct((share, RANK), F32),
             jax.ShapeDtypeStruct((RANK, share), F32),
-        ],
-        scratch_shapes=[
-            pltpu.VMEM((groups, RANK, RANK), BF),
-            pltpu.VMEM((groups, RANK, RANK), BF),
         ],
         compiler_params=PARAMS,
     )(scalars(sec % 4), *cols, factors)
@@ -620,16 +600,14 @@
             sec, grp, keep, text, cot, weight_down, weight_up, proj_out, sections, groups
         )
     )
-    gath = lax.all_gather(proj, "section", axis=0)
     own_images = images[0, 0].reshape(slot_count * tokens, 4, enc_width).transpose(1, 0, 2)
 
     image_rows = lax.dynamic_slice_in_dim(proj_out, grp * piece, piece, 0)
-    up_rows, cols, image_rows = lax.optimization_barrier((up_rows, cols, image_rows))
+    up_rows, cols, own_images, image_rows = lax.optimization_barrier(
+        (up_rows, cols, own_images, image_rows)
+    )
     cols = lax.all_to_all(cols, "dp", 0, 0)
-    gath, own_images = lax.optimization_barrier((gath, own_images))
     group_images = lax.all_gather(own_images, "section", axis=0)
-    own_slices, group_images = lax.optimization_barrier((own_slices, group_images))
-    slices = lax.all_gather(own_slices, "section", axis=0)
     rows = jnp.concatenate([image_rows[None], up_rows], axis=0).reshape(-1, width)
     gram = jnp.stack(
         [
@@ -639,21 +617,22 @@
         axis=1,
     ).astype(BF).reshape(-1, rank)
     packed = pack_gram(core, lax.all_gather(gram, "section", axis=0), groups)
-    packed, cols = lax.optimization_barrier((packed, cols))
+    packed, cols, proj = lax.optimization_barrier((packed, cols, proj))
     own_gram = lax.all_to_all(packed, "dp", 0, 0)
 
+    gath = lax.all_gather(proj, "section", axis=0)
     quarters = proj_in.reshape(4, enc_width, rank)
     state, proj_pre, wide, in_window = encoder_front(
         sec, group_images, enc_down, enc_up, quarters
     )
-    own_gram, gath, state, proj_pre, wide, in_window, cols = lax.optimization_barrier(
-        (own_gram, gath, state, proj_pre, wide, in_window, cols)
-    )
+    own_gram, gath, state, proj_pre, wide, in_window, cols, own_slices = lax.optimization_barrier(
+        (own_gram, gath, state, proj_pre, wide, in_window, cols, own_slices)
+    )
+    slices = lax.all_gather(own_slices, "section", axis=0)
     other_gram = lax.ppermute(own_gram, "section", swap)
     far = [(at, at ^ 2) for at in range(sections)]
     far_cols = lax.ppermute(cols, "section", far)
 
-    gath, slices = lax.optimization_barrier((gath, slices))
     coef, factor, image = rank_space(
         sec, core, own_gram, other_gram, gath, proj_pre, base, sel, width
     )

time: 231 us -> 199 us (0.86)
  waiting for transfers between devices: 110 us -> 69.4 us
  starting transfers between devices: 29.6 us -> 33.6 us
    all_gather x1, waiting for transfers between devices: 25.8 us -> 0.01 us  [shards(): gath = lax.all_gather(proj, 'section', axis=0)]
    all_to_all x1, waiting for transfers between devices: 21.3 us -> 1.63 us  [spread(): lax.all_to_all(jnp.broadcast_to(value[None], (count,) + value.shape), axi...]
    all_gather x1, waiting for transfers between devices: 18.1 us -> 0.01 us  [shards(): factors = lax.all_gather(factor, 'dp', axis=0)]
    all_gather x1, waiting for transfers between devices: 0.01 us -> 7.5 us  [shards(): slices = lax.all_gather(own_slices, 'section', axis=0)]
    all_to_all x1, waiting for transfers between devices: 22.2 us -> 29.2 us  [shards(): mixed = lax.all_to_all(mixed, 'dp', 0, 0)]
    ppermute x1, waiting for transfers between devices: 0.01 us -> 5.38 us  [shards(): far_cols = lax.ppermute(cols, 'section', far)]
    all_to_all x1, waiting for transfers between devices: 0.01 us -> 4.68 us  [shards(): lax.all_to_all(term.astype(BF).reshape(sections, few, rank), 'section', 0...]
    unnamed x46 -> x50, local copies, waits for them, and re-layouts: 13.9 us -> 14.3 us
  transfers between devices with their start and end apart: 14 -> 14, of which waited for: 8 -> 8; matrix products, arithmetic and copies ran while one was open for 4% -> 7% of each run, Pallas kernels for 11% -> 13%
where the time goes in v6:
time: 199 us; the launch traced here: 197 us
  waiting for transfers between devices  69.4 us (35%)
  Pallas kernels  34.7 us (17%)
  starting transfers between devices  33.6 us (17%)
  local copies, waits for them, and re-layouts  21.7 us (11%)
  between operations  14 us (7%)
  blocking collectives  13.3 us (7%)
  matrix products  5.1 us (3%)
  other arithmetic  4.89 us (2%)
    all_to_all x1, waiting for transfers between devices, shards(): mixed = lax.all_to_all(mixed, 'dp', 0, 0)  29.2 us
    unnamed x50, local copies, waits for them, and re-layouts  14.3 us
    all_gather x1, blocking collectives, shards(): packed = pack_gram(core, lax.all_gather(gram, 'section', axis=0), groups)  13.3 us
    all_to_all x1, waiting for transfers between devices, shards(): own_gram = lax.all_to_all(packed, 'dp', 0, 0)  11 us
    pallas_call x1, Pallas kernels, encoder_front(): pl.pallas_call(functools.partial(front_kernel, sections, windows, in_wind...  9.26 us
    pallas_call x1, Pallas kernels, text_products(): pl.pallas_call(functools.partial(text_kernel, part, share, few, steps), g...  9.24 us
    all_to_all x1, starting transfers between devices, shards(): cols = lax.all_to_all(cols, 'dp', 0, 0)  8.06 us
    pallas_call x1, Pallas kernels, rank_space(): pl.pallas_call(functools.partial(rank_kernel, layers, width), grid=(1,),...  7.54 us
  transfers between devices with their start and end apart: 14, of which 8 were waited for; matrix products, arithmetic and copies ran while one was open for 7% of the time, Pallas kernels for 13%

profile of v6, /device:TPU:0, one launch (start us, length us, event | category | flops | bytes accessed | tf_op | source)
XLA Modules:
  0.0 196.8 jit_solution(15876723464932966269)
XLA Ops:
  9.2 4.5 %all-to-all-start = ((bf16[8,8,8192]{2,1,0:T(8,128)(2,1)}), bf16[8,8,8192]{2,1,0:T(8,128)(2,1)}, u32[]{:S(2)}, u32[]{:S(2)}) async-start(bf16[8,8,8192]{2,1,0:T(8,128)(2,1)} %broadcast_in_dim.12), calls=%async_computation | async-start | bytes 2097152 | tf_op jit(solution)/shard_map/all_to_all | solution.py:567
  15.7 9.2 %shard_map.145 = (bf16[16,64,512]{2,1,0:T(8,128)(2,1)S(1)}, bf16[512,128]{1,0:T(8,128)(2,1)}, f32[3,128,128]{2,1,0:T(8,128)S(1)}, bf16[8,2,64,128]{3,2,1,0:T(8,1...) custom-call(s32[2]{0:T(128)S(1)} %pad_add_fusion.place_ref, ...), custom_call_target="tpu_custom_call" | custom-call | tf_op jit(solution)/shard_map/pallas_call | solution.py:133
  28.1 1.6 all-to-all-done
  29.8 1.9 copy.25
  31.7 8.1 %all-to-all-start.1 = ((bf16[16,64,512]{2,1,0:T(8,128)(2,1)}), bf16[16,64,512]{2,1,0:T(8,128)(2,1)S(1)}, u32[]{:S(2)}, u32[]{:S(2)}) async-start(bf16[16,64,512]{2,1,0:T(8,128)(2,1)} %copy-done.4), calls=%async_computation.1 | async-start | bytes 2097152 | tf_op jit(solution)/shard_map/all_to_all | solution.py:609
  39.9 1.9 fusion.14
  41.8 2.1 %fusion.11 = bf16[9,1,8,128]{3,2,0,1:T(8,128)(2,1)S(1)} fusion(bf16[1,128,8192]{2,1,0:T(8,128)(2,1)S(1)} %copy-done.20, bf16[8,8,8192]{2,1,0:T(8,128)(2,1)} %all-to-all-done, bf16[1,8,8192]{2,1,0:T(8,128)(2,1)S(1)} %bitcast.71), kind=kOutput, calls=%fused_computation.11 | convolution fusion | flops 151593984 | bytes 3295232 | tf_op jit(solution)/shard_map/dot_general | solution.py:32
  44.0 13.3 %all_gather.27.gram_ref = bf16[8,144,128]{2,1,0:T(8,128)(2,1)S(1)} all-gather(bf16[1,144,128]{2,1,0:T(8,128)(2,1)S(1)} %bitcast.76), channel_id=1, replica_groups=mesh['section'=8,'dp'=16] {'section'}, dimensions={0}, use_global_device_ids=true | all-gather | bytes 331776 | tf_op jit(solution)/shard_map/all_gather | solution.py:619
  58.8 7.4 %all-to-all-start.2 = ((bf16[16,352,128]{2,1,0:T(8,128)(2,1)}), bf16[16,352,128]{2,1,0:T(8,128)(2,1)}, u32[]{:S(2)}, u32[]{:S(2)}) async-start(bf16[16,352,128]{2,1,0:T(8,128)(2,1)} %shard_map.146), calls=%async_computation.2 | async-start | bytes 2883584 | tf_op jit(solution)/shard_map/all_to_all | solution.py:621
  66.2 9.3 %shard_map.147 = (f32[10,128,128]{2,1,0:T(8,128)S(1)}, f32[128,128]{1,0:T(8,128)S(1)}, bf16[128,6784]{1,0:T(8,128)(2,1)S(1)}, bf16[2048,128]{1,0:T(8,128)(2,1)S(1)}) custom-call(s32[1]{0:T(128)} %bitcast.place_ref, bf16[8,4,16,3200]{3,2,1,0:T(8,128)(2,1)} %bitcast.66, bf16[3200,128]{1,0:T(8,128)(2,1)S(1)} %copy-done.7, bf16[128,3200]{1,0:T(8,128)(2,1)S(1)} %copy-done.8, ...), custom_call_target="tpu_custom_call" | custom-call | tf_op jit(solution)/shard_map/pallas_call | solution.py:233
  79.0 11.0 %all-to-all-done.2.own_ref = bf16[16,352,128]{2,1,0:T(8,128)(2,1)} async-done(((bf16[16,352,128]{2,1,0:T(8,128)(2,1)}), bf16[16,352,128]{2,1,0:T(8,128)(2,1)}, u32[]{:S(2)}, u32[]{:S(2)}) %all-to-all-start.2) | async-done | bytes 1441824 | tf_op jit(solution)/shard_map/all_to_all | solution.py:621
  90.6 2.8 %collective-permute-done.1.other_ref = bf16[16,352,128]{2,1,0:T(8,128)(2,1)S(1)} collective-permute-done((bf16[16,352,128]{2,1,0:T(8,128)(2,1)}, bf16[16,352,128]{2,1,0:T(8,128)(2,1)S(1)}, u32[]{:S(2)}, u32[]{:S(2)}) %collective-permute-start.1) | collective-permute-done | bytes 1441824 | tf_op jit(solution)/shard_map/ppermute | solution.py:632
  94.6 7.5 %shard_map.148 = (bf16[18,128,128]{2,1,0:T(8,128)(2,1)}, bf16[3,128,128]{2,1,0:T(8,128)(2,1)}, bf16[3,128,128]{2,1,0:T(8,128)(2,1)}) custom-call(s32[2]{0:T(128)} %pad_add_fusion.1.place_ref, bf16[16,352,128]{2,1,0:T(8,128)(2,1)} %all-to-all-done.2.own_ref, bf16[16,352,128]{2,1,0:T(8,128)(2,1)} %copy-done.22, bf16[8,512,128]{2,1,0:T(8,128)(2,1)} %bitcast.72, ...), custom_call_target="tpu_custom_call" | custom-call | tf_op jit(solution)/shard_map/pallas_call | solution.py:373
  102.8 4.5 %all-to-all-start.3 = ((bf16[16,144,128]{2,1,0:T(8,128)(2,1)}), bf16[16,144,128]{2,1,0:T(8,128)(2,1)}, u32[]{:S(2)}, u32[]{:S(2)}) async-start(bf16[16,144,128]{2,1,0:T(8,128)(2,1)} %bitcast.73), calls=%async_computation.3 | async-start | bytes 1179648 | tf_op jit(solution)/shard_map/all_to_all | solution.py:639
  112.0 1.9 shard_map.150
  114.0 7.0 %all-to-all-done.3 = bf16[16,144,128]{2,1,0:T(8,128)(2,1)} async-done(((bf16[16,144,128]{2,1,0:T(8,128)(2,1)}), bf16[16,144,128]{2,1,0:T(8,128)(2,1)}, u32[]{:S(2)}, u32[]{:S(2)}) %all-to-all-start.3) | async-done | bytes 589856 | tf_op jit(solution)/shard_map/all_to_all | solution.py:639
  122.1 5.4 %collective-permute-done.2.third_ref = bf16[16,64,512]{2,1,0:T(8,128)(2,1)S(1)} collective-permute-done((bf16[16,64,512]{2,1,0:T(8,128)(2,1)S(1)}, bf16[16,64,512]{2,1,0:T(8,128)(2,1)S(1)}, u32[]{:S(2)}, u32[]{:S(2)}) %collective-permute-start.2) | collective-permute-done | bytes 1048608 | tf_op jit(solution)/shard_map/ppermute | solution.py:634
  129.1 4.6 %all-to-all-start.4 = ((bf16[16,384,128]{2,1,0:T(8,128)(2,1)}), bf16[16,384,128]{2,1,0:T(8,128)(2,1)S(1)}, u32[]{:S(2)}, u32[]{:S(2)}) async-start(bf16[16,384,128]{2,1,0:T(8,128)(2,1)} %pad_maximum_fusion), calls=%async_computation.4 | async-start | bytes 3145728 | tf_op jit(solution)/shard_map/all_to_all | solution.py:651
  134.3 29.2 %all-to-all-done.4.mixed_ref = bf16[16,384,128]{2,1,0:T(8,128)(2,1)S(1)} async-done(((bf16[16,384,128]{2,1,0:T(8,128)(2,1)}), bf16[16,384,128]{2,1,0:T(8,128)(2,1)S(1)}, u32[]{:S(2)}, u32[]{:S(2)}) %all-to-all-start.4) | async-done | bytes 1572896 | tf_op jit(solution)/shard_map/all_to_all | solution.py:651
  164.5 3.4 %all-to-all-start.5 = ((bf16[8,64,128]{2,1,0:T(8,128)(2,1)}), bf16[8,64,128]{2,1,0:T(8,128)(2,1)S(1)}, u32[]{:S(2)}, u32[]{:S(2)}) async-start(bf16[8,64,128]{2,1,0:T(8,128)(2,1)} %bitcast.33), calls=%async_computation.5 | async-start | bytes 262144 | tf_op jit(solution)/shard_map/all_to_all | solution.py:659
  169.2 4.7 %all-to-all-done.5 = bf16[8,64,128]{2,1,0:T(8,128)(2,1)S(1)} async-done(((bf16[8,64,128]{2,1,0:T(8,128)(2,1)}), bf16[8,64,128]{2,1,0:T(8,128)(2,1)S(1)}, u32[]{:S(2)}, u32[]{:S(2)}) %all-to-all-start.5) | async-done | bytes 131104 | tf_op jit(solution)/shard_map/all_to_all | solution.py:659
  175.8 3.4 %shard_map.149 = (f32[512,128]{1,0:T(8,128)S(1)}, f32[128,512]{1,0:T(8,128)S(1)}) custom-call(s32[1]{0:T(128)} %bitcast.1.place_ref, bf16[16,64,512]{2,1,0:T(8,128)(2,1)S(1)} %all-to-all-done.1.first_ref, bf16[16,64,512]{2,1,0:T(8,128)(2,1)} %collective-permute-done.second_ref, bf16[16,64,512]{2,1,0:T(8,128)(2,1)S(1)} %copy-done.6, ...), custom_call_target="tpu_custom_call" | custom-call | tf_op jit(solution)/shard_map/pallas_call | solution.py:501
  179.2 7.5 %all-gather.15.cloned.1.call-done = bf16[8192,128]{1,0:T(8,128)(2,1)} async-done(((bf16[1024,128]{1,0:T(8,128)(2,1)}), bf16[8192,128]{1,0:T(8,128)(2,1)}) %all-gather.15.cloned.1.call-update) | async-done | bytes 2097168 | tf_op jit(solution)/shard_map/all_gather | solution.py:631
  188.3 1.9 shard_map.151
  (95 shorter events, 28.4 us)
Async XLA Ops:
  8.1 5.7 %copy-start.24 = (s32[1,16]{1,0:T(1,128)S(1)}, s32[1,16]{1,0:T(1,128)}, u32[]{:S(2)}) copy-start(s32[1,16]{1,0:T(1,128)} %param.19) | copy-start | bytes 196
  8.1 6.7 %copy-start.23 = (bf16[1,1,2,32,3200]{4,3,2,1,0:T(8,128)(2,1)S(1)}, bf16[1,1,2,32,3200]{4,3,2,1,0:T(8,128)(2,1)}, u32[]{:S(2)}) copy-start(bf16[1,1,2,32,3200]{4,3,2,1,0:T(8,128)(2,1)} %param.14) | copy-start | bytes 1228804
  9.2 6.5 %copy-start.1 = (bf16[1,128,8192]{2,1,0:T(8,128)(2,1)S(1)}, bf16[1,128,8192]{2,1,0:T(8,128)(2,1)}, u32[]{:S(2)}) copy-start(bf16[1,128,8192]{2,1,0:T(8,128)(2,1)} %param.10) | copy-start | bytes 6291460
  9.2 20.6 %all-to-all-start = ((bf16[8,8,8192]{2,1,0:T(8,128)(2,1)}), bf16[8,8,8192]{2,1,0:T(8,128)(2,1)}, u32[]{:S(2)}, u32[]{:S(2)}) async-start(bf16[8,8,8192]{2,1,0:T(8,128)(2,1)} %broadcast_in_dim.12), calls=%async_computation | async-start | bytes 2097152 | tf_op jit(solution)/shard_map/all_to_all | solution.py:567
  13.7 52.5 %all-gather.11.cloned.1.call-start = ((), (), s32[]{:S(2)}) async-start(), calls=%async_computation.7 | async-start | bytes 3686400 | tf_op jit(solution)/shard_map/all_gather | solution.py:610
  27.1 4.6 %copy-start.4 = (bf16[16,64,512]{2,1,0:T(8,128)(2,1)}, bf16[16,64,512]{2,1,0:T(8,128)(2,1)S(1)}, u32[]{:S(2)}) copy-start(bf16[16,64,512]{2,1,0:T(8,128)(2,1)S(1)} %get-tuple-element.48) | copy-start | bytes 3145732
  29.8 10.1 %copy-start.21 = (bf16[1,8192,128]{2,1,0:T(8,128)(2,1)S(1)}, bf16[1,8192,128]{2,1,0:T(8,128)(2,1)}, u32[]{:S(2)}) copy-start(bf16[1,8192,128]{2,1,0:T(8,128)(2,1)} %param.12) | copy-start | bytes 6291460
  31.7 27.0 %all-to-all-start.1 = ((bf16[16,64,512]{2,1,0:T(8,128)(2,1)}), bf16[16,64,512]{2,1,0:T(8,128)(2,1)S(1)}, u32[]{:S(2)}, u32[]{:S(2)}) async-start(bf16[16,64,512]{2,1,0:T(8,128)(2,1)} %copy-done.4), calls=%async_computation.1 | async-start | bytes 2097152 | tf_op jit(solution)/shard_map/all_to_all | solution.py:609
  39.8 50.2 %all-gather.9.cloned.1.call-start = ((), (), s32[]{:S(2)}) async-start(), calls=%async_computation.6 | async-start | bytes 1179648 | tf_op jit(solution)/shard_map/all_gather | solution.py:623
  39.9 2.0 copy-start.20
  58.7 7.5 %copy-start.7 = (bf16[3200,128]{1,0:T(8,128)(2,1)S(1)}, bf16[3200,128]{1,0:T(8,128)(2,1)}, u32[]{:S(2)}) copy-start(bf16[3200,128]{1,0:T(8,128)(2,1)} %down_ref.1) | copy-start | bytes 2457604
  58.7 7.5 %copy-start.8 = (bf16[128,3200]{1,0:T(8,128)(2,1)S(1)}, bf16[128,3200]{1,0:T(8,128)(2,1)}, u32[]{:S(2)}) copy-start(bf16[128,3200]{1,0:T(8,128)(2,1)} %up_ref.1) | copy-start | bytes 2457604
  58.8 31.2 %all-to-all-start.2 = ((bf16[16,352,128]{2,1,0:T(8,128)(2,1)}), bf16[16,352,128]{2,1,0:T(8,128)(2,1)}, u32[]{:S(2)}, u32[]{:S(2)}) async-start(bf16[16,352,128]{2,1,0:T(8,128)(2,1)} %shard_map.146), calls=%async_computation.2 | async-start | bytes 2883584 | tf_op jit(solution)/shard_map/all_to_all | solution.py:621
  66.1 108.4 %all-gather.13.cloned.1.call-start = ((), (), s32[]{:S(2)}) async-start(), calls=%async_computation.8 | async-start | bytes 1671168 | tf_op jit(solution)/shard_map/all_gather | solution.py:640
  90.0 3.4 %collective-permute-start.1 = (bf16[16,352,128]{2,1,0:T(8,128)(2,1)}, bf16[16,352,128]{2,1,0:T(8,128)(2,1)S(1)}, u32[]{:S(2)}, u32[]{:S(2)}) collective-permute-start(bf16[16,352,128]{2,1,0:T(8,128)(2,1)} %all-to-all-done.2.own_ref), channel_id=1, source_target_pairs={{0,16},{16,0},{32,48},{48,32},{64,80},{80,64},{96,112},{112,96},{1... | collective-permute-start | bytes 4325384 | tf_op jit(solution)/shard_map/ppermute | solution.py:632
  102.1 5.2 %copy-start.18 = (bf16[3,128,128]{2,1,0:T(8,128)(2,1)S(1)}, bf16[3,128,128]{2,1,0:T(8,128)(2,1)}, u32[]{:S(2)}) copy-start(bf16[3,128,128]{2,1,0:T(8,128)(2,1)} %get-tuple-element.70.image_ref) | copy-start | bytes 294916
  102.2 84.6 %all-gather.15.cloned.1.call-start = ((), (), s32[]{:S(2)}) async-start(), calls=%async_computation.9 | async-start | bytes 2359296 | tf_op jit(solution)/shard_map/all_gather | solution.py:631
  102.2 25.3 %collective-permute-start.2 = (bf16[16,64,512]{2,1,0:T(8,128)(2,1)S(1)}, bf16[16,64,512]{2,1,0:T(8,128)(2,1)S(1)}, u32[]{:S(2)}, u32[]{:S(2)}) collective-permute-start(bf16[16,64,512]{2,1,0:T(8,128)(2,1)S(1)} %all-to-all-done.1.first_ref), channel_id=1, source_target_pairs={{0,32},{16,48},{32,0},{48,16},{64,96},{80,112},{96,64},{112,80},{1... | collective-permute-start | bytes 3145736 | tf_op jit(solution)/shard_map/ppermute | solution.py:634
  102.8 18.2 %all-to-all-start.3 = ((bf16[16,144,128]{2,1,0:T(8,128)(2,1)}), bf16[16,144,128]{2,1,0:T(8,128)(2,1)}, u32[]{:S(2)}, u32[]{:S(2)}) async-start(bf16[16,144,128]{2,1,0:T(8,128)(2,1)} %bitcast.73), calls=%async_computation.3 | async-start | bytes 1179648 | tf_op jit(solution)/shard_map/all_to_all | solution.py:639
  129.1 34.4 %all-to-all-start.4 = ((bf16[16,384,128]{2,1,0:T(8,128)(2,1)}), bf16[16,384,128]{2,1,0:T(8,128)(2,1)S(1)}, u32[]{:S(2)}, u32[]{:S(2)}) async-start(bf16[16,384,128]{2,1,0:T(8,128)(2,1)} %pad_maximum_fusion), calls=%async_computation.4 | async-start | bytes 3145728 | tf_op jit(solution)/shard_map/all_to_all | solution.py:651
  133.7 40.9 %collective-permute-start = (bf16[16,64,512]{2,1,0:T(8,128)(2,1)S(1)}, bf16[16,64,512]{2,1,0:T(8,128)(2,1)}, u32[]{:S(2)}, u32[]{:S(2)}) collective-permute-start(bf16[16,64,512]{2,1,0:T(8,128)(2,1)S(1)} %all-to-all-done.1.first_ref), channel_id=1, source_target_pairs={{0,16},{16,0},{32,48},{48,32},{64,80},{80,64},{96,112},{112,96},{1... | collective-permute-start | bytes 3145736 | tf_op jit(solution)/shard_map/ppermute | solution.py:662
  133.8 40.8 %collective-permute-start.3 = (bf16[16,64,512]{2,1,0:T(8,128)(2,1)}, bf16[16,64,512]{2,1,0:T(8,128)(2,1)}, u32[]{:S(2)}, u32[]{:S(2)}) collective-permute-start(bf16[16,64,512]{2,1,0:T(8,128)(2,1)} %copy-done.5), channel_id=1, source_target_pairs={{0,16},{16,0},{32,48},{48,32},{64,80},{80,64},{96,112},{112,96},{1... | collective-permute-start | bytes 3145736 | tf_op jit(solution)/shard_map/ppermute | solution.py:663
  164.5 9.4 %all-to-all-start.5 = ((bf16[8,64,128]{2,1,0:T(8,128)(2,1)}), bf16[8,64,128]{2,1,0:T(8,128)(2,1)S(1)}, u32[]{:S(2)}, u32[]{:S(2)}) async-start(bf16[8,64,128]{2,1,0:T(8,128)(2,1)} %bitcast.33), calls=%async_computation.5 | async-start | bytes 262144 | tf_op jit(solution)/shard_map/all_to_all | solution.py:659
  175.8 10.9 %copy-start.17 = (bf16[128,512]{1,0:T(8,128)(2,1)S(1)}, bf16[128,512]{1,0:T(8,128)(2,1)}, u32[]{:S(2)}) copy-start(bf16[128,512]{1,0:T(8,128)(2,1)} %copy-done.16) | copy-start | bytes 393220
  (15 other events, 15.8 us)
Sparse Core Ops, SparseCore 0:
  31.9 30.6 all-gather.10
  64.2 23.2 all-gather.8
  102.3 55.0 all-gather.12
  159.5 27.1 all-gather.14
